TPU v7x, 512 devices: a whole 4x4x16 slice. The times are simulated.
512 devices in a mesh: row: 16 (over x, z_hi), col: 32 (over y, z_lo, core).
Axes of the slice: x: 4, y: 4, z: 16 (z_hi: 4, z_lo: 4; z = z_hi * 4 + z_lo), core: 2. Of those that a mesh axis runs over, the one named last changes fastest.
Arguments:
- nodes: bfloat16 [16384, 256], P(('row', 'col')), may hold values from -6 to 6
- harmonics: bfloat16 [16, 512, 25, 128], P('row', 'col'), may hold values from -6 to 6
- grad_blocks: bfloat16 [16, 512, 169, 128], P('row', 'col'), may hold values from -6 to 6
- pair_rows: int32 [16, 512, 128], P('row', 'col'), may hold values from 0 to 1023
- pair_cols: int32 [16, 512, 128], P('row', 'col'), may hold values from 0 to 511, as said below
- pair_mask: int32 [16, 512, 128], P('row', 'col'), may hold values 0 or 1
- block_counts: int32 [16, 32], P('row', 'col'), may hold values from 1 to 16
- w_left: bfloat16 [256, 256], replicated, may hold values from -0.375 to 0.375
- w_right: bfloat16 [256, 256], replicated, may hold values from -0.375 to 0.375
- w_harm: bfloat16 [25, 256], replicated, may hold values from -1.25 to 1.25
- w_out: bfloat16 [169, 256], replicated, may hold values from -0.375 to 0.375
Outputs:
- grad_nodes: float32 [16384, 256], P(('row', 'col'))
- grad_w_left: float32 [256, 256], replicated
- grad_w_right: float32 [256, 256], replicated
- grad_w_harm: float32 [25, 256], replicated
- grad_w_out: float32 [169, 256], replicated
Inputs may be any that keep to these rules, and one draw needn't show every extreme that they name: pair_cols // 32 differs by at most one from the row index r of the pair's grid cell.
All inputs are finite; a program needn't handle non-finite values. No bound on the sum of `pair_mask` on one device may be relied on, other than what follows from the above.
Results may differ from a plain program's by a relative error of at most 0.0032.
Values may be sent and summed in bfloat16 or wider, within the bound.
No kernel may reach another device: no remote copies, remote signals or barrier semaphores. Data moves between devices by JAX's collectives and lax.ppermute only.
A program may use at most 64 MiB of HBM per device.

v0:
```python
import jax
import jax.numpy as jnp
from jax import lax
from jax.sharding import PartitionSpec as P


def extended(array, sides, width):
    for axis, dim in sides:
        devices, length = (lax.axis_size(axis), array.shape[dim])
        up = [(i, (i + 1) % devices) for i in range(devices - 1)]
        down = [(j, i) for i, j in up]
        last = lax.slice_in_dim(array, length - width, length, axis=dim)
        first = lax.slice_in_dim(array, 0, width, axis=dim)
        before = lax.ppermute(last, axis, up)
        after = lax.ppermute(first, axis, down)
        array = jnp.concatenate([before, array, after], axis=dim)
    return array


def shifted(block, axis, distance):
    devices = range(lax.axis_size(axis))
    route = [(i - distance, i) for i in devices if i - distance in devices]
    return lax.ppermute(block, axis, route)


def body(
    nodes,
    harmonics,
    grad_blocks,
    pair_rows,
    pair_cols,
    pair_mask,
    block_counts,
    w_left,
    w_right,
    w_harm,
    w_out,
):
    shard_rows = nodes.shape[0]
    width = nodes.shape[1]
    blocks_per_turn = 4
    highest = lax.Precision.HIGHEST
    row_nodes = lax.all_gather(nodes, "col", axis=0, tiled=True)
    row_proj = jnp.dot(row_nodes, w_left, preferred_element_type=jnp.float32)
    column_nodes = extended(nodes, (("row", 0),), shard_rows)
    column_base = (lax.axis_index("row") - 1) * shard_rows
    column_proj = jnp.dot(column_nodes, w_right, preferred_element_type=jnp.float32)
    local_rows = pair_rows[0]
    local_cols = pair_cols[0] - column_base
    local_mask = pair_mask[0]
    local_harm = harmonics[0]
    local_grads = grad_blocks[0]
    pairs = local_rows.shape[1]
    count = block_counts[0, 0]
    turns = (count + blocks_per_turn - 1) // blocks_per_turn

    def turn(step, carry):
        sum_u, sum_v, grad_out, grad_harm = carry
        first = step * blocks_per_turn
        rows = lax.dynamic_slice_in_dim(local_rows, first, blocks_per_turn, 0).reshape(-1)
        cols = lax.dynamic_slice_in_dim(local_cols, first, blocks_per_turn, 0).reshape(-1)
        masks = lax.dynamic_slice_in_dim(local_mask, first, blocks_per_turn, 0)
        harm = lax.dynamic_slice_in_dim(local_harm, first, blocks_per_turn, 0)
        grads = lax.dynamic_slice_in_dim(local_grads, first, blocks_per_turn, 0)
        live = first + jnp.arange(blocks_per_turn, dtype=jnp.int32) < count
        weight_mask = (masks * live[:, None].astype(jnp.int32)).astype(jnp.bfloat16)
        g_masked = grads * weight_mask[:, None, :]
        u_pair = row_proj[rows]
        v_pair = column_proj[cols]
        embed = jnp.einsum("bmp,mk->bpk", harm, w_harm, preferred_element_type=jnp.float32).reshape(
            -1, width
        )
        grad_z = jnp.einsum(
            "bop,ok->bpk", g_masked, w_out, preferred_element_type=jnp.float32
        ).reshape(-1, width)
        z_pair = (
            (u_pair * v_pair * embed).astype(jnp.bfloat16).reshape(blocks_per_turn, pairs, width)
        )
        grad_out = grad_out + jnp.einsum(
            "bop,bpk->ok", g_masked, z_pair, preferred_element_type=jnp.float32
        )
        grad_e = (
            (grad_z * u_pair * v_pair).astype(jnp.bfloat16).reshape(blocks_per_turn, pairs, width)
        )
        grad_harm = grad_harm + jnp.einsum(
            "bmp,bpk->mk", harm, grad_e, preferred_element_type=jnp.float32
        )
        sum_u = sum_u.at[rows].add(grad_z * v_pair * embed)
        sum_v = sum_v.at[cols].add(grad_z * u_pair * embed)
        return (sum_u, sum_v, grad_out, grad_harm)

    start_carry = (
        jnp.zeros(row_proj.shape, jnp.float32),
        jnp.zeros(column_proj.shape, jnp.float32),
        jnp.zeros(w_out.shape, jnp.float32),
        jnp.zeros(w_harm.shape, jnp.float32),
    )
    sum_u, sum_v, grad_out, grad_harm = lax.fori_loop(0, turns, turn, start_carry)
    left_float = w_left.astype(jnp.float32)
    grad_left = jnp.dot(row_nodes.astype(jnp.float32).T, sum_u, precision=highest)
    grad_right = jnp.dot(column_nodes.astype(jnp.float32).T, sum_v, precision=highest)
    row_sums = lax.psum_scatter(sum_u, "col", scatter_dimension=0, tiled=True)
    row_part = jnp.dot(row_sums, left_float.T, precision=highest)
    upper = shifted(sum_v[:shard_rows], "row", -1)
    lower = shifted(sum_v[2 * shard_rows :], "row", 1)
    column_sums = sum_v[shard_rows : 2 * shard_rows] + upper + lower
    grad_nodes = row_part + jnp.dot(column_sums, w_right.astype(jnp.float32).T, precision=highest)
    totals = lax.psum((grad_out, grad_harm, grad_left, grad_right), ("row", "col"))
    return (grad_nodes, totals[2], totals[3], totals[1], totals[0])


def solution(mesh):
    return jax.shard_map(
        body,
        mesh=mesh,
        in_specs=(
            P(("row", "col"), None),
            P("row", "col", None, None),
            P("row", "col", None, None),
            P("row", "col", None),
            P("row", "col", None),
            P("row", "col", None),
            P("row", "col"),
            P(),
            P(),
            P(),
            P(),
        ),
        out_specs=(P(("row", "col"), None), P(), P(), P(), P()),
        check_vma=False,
    )
```

profile of v0, /device:TPU:1, one launch (start us, length us, event | category | flops | bytes accessed | tf_op | source)
XLA Modules:
  0.0 625.9 jit_solution(10189884287857283016)
XLA Ops:
  9.4 10.3 %collective-permute-start = (bf16[32,256]{1,0:T(8,128)(2,1)}, bf16[32,256]{1,0:T(8,128)(2,1)S(1)}, u32[]{:S(2)}, u32[]{:S(2)}) collective-permute-start(bf16[32,256]{1,0:T(8,128)(2,1)} %param.13), channel_id=1, source_target_pairs={{0,32},{32,64},{64,96},{96,128},{128,160},{160,192},{192,224},{224... | collective-permute-start | bytes 49160 | tf_op jit(solution)/shard_map/ppermute | solution.py:14
  19.6 48.0 %all_gather.3 = bf16[1024,256]{1,0:T(8,128)(2,1)S(1)} all-gather(bf16[32,256]{1,0:T(8,128)(2,1)} %param.13), channel_id=1, replica_groups=mesh['row'=16,'col'=32] {'col'}, dimensions={0}, use_global_device_ids=true | all-gather | bytes 540672 | tf_op jit(solution)/shard_map/all_gather | solution.py:43
  73.6 53.4 %while.16 = (s32[]{:T(128)}, f32[1024,256]{1,0:T(8,128)S(1)}, f32[96,256]{1,0:T(8,128)S(1)}, f32[169,256]{1,0:T(8,128)}, f32[25,256]{1,0:T(8,128)S(1)}, /*index=...) while((s32[]{:T(128)}, f32[1024,256]{1,0:T(8,128)S(1)}, ...), condition=%wide.region_3.4_spmd, body=%wide.region_0.3_spmd.sunk | while | flops 103513616 | bytes 16076123 | solution.py:98
  75.8 1.6 gather_fusion
  77.3 1.6 gather_fusion.1
  80.7 1.9 fusion.47
  83.7 3.9 scatter_fusion.1
  87.7 3.7 scatter_fusion
  93.6 1.6 gather_fusion
  95.2 1.6 gather_fusion.1
  98.5 1.9 fusion.47
  101.5 3.9 scatter_fusion.1
  105.5 3.7 scatter_fusion
  111.4 1.6 gather_fusion
  113.0 1.6 gather_fusion.1
  116.3 1.9 fusion.47
  119.4 3.9 scatter_fusion.1
  123.3 3.7 scatter_fusion
  127.0 3.1 convolution_bitcast_fusion.2
  131.8 1.3 collective-permute-start.2
  133.1 7.9 %collective-permute-start.3 = (f32[32,256]{1,0:T(8,128)S(1)}, f32[32,256]{1,0:T(8,128)S(1)}, u32[]{:S(2)}, u32[]{:S(2)}) collective-permute-start(f32[32,256]{1,0:T(8,128)S(1)} %get-tuple-element.140), channel_id=1, source_target_pairs={{0,32},{32,64},{64,96},{96,128},{128,160},{160,192},{192,224},{224... | collective-permute-start | bytes 98312 | tf_op jit(solution)/shard_map/ppermute | solution.py:23
  141.0 120.4 %psum.30 = f32[25,256]{1,0:T(8,128)} all-reduce(f32[25,256]{1,0:T(8,128)S(1)} %get-tuple-element.93), channel_id=1, replica_groups=mesh['row'=16,'col'=32] {'row','col'}, use_global_device_ids=true, to_apply=%region_7.8 | all-reduce | flops 6400 | bytes 51200 | tf_op jit(solution)/shard_map/psum | solution.py:108
  261.4 351.6 %all-reduce.3.cloned.1.call-done = (f32[256,256]{0,1:T(8,128)}, f32[256,256]{1,0:T(8,128)}, f32[169,256]{1,0:T(8,128)}) async-done(((f32[256,256]{0,1:T(8,128)}, f32[256,256]{1,0:T(8,128)}, f32[169,256]{1,0:T(8,128)}), (f32[256,256]{0,1:T(8,128)}, f32[256,256]{1,0:T(8,128)}, f32[169,256]{1,0:T(8,128)})) %all-reduce.3.cloned.1.call-update) | async-done | bytes 697360 | tf_op jit(solution)/shard_map/psum | solution.py:108
  613.0 1.8 copy.18
  (101 shorter events, 26.8 us)
Async XLA Ops:
  8.0 59.6 %copy-start = (bf16[256,256]{1,0:T(8,128)(2,1)S(1)}, bf16[256,256]{1,0:T(8,128)(2,1)}, u32[]{:S(2)}) copy-start(bf16[256,256]{1,0:T(8,128)(2,1)} %param.20) | copy-start | bytes 393220
  8.0 604.9 %all-reduce.3.cloned.1.call-start = ((), (), s32[]{:S(2)}) async-start(), calls=%async_computation.2 | async-start | bytes 1409024 | tf_op jit(solution)/shard_map/psum | solution.py:108
  8.1 63.5 %collective-permute-start.1 = (bf16[32,256]{1,0:T(8,128)(2,1)}, bf16[32,256]{1,0:T(8,128)(2,1)S(1)}, u32[]{:S(2)}, u32[]{:S(2)}) collective-permute-start(bf16[32,256]{1,0:T(8,128)(2,1)} %param.13), channel_id=1, source_target_pairs={{32,0},{64,32},{96,64},{128,96},{160,128},{192,160},{224,192},{256... | collective-permute-start | bytes 49160 | tf_op jit(solution)/shard_map/ppermute | solution.py:15
  9.4 61.5 %collective-permute-start = (bf16[32,256]{1,0:T(8,128)(2,1)}, bf16[32,256]{1,0:T(8,128)(2,1)S(1)}, u32[]{:S(2)}, u32[]{:S(2)}) collective-permute-start(bf16[32,256]{1,0:T(8,128)(2,1)} %param.13), channel_id=1, source_target_pairs={{0,32},{32,64},{64,96},{96,128},{128,160},{160,192},{192,224},{224... | collective-permute-start | bytes 49160 | tf_op jit(solution)/shard_map/ppermute | solution.py:14
  67.6 0.8 copy-start.3
  67.6 0.8 copy-start.15
  67.6 1.5 copy-start.13
  67.6 2.1 copy-start.5
  69.8 1.8 copy-start.6
  70.8 0.7 copy-start.14
  78.9 1.3 copy-start.4
  83.7 3.9 copy-start.2
  96.7 1.3 copy-start.4
  101.5 3.9 copy-start.2
  114.5 1.3 copy-start.4
  119.4 3.9 copy-start.2
  127.0 4.2 copy-start.1
  127.0 3.1 copy-start.10
  131.2 483.5 %reduce-scatter.2.cloned.1.call-start = ((), (), s32[]{:S(2)}) async-start(), calls=%async_computation.1 | async-start | bytes 1081344 | tf_op jit(solution)/shard_map/reduce_scatter | solution.py:102
  131.8 484.0 %collective-permute-start.2 = (f32[32,256]{1,0:T(8,128)S(1)}, f32[32,256]{1,0:T(8,128)S(1)}, u32[]{:S(2)}, u32[]{:S(2)}) collective-permute-start(f32[32,256]{1,0:T(8,128)S(1)} %get-tuple-element.139), channel_id=1, source_target_pairs={{32,0},{64,32},{96,64},{128,96},{160,128},{192,160},{224,192},{256... | collective-permute-start | bytes 98312 | tf_op jit(solution)/shard_map/ppermute | solution.py:23
  133.1 482.7 %collective-permute-start.3 = (f32[32,256]{1,0:T(8,128)S(1)}, f32[32,256]{1,0:T(8,128)S(1)}, u32[]{:S(2)}, u32[]{:S(2)}) collective-permute-start(f32[32,256]{1,0:T(8,128)S(1)} %get-tuple-element.140), channel_id=1, source_target_pairs={{0,32},{32,64},{64,96},{96,128},{128,160},{160,192},{192,224},{224... | collective-permute-start | bytes 98312 | tf_op jit(solution)/shard_map/ppermute | solution.py:23
  614.7 1.1 copy-start.7
  614.7 2.0 copy-start.11
  616.7 1.0 copy-start.12
  (2 other events, 1.3 us)
Sparse Core Ops, SparseCore 0:
  131.3 481.5 all-reduce.2
Sparse Core Ops, SparseCore 1:
  134.5 160.6 reduce-scatter.1
where the time goes:
time: 627 us; the launch traced here: 626 us
  waiting for transfers between devices  352 us (56%)
  blocking collectives  168 us (27%)
  other arithmetic  30.5 us (5%)
  starting transfers between devices  20.8 us (3%)
  local copies, waits for them, and re-layouts  19.9 us (3%)
  matrix products  17.6 us (3%)
  between operations  16.3 us (3%)
    psum x1, waiting for transfers between devices, body(): lax.psum((grad_out, grad_harm, grad_left, grad_right), ('row', 'col'))  352 us
    psum x1, blocking collectives, body(): lax.psum((grad_out, grad_harm, grad_left, grad_right), ('row', 'col'))  120 us
    all_gather x1, blocking collectives, body(): row_nodes = lax.all_gather(nodes, 'col', axis=0, tiled=True)  48 us
  transfers between devices with their start and end apart: 6, of which 1 were waited for; matrix products, arithmetic and copies ran while one was open for 1% of the time, Pallas kernels for 0%

commit v1 on v0

v1 whole, which is shorter than its diff:
```python
import jax
import jax.numpy as jnp
from jax import lax
from jax.experimental import pallas as pl
from jax.experimental.pallas import tpu as pltpu
from jax.sharding import PartitionSpec as P

F32, BF16 = jnp.float32, jnp.bfloat16
VMEM = pl.BlockSpec(memory_space=pltpu.VMEM)
SMEM = pl.BlockSpec(memory_space=pltpu.SMEM)
PARAMS = pltpu.CompilerParams(vmem_limit_bytes=48 * 1024 * 1024)
BOTH = ("row", "col")


def like(*shape):
    return jax.ShapeDtypeStruct(shape, F32)


def dot(a, b, da, db):
    return lax.dot_general(a, b, (((da,), (db,)), ((), ())), preferred_element_type=F32)


def halves(x):
    high = x.astype(BF16)
    return high, (x - high.astype(F32)).astype(BF16)


def pair_kernel(
    places, rows, cols, mask, harm, grads, own, other, column_nodes, w_left, w_right, w_harm, w_out,
    keep, send, sum_v, u_parts, v_parts, sum_u, weights,
):
    count, column_base, core = places[0], places[1], places[2]
    width = w_left.shape[0]
    half = own.shape[0]
    shard = column_nodes.shape[0] // 3
    pairs = 2 * mask.shape[1]
    orbitals, harmonics = w_out.shape[0], w_harm.shape[0]
    for first, nodes in ((0, own), (half, other)):
        high, low = halves(dot(w_left[...], nodes[...], 0, 1))
        u_parts[:width, first : first + half] = high
        u_parts[width:, first : first + half] = low
    high, low = halves(dot(w_right[...], column_nodes[...], 0, 1))
    v_parts[:width] = high
    v_parts[width:] = low
    for total in (sum_u, sum_v, weights):
        total[...] = jnp.zeros_like(total)
    at_out = 2 * width
    at_harm = at_out + 176

    def line(ref, first):
        return jnp.concatenate([ref[pl.ds(first, 1), :], ref[pl.ds(first + 1, 1), :]], axis=1)

    def step(i, carry):
        first = 2 * i
        second = (first + 1 < count).astype(jnp.int32)
        live = jnp.concatenate(
            [mask[pl.ds(first, 1), :], mask[pl.ds(first + 1, 1), :] * second], axis=1
        )
        g = jnp.concatenate([grads[first], grads[first + 1]], axis=1)
        g = g * live.astype(F32).astype(BF16)
        h = jnp.concatenate([harm[first], harm[first + 1]], axis=1)
        atom = line(rows, first)
        owner = lax.shift_right_logical(atom, 5)
        away = jnp.bitwise_and(owner, 1) != core
        place = lax.shift_right_logical(owner, 1) * shard + jnp.bitwise_and(atom, shard - 1)
        place = place + jnp.where(away, half, 0)
        at_u = lax.broadcasted_iota(jnp.int32, (2 * half, pairs), 0) == place
        at_v = lax.broadcasted_iota(jnp.int32, (3 * shard, pairs), 0) == (
            line(cols, first) - column_base
        )
        pick_u = at_u.astype(F32).astype(BF16)
        pick_v = at_v.astype(F32).astype(BF16)
        parts = dot(u_parts[...], pick_u, 1, 0)
        u = parts[:width] + parts[width:]
        parts = dot(v_parts[...], pick_v, 1, 0)
        v = parts[:width] + parts[width:]
        e = dot(w_harm[...], h, 0, 0)
        gz = dot(w_out[...], g, 0, 0)
        uv = u * v
        weights[at_out : at_out + orbitals] += dot(g, (uv * e).astype(BF16), 1, 1)
        weights[at_harm : at_harm + harmonics] += dot(h, (gz * uv).astype(BF16), 1, 1)
        ge = gz * e
        high, low = halves(ge * v)
        sum_u[...] += dot(pick_u, high, 1, 1) + dot(pick_u, low, 1, 1)
        high, low = halves(ge * u)
        sum_v[...] += dot(pick_v, high, 1, 1) + dot(pick_v, low, 1, 1)
        return carry

    lax.fori_loop(0, lax.shift_right_logical(count + 1, 1), step, 0)
    left = jnp.zeros((width, width), F32)
    for first, nodes in ((0, own), (half, other)):
        for part in halves(sum_u[first : first + half]):
            left = left + dot(nodes[...], part, 0, 0)
    weights[:width] = left
    right = jnp.zeros((width, width), F32)
    for part in halves(sum_v[...]):
        right = right + dot(column_nodes[...], part, 0, 0)
    weights[width : 2 * width] = right
    chips, chunk = keep.shape[0], keep.shape[1]
    share = chunk - shard
    for chip in range(chips):
        keep[chip, :shard] = sum_u[chip * shard : (chip + 1) * shard]
        send[chip, :shard] = sum_u[half + chip * shard : half + (chip + 1) * shard]
        for to, which in ((keep, core), (send, 1 - core)):
            start = pl.multiple_of((which * chips + chip) * share, 8)
            to[chip, shard:] = weights[pl.ds(start, share), :]


def pair_sums(places, rows, cols, mask, harm, grads, own, other, column_nodes, weights_in, chips, share):
    width = own.shape[1]
    shard = column_nodes.shape[0] // 3
    half = own.shape[0]
    return pl.pallas_call(
        pair_kernel,
        out_shape=(
            like(chips, shard + share, width),
            like(chips, shard + share, width),
            like(3 * shard, width),
        ),
        in_specs=[SMEM] + [VMEM] * 12,
        out_specs=(VMEM,) * 3,
        scratch_shapes=[
            pltpu.VMEM((2 * width, 2 * half), BF16),
            pltpu.VMEM((2 * width, 3 * shard), BF16),
            pltpu.VMEM((2 * half, width), F32),
            pltpu.VMEM((2 * chips * share, width), F32),
        ],
        compiler_params=PARAMS,
    )(places, rows, cols, mask, harm, grads, own, other, column_nodes, *weights_in)


def node_kernel(parts, middle, upper, lower, w_left, w_right, grad_nodes, shares):
    shard = middle.shape[0]
    total = parts[0].astype(F32)
    for chip in range(1, parts.shape[0]):
        total = total + parts[chip].astype(F32)
    out = jnp.zeros(grad_nodes.shape, F32)
    columns = middle[...] + upper[...] + lower[...]
    for sums, weight in ((total[:shard], w_left), (columns, w_right)):
        for part in halves(sums):
            out = out + dot(part, weight[...], 1, 1)
    grad_nodes[...] = out
    for x in range(shares.shape[0]):
        shares[x] = total[shard:]


def node_grads(parts, middle, upper, lower, w_left, w_right, copies):
    shard, width = middle.shape
    return pl.pallas_call(
        node_kernel,
        out_shape=(like(shard, width), like(copies, parts.shape[1] - shard, width)),
        in_specs=[VMEM] * 6,
        out_specs=(VMEM,) * 2,
        compiler_params=PARAMS,
    )(parts, middle, upper, lower, w_left, w_right)


def sum_kernel(parts, out):
    total = parts[0]
    for i in range(1, parts.shape[0]):
        total = total + parts[i]
    for i in range(out.shape[0]):
        out[i] = total.astype(out.dtype)


def summed(parts, copies, dtype):
    return pl.pallas_call(
        sum_kernel,
        out_shape=jax.ShapeDtypeStruct((copies,) + parts.shape[1:], dtype),
        in_specs=[VMEM],
        out_specs=VMEM,
        compiler_params=PARAMS,
    )(parts)


def split_kernel(core, own, other, left, right, harm, out, whole):
    chips, share = own.shape[0], own.shape[1]
    width = left.shape[0]
    for which, part in ((core[0], own), (1 - core[0], other)):
        for chip in range(chips):
            start = pl.multiple_of((which * chips + chip) * share, 8)
            whole[pl.ds(start, share), :] = part[chip].astype(F32)
    left[...] = whole[:width]
    right[...] = whole[width : 2 * width]
    at_out = 2 * width
    out[...] = whole[at_out : at_out + out.shape[0]]
    at_harm = at_out + 176
    harm[...] = whole[at_harm : at_harm + harm.shape[0]]


def split(core, own, other, harmonics, orbitals):
    chips, share, width = own.shape
    return pl.pallas_call(
        split_kernel,
        out_shape=(
            like(width, width), like(width, width), like(harmonics, width), like(orbitals, width),
        ),
        in_specs=[SMEM, VMEM, VMEM],
        out_specs=(VMEM,) * 4,
        scratch_shapes=[pltpu.VMEM((2 * chips * share, width), F32)],
        compiler_params=PARAMS,
    )(core, own, other)


def groups(size, bits):
    mask = sum(bits)
    found = {}
    for i in range(size):
        found.setdefault(i & ~mask, []).append(i)
    return list(found.values())


def exchange(blocks, axis, bits):
    return lax.all_to_all(
        blocks, axis, 0, 0, tiled=True, axis_index_groups=groups(lax.axis_size(axis), bits)
    )


def swapped(block):
    return lax.ppermute(block, "col", [(i, i ^ 1) for i in range(lax.axis_size("col"))])


def shifted(block, distance):
    devices = range(lax.axis_size("row"))
    return lax.ppermute(
        block, "row", [(i, i + distance) for i in devices if i + distance in devices]
    )


def repeated(block, copies):
    return jnp.broadcast_to(block[None], (copies,) + block.shape)


def body(
    nodes,
    harmonics,
    grad_blocks,
    pair_rows,
    pair_cols,
    pair_mask,
    block_counts,
    w_left,
    w_right,
    w_harm,
    w_out,
):
    shard, width = nodes.shape
    chips = lax.axis_size("col") // 2
    share = 24
    core = jnp.bitwise_and(lax.axis_index("col"), 1)
    before = shifted(nodes, 1)
    after = shifted(nodes, -1)
    own = exchange(repeated(nodes, chips), "col", (2, 4, 8, 16)).reshape(-1, width)
    other = swapped(own)
    column_nodes = jnp.concatenate([before, nodes, after])
    places = jnp.stack(
        [block_counts[0, 0], (lax.axis_index("row") - 1) * shard, core]
    ).astype(jnp.int32)
    keep, send, sum_v = pair_sums(
        places, pair_rows[0], pair_cols[0], pair_mask[0], harmonics[0], grad_blocks[0],
        own, other, column_nodes, (w_left, w_right, w_harm, w_out), chips, share,
    )
    upper = shifted(sum_v[:shard], -1)
    lower = shifted(sum_v[2 * shard :], 1)
    parts = (keep + swapped(send)).astype(BF16)
    parts = exchange(parts, "col", (2, 4, 8, 16))
    grad_nodes, shares = node_grads(
        parts, sum_v[shard : 2 * shard], upper, lower, w_left, w_right, 4
    )
    shares = summed(exchange(shares, "row", (4, 8)), 4, F32)
    shares = summed(exchange(shares, "row", (1, 2)), chips, BF16)
    own_shares = exchange(shares, "col", (2, 4, 8, 16))
    left, right, harm, out = split(
        core.reshape(1), own_shares, swapped(own_shares), w_harm.shape[0], w_out.shape[0]
    )
    return (grad_nodes, left, right, harm, out)


def solution(mesh):
    return jax.shard_map(
        body,
        mesh=mesh,
        in_specs=(
            P(BOTH, None),
            P("row", "col", None, None),
            P("row", "col", None, None),
            P("row", "col", None),
            P("row", "col", None),
            P("row", "col", None),
            P("row", "col"),
            P(),
            P(),
            P(),
            P(),
        ),
        out_specs=(P(BOTH, None), P(), P(), P(), P()),
        check_vma=False,
    )
```

time: 627 us -> 134 us (0.21)
  waiting for transfers between devices: 352 us -> 17.3 us
  blocking collectives: 168 us -> 62 us
  other arithmetic: 30.5 us -> 0.95 us
  local copies, waits for them, and re-layouts: 19.9 us -> 1.73 us
  matrix products: 17.6 us -> 0 us
  Pallas kernels: 0 us -> 15 us
  between operations: 16.3 us -> 1.55 us
  starting transfers between devices: 20.8 us -> 34.4 us
    psum x1 -> x0, waiting for transfers between devices: 352 us -> none  [body(): lax.psum((grad_out, grad_harm, grad_left, grad_right), ('row', 'col'))]
    psum x1 -> x0, blocking collectives: 120 us -> none  [body(): lax.psum((grad_out, grad_harm, grad_left, grad_right), ('row', 'col'))]
    all_to_all x0 -> x4, blocking collectives: none -> 62 us  [exchange(): lax.all_to_all(blocks, axis, 0, 0, tiled=True, axis_index_groups=groups(l...]
    all_gather x1 -> x0, blocking collectives: 48 us -> none  [body(): row_nodes = lax.all_gather(nodes, 'col', axis=0, tiled=True)]
    scatter-add x6 -> x0, other arithmetic: 22.9 us -> none  [the longest x3 11.7 us: turn(): sum_v = sum_v.at[cols].add(grad_z * u_pair * embed)]
    dot_general x18 -> x0, matrix products: 17.6 us -> none  [the longest x3 5.81 us: turn(): jnp.einsum('bop,bpk->ok', g_masked, z_pair, preferred_element_type=jnp.fl...]
    ppermute x4 -> x7, waiting for transfers between devices: 0.01 us -> 17.2 us  [the longest x4 13.8 us: shifted(): lax.ppermute(block, 'row', [(i, i + distance) for i in devices if i + dis...]
    pallas_call x0 -> x5, Pallas kernels: none -> 15 us  [the longest x1 13.2 us: pair_sums(): pl.pallas_call(pair_kernel, out_shape=(like(chips, shard + share, width),...]
  transfers between devices with their start and end apart: 6 -> 8, of which waited for: 1 -> 4; matrix products, arithmetic and copies ran while one was open for 1% -> 0% of each run, Pallas kernels for 0% -> 0%
where the time goes in v1:
time: 134 us; the launch traced here: 133 us
  blocking collectives  62 us (46%)
  starting transfers between devices  34.4 us (26%)
  waiting for transfers between devices  17.3 us (13%)
  Pallas kernels  15 us (11%)
  local copies, waits for them, and re-layouts  1.73 us (1%)
  between operations  1.55 us (1%)
    all_to_all x4, blocking collectives, exchange(): lax.all_to_all(blocks, axis, 0, 0, tiled=True, axis_index_groups=groups(l...  62 us
    ppermute x4, starting transfers between devices, shifted(): lax.ppermute(block, 'row', [(i, i + distance) for i in devices if i + dis...  18.5 us
    ppermute x4, waiting for transfers between devices, shifted(): lax.ppermute(block, 'row', [(i, i + distance) for i in devices if i + dis...  13.8 us
    pallas_call x1, Pallas kernels, pair_sums(): pl.pallas_call(pair_kernel, out_shape=(like(chips, shard + share, width),...  13.2 us
    ppermute x3, starting transfers between devices, swapped(): lax.ppermute(block, 'col', [(i, i ^ 1) for i in range(lax.axis_size('col'...  12.1 us
    all_to_all x1, starting transfers between devices, exchange(): lax.all_to_all(blocks, axis, 0, 0, tiled=True, axis_index_groups=groups(l...  3.86 us
    ppermute x3, waiting for transfers between devices, swapped(): lax.ppermute(block, 'col', [(i, i ^ 1) for i in range(lax.axis_size('col'...  3.49 us
  transfers between devices with their start and end apart: 8, of which 4 were waited for; matrix products, arithmetic and copies ran while one was open for 0% of the time, Pallas kernels for 0%

profile of v1, /device:TPU:1, one launch (start us, length us, event | category | flops | bytes accessed | tf_op | source)
XLA Modules:
  0.0 132.9 jit_solution(2503932324812018928)
XLA Ops:
  0.7 0.8 broadcast_in_dim.2
  1.5 18.8 %all_to_all.25 = bf16[16,32,256]{2,1,0:T(8,128)(2,1)S(1)} all-to-all(bf16[16,32,256]{2,1,0:T(8,128)(2,1)S(1)} %broadcast_in_dim.2), channel_id=1, replica_groups={{0,2,4,6,8,10,12,14,16,18,20,22,24,26,28,30},{1,3,5,7,9,11,13,15,17,19,..., dimensions={0} | all-to-all | bytes 524288 | tf_op jit(solution)/shard_map/all_to_all | solution.py:214
  20.3 4.0 %collective-permute-start = (bf16[512,256]{1,0:T(8,128)(2,1)S(1)}, bf16[512,256]{1,0:T(8,128)(2,1)S(1)}, u32[]{:S(2)}, u32[]{:S(2)}) collective-permute-start(bf16[512,256]{1,0:T(8,128)(2,1)S(1)} %bitcast.15), channel_id=1, source_target_pairs={{0,1},{1,0},{2,3},{3,2},{4,5},{5,4},{6,7},{7,6},{8,9},{9,8},{10,11... | collective-permute-start | bytes 786440 | tf_op jit(solution)/shard_map/ppermute | solution.py:220
  24.4 8.8 %collective-permute-start.1 = (bf16[32,256]{1,0:T(8,128)(2,1)S(1)}, bf16[32,256]{1,0:T(8,128)(2,1)S(1)}, u32[]{:S(2)}, u32[]{:S(2)}) collective-permute-start(bf16[32,256]{1,0:T(8,128)(2,1)S(1)} %copy-done.9), channel_id=1, source_target_pairs={{0,32},{32,64},{64,96},{96,128},{128,160},{160,192},{192,224},{224... | collective-permute-start | bytes 49160 | tf_op jit(solution)/shard_map/ppermute | solution.py:225
  33.2 1.3 collective-permute-start.2
  35.1 0.1 pad_add_fusion.places
  35.3 0.2 copy.20
  35.5 6.5 %collective-permute-done.2 = bf16[32,256]{1,0:T(8,128)(2,1)S(1)} collective-permute-done((bf16[32,256]{1,0:T(8,128)(2,1)S(1)}, bf16[32,256]{1,0:T(8,128)(2,1)S(1)}, u32[]{:S(2)}, u32[]{:S(2)}) %collective-permute-start.2) | collective-permute-done | bytes 16416 | tf_op jit(solution)/shard_map/ppermute | solution.py:225
  42.1 0.6 copy-done.3
  42.7 13.2 %shard_map.146 = (f32[16,56,256]{2,1,0:T(8,128)S(1)}, f32[16,56,256]{2,1,0:T(8,128)S(1)}, f32[96,256]{1,0:T(8,128)S(1)}) custom-call(s32[3]{0:T(128)S(1)} %pad_add_fusion.places, s32[16,128]{1,0:T(8,128)S(1)} %bitcast.18, s32[16,128]{1,0:T(8,128)S(1)} %bitcast.19, s32[16,128]{1,0:T(8,128)S(1)} %bitcast.20, bf16[16,25,128]{2,1,0:T(8,128)(2,1)S(1)} %bitcast.17, ...), custom_call_target="tpu_custom_call" | custom-call | tf_op jit(solution)/shard_map/pallas_call | solution.py:113
  55.9 1.9 %collective-permute-start.3 = (f32[16,56,256]{2,1,0:T(8,128)S(1)}, f32[16,56,256]{2,1,0:T(8,128)S(1)}, u32[]{:S(2)}, u32[]{:S(2)}) collective-permute-start(f32[16,56,256]{2,1,0:T(8,128)S(1)} %get-tuple-element.15), channel_id=1, source_target_pairs={{0,1},{1,0},{2,3},{3,2},{4,5},{5,4},{6,7},{7,6},{8,9},{9,8},{10,11... | collective-permute-start | bytes 2752520 | tf_op jit(solution)/shard_map/ppermute | solution.py:220
  57.9 2.4 %collective-permute-done.3 = f32[16,56,256]{2,1,0:T(8,128)S(1)} collective-permute-done((f32[16,56,256]{2,1,0:T(8,128)S(1)}, f32[16,56,256]{2,1,0:T(8,128)S(1)}, u32[]{:S(2)}, u32[]{:S(2)}) %collective-permute-start.3) | collective-permute-done | bytes 917536 | tf_op jit(solution)/shard_map/ppermute | solution.py:220
  60.3 0.9 add_convert_fusion
  61.2 3.9 %all-to-all-start.1 = ((bf16[16,56,256]{2,1,0:T(8,128)(2,1)}), bf16[16,56,256]{2,1,0:T(8,128)(2,1)S(1)}, u32[]{:S(2)}, u32[]{:S(2)}) async-start(bf16[16,56,256]{2,1,0:T(8,128)(2,1)} %add_convert_fusion), calls=%async_computation.1 | async-start | bytes 917504 | tf_op jit(solution)/shard_map/all_to_all | solution.py:214
  65.0 7.1 %collective-permute-start.5 = (f32[32,256]{1,0:T(8,128)S(1)}, f32[32,256]{1,0:T(8,128)S(1)}, u32[]{:S(2)}, u32[]{:S(2)}) collective-permute-start(f32[32,256]{1,0:T(8,128)S(1)} %get-tuple-element.23), channel_id=1, source_target_pairs={{0,32},{32,64},{64,96},{96,128},{128,160},{160,192},{192,224},{224... | collective-permute-start | bytes 98312 | tf_op jit(solution)/shard_map/ppermute | solution.py:225
  72.1 1.3 collective-permute-start.4
  73.4 7.3 %collective-permute-done.4.upper = f32[32,256]{1,0:T(8,128)S(1)} collective-permute-done((f32[32,256]{1,0:T(8,128)S(1)}, f32[32,256]{1,0:T(8,128)S(1)}, u32[]{:S(2)}, u32[]{:S(2)}) %collective-permute-start.4) | collective-permute-done | bytes 32800 | tf_op jit(solution)/shard_map/ppermute | solution.py:225
  80.7 0.9 shard_map.147
  81.6 8.6 %all_to_all.26.parts = f32[4,24,256]{2,1,0:T(8,128)S(1)} all-to-all(f32[4,24,256]{2,1,0:T(8,128)S(1)} %get-tuple-element.18), channel_id=1, replica_groups={{0,128,256,384},{32,160,288,416},{64,192,320,448},{96,224,352,480},{1,1..., dimensions={0} | all-to-all | bytes 196608 | tf_op jit(solution)/shard_map/all_to_all | solution.py:214
  90.2 20.0 %all_to_all.27.parts = f32[4,24,256]{2,1,0:T(8,128)S(1)} all-to-all(f32[4,24,256]{2,1,0:T(8,128)S(1)} %shard_map.148), channel_id=1, replica_groups={{0,32,64,96},{128,160,192,224},{256,288,320,352},{384,416,448,480},{1,3..., dimensions={0} | all-to-all | bytes 196608 | tf_op jit(solution)/shard_map/all_to_all | solution.py:214
  110.2 14.6 %all_to_all.28.own = bf16[16,24,256]{2,1,0:T(8,128)(2,1)S(1)} all-to-all(bf16[16,24,256]{2,1,0:T(8,128)(2,1)S(1)} %shard_map.149), channel_id=1, replica_groups={{0,2,4,6,8,10,12,14,16,18,20,22,24,26,28,30},{1,3,5,7,9,11,13,15,17,19,..., dimensions={0} | all-to-all | bytes 393216 | tf_op jit(solution)/shard_map/all_to_all | solution.py:214
  124.8 6.1 %collective-permute-start.6 = (bf16[16,24,256]{2,1,0:T(8,128)(2,1)S(1)}, bf16[16,24,256]{2,1,0:T(8,128)(2,1)S(1)}, u32[]{:S(2)}, u32[]{:S(2)}) collective-permute-start(bf16[16,24,256]{2,1,0:T(8,128)(2,1)S(1)} %all_to_all.28.own), channel_id=1, source_target_pairs={{0,1},{1,0},{2,3},{3,2},{4,5},{5,4},{6,7},{7,6},{8,9},{9,8},{10,11... | collective-permute-start | bytes 589832 | tf_op jit(solution)/shard_map/ppermute | solution.py:220
  130.9 1.0 collective-permute-done.6.other
  132.0 0.9 shard_map.150
  (28 shorter events, 0.1 us)
Async XLA Ops:
  0.6 34.6 %copy-start.7 = (bf16[1,16,169,128]{3,1,2,0:T(8,128)(2,1)S(1)}, bf16[1,16,169,128]{3,1,2,0:T(8,128)(2,1)}, u32[]{:S(2)}) copy-start(bf16[1,16,169,128]{3,1,2,0:T(8,128)(2,1)} %param.13) | copy-start | bytes 2076676
  0.6 23.7 %copy-start.9 = (bf16[32,256]{1,0:T(8,128)(2,1)S(1)}, bf16[32,256]{1,0:T(8,128)(2,1)}, u32[]{:S(2)}) copy-start(bf16[32,256]{1,0:T(8,128)(2,1)} %param.11) | copy-start | bytes 49156
  1.5 33.7 %copy-start.8 = (bf16[1,16,25,128]{3,1,2,0:T(8,128)(2,1)S(1)}, bf16[1,16,25,128]{3,1,2,0:T(8,128)(2,1)}, u32[]{:S(2)}) copy-start(bf16[1,16,25,128]{3,1,2,0:T(8,128)(2,1)} %param.12) | copy-start | bytes 307204
  20.3 21.8 %collective-permute-start = (bf16[512,256]{1,0:T(8,128)(2,1)S(1)}, bf16[512,256]{1,0:T(8,128)(2,1)S(1)}, u32[]{:S(2)}, u32[]{:S(2)}) collective-permute-start(bf16[512,256]{1,0:T(8,128)(2,1)S(1)} %bitcast.15), channel_id=1, source_target_pairs={{0,1},{1,0},{2,3},{3,2},{4,5},{5,4},{6,7},{7,6},{8,9},{9,8},{10,11... | collective-permute-start | bytes 786440 | tf_op jit(solution)/shard_map/ppermute | solution.py:220
  24.4 11.2 %collective-permute-start.1 = (bf16[32,256]{1,0:T(8,128)(2,1)S(1)}, bf16[32,256]{1,0:T(8,128)(2,1)S(1)}, u32[]{:S(2)}, u32[]{:S(2)}) collective-permute-start(bf16[32,256]{1,0:T(8,128)(2,1)S(1)} %copy-done.9), channel_id=1, source_target_pairs={{0,32},{32,64},{64,96},{96,128},{128,160},{160,192},{192,224},{224... | collective-permute-start | bytes 49160 | tf_op jit(solution)/shard_map/ppermute | solution.py:225
  33.2 8.9 %collective-permute-start.2 = (bf16[32,256]{1,0:T(8,128)(2,1)S(1)}, bf16[32,256]{1,0:T(8,128)(2,1)S(1)}, u32[]{:S(2)}, u32[]{:S(2)}) collective-permute-start(bf16[32,256]{1,0:T(8,128)(2,1)S(1)} %copy-done.9), channel_id=1, source_target_pairs={{32,0},{64,32},{96,64},{128,96},{160,128},{192,160},{224,192},{256... | collective-permute-start | bytes 49160 | tf_op jit(solution)/shard_map/ppermute | solution.py:225
  35.3 6.8 %copy-start = (bf16[256,256]{1,0:T(8,128)(2,1)S(1)}, bf16[256,256]{1,0:T(8,128)(2,1)}, u32[]{:S(2)}) copy-start(bf16[256,256]{1,0:T(8,128)(2,1)} %w_left.3) | copy-start | bytes 393220
  35.3 6.8 %copy-start.1 = (bf16[256,256]{1,0:T(8,128)(2,1)S(1)}, bf16[256,256]{1,0:T(8,128)(2,1)}, u32[]{:S(2)}) copy-start(bf16[256,256]{1,0:T(8,128)(2,1)} %w_right.3) | copy-start | bytes 393220
  35.3 6.8 %copy-start.4 = (s32[1,16,128]{2,1,0:T(8,128)S(1)}, s32[1,16,128]{2,1,0:T(8,128)}, u32[]{:S(2)}) copy-start(s32[1,16,128]{2,1,0:T(8,128)} %param.14) | copy-start | bytes 24580
  35.3 6.8 %copy-start.5 = (s32[1,16,128]{2,1,0:T(8,128)S(1)}, s32[1,16,128]{2,1,0:T(8,128)}, u32[]{:S(2)}) copy-start(s32[1,16,128]{2,1,0:T(8,128)} %param.15) | copy-start | bytes 24580
  35.3 6.8 %copy-start.6 = (s32[1,16,128]{2,1,0:T(8,128)S(1)}, s32[1,16,128]{2,1,0:T(8,128)}, u32[]{:S(2)}) copy-start(s32[1,16,128]{2,1,0:T(8,128)} %param.16) | copy-start | bytes 24580
  35.5 6.6 %copy-start.2 = (bf16[169,256]{1,0:T(8,128)(2,1)S(1)}, bf16[169,256]{1,0:T(8,128)(2,1)}, u32[]{:S(2)}) copy-start(bf16[169,256]{1,0:T(8,128)(2,1)} %w_out.1) | copy-start | bytes 259588
  42.0 0.7 copy-start.3
  55.9 4.4 %collective-permute-start.3 = (f32[16,56,256]{2,1,0:T(8,128)S(1)}, f32[16,56,256]{2,1,0:T(8,128)S(1)}, u32[]{:S(2)}, u32[]{:S(2)}) collective-permute-start(f32[16,56,256]{2,1,0:T(8,128)S(1)} %get-tuple-element.15), channel_id=1, source_target_pairs={{0,1},{1,0},{2,3},{3,2},{4,5},{5,4},{6,7},{7,6},{8,9},{9,8},{10,11... | collective-permute-start | bytes 2752520 | tf_op jit(solution)/shard_map/ppermute | solution.py:220
  61.2 19.5 %all-to-all-start.1 = ((bf16[16,56,256]{2,1,0:T(8,128)(2,1)}), bf16[16,56,256]{2,1,0:T(8,128)(2,1)S(1)}, u32[]{:S(2)}, u32[]{:S(2)}) async-start(bf16[16,56,256]{2,1,0:T(8,128)(2,1)} %add_convert_fusion), calls=%async_computation.1 | async-start | bytes 917504 | tf_op jit(solution)/shard_map/all_to_all | solution.py:214
  65.0 8.4 %collective-permute-start.5 = (f32[32,256]{1,0:T(8,128)S(1)}, f32[32,256]{1,0:T(8,128)S(1)}, u32[]{:S(2)}, u32[]{:S(2)}) collective-permute-start(f32[32,256]{1,0:T(8,128)S(1)} %get-tuple-element.23), channel_id=1, source_target_pairs={{0,32},{32,64},{64,96},{96,128},{128,160},{160,192},{192,224},{224... | collective-permute-start | bytes 98312 | tf_op jit(solution)/shard_map/ppermute | solution.py:225
  72.1 8.6 %collective-permute-start.4 = (f32[32,256]{1,0:T(8,128)S(1)}, f32[32,256]{1,0:T(8,128)S(1)}, u32[]{:S(2)}, u32[]{:S(2)}) collective-permute-start(f32[32,256]{1,0:T(8,128)S(1)} %get-tuple-element.24), channel_id=1, source_target_pairs={{32,0},{64,32},{96,64},{128,96},{160,128},{192,160},{224,192},{256... | collective-permute-start | bytes 98312 | tf_op jit(solution)/shard_map/ppermute | solution.py:225
  124.8 7.2 %collective-permute-start.6 = (bf16[16,24,256]{2,1,0:T(8,128)(2,1)S(1)}, bf16[16,24,256]{2,1,0:T(8,128)(2,1)S(1)}, u32[]{:S(2)}, u32[]{:S(2)}) collective-permute-start(bf16[16,24,256]{2,1,0:T(8,128)(2,1)S(1)} %all_to_all.28.own), channel_id=1, source_target_pairs={{0,1},{1,0},{2,3},{3,2},{4,5},{5,4},{6,7},{7,6},{8,9},{9,8},{10,11... | collective-permute-start | bytes 589832 | tf_op jit(solution)/shard_map/ppermute | solution.py:220

commit v2 on v1

v2 whole, which is shorter than its diff:
```python
import jax
import jax.numpy as jnp
from jax import lax
from jax.experimental import pallas as pl
from jax.experimental.pallas import tpu as pltpu
from jax.sharding import PartitionSpec as P

F32, BF16 = jnp.float32, jnp.bfloat16
VMEM = pl.BlockSpec(memory_space=pltpu.VMEM)
SMEM = pl.BlockSpec(memory_space=pltpu.SMEM)
PARAMS = pltpu.CompilerParams(vmem_limit_bytes=48 * 1024 * 1024)
BOTH = ("row", "col")
BLOCKS_PER_STEP = 8
OUT_ROWS = 176
X_BITS, Z_BITS, CHIP_BITS, COL_BITS = (4, 8), (1, 2), (2, 4, 8, 16), (1, 2, 4, 8, 16)


def like(*shape):
    return jax.ShapeDtypeStruct(shape, F32)


def dot(a, b, da, db):
    return lax.dot_general(a, b, (((da,), (db,)), ((), ())), preferred_element_type=F32)


def halves(x):
    high = x.astype(BF16)
    return high, (x - high.astype(F32)).astype(BF16)


def pair_kernel(
    places, rows, cols, mask, harm, grads, row_nodes, column_nodes, w_left, w_right, w_harm, w_out,
    keep, send, sum_v, u_parts, v_parts, harm_t, out_t, sum_u, weights,
):
    count, column_base, core = places[0], places[1], places[2]
    width = w_left.shape[0]
    atoms, near = row_nodes.shape[0], column_nodes.shape[0]
    shard = near // 3
    pairs = BLOCKS_PER_STEP * mask.shape[1]
    orbitals, harmonics = w_out.shape[0], w_harm.shape[0]
    for parts, weight, nodes in ((u_parts, w_left, row_nodes), (v_parts, w_right, column_nodes)):
        high, low = halves(dot(weight[...], nodes[...], 0, 1))
        parts[:width] = high
        parts[width:] = low
    harm_t[...] = w_harm[...].astype(F32).T.astype(BF16)
    out_t[...] = w_out[...].astype(F32).T.astype(BF16)
    for total in (sum_u, sum_v, weights):
        total[...] = jnp.zeros_like(total)
    at_out = 2 * width
    at_harm = at_out + OUT_ROWS

    def line(ref, first):
        return jnp.concatenate(
            [ref[pl.ds(first + k, 1), :] for k in range(BLOCKS_PER_STEP)], axis=1
        )

    def step(i, carry):
        first = BLOCKS_PER_STEP * i
        live = jnp.concatenate(
            [
                mask[pl.ds(first + k, 1), :] * (first + k < count).astype(jnp.int32)
                for k in range(BLOCKS_PER_STEP)
            ],
            axis=1,
        )
        g = jnp.concatenate([grads[first + k] for k in range(BLOCKS_PER_STEP)], axis=1)
        g = g * live.astype(F32).astype(BF16)
        h = jnp.concatenate([harm[first + k] for k in range(BLOCKS_PER_STEP)], axis=1)
        at_u = lax.broadcasted_iota(jnp.int32, (atoms, pairs), 0) == line(rows, first)
        at_v = lax.broadcasted_iota(jnp.int32, (near, pairs), 0) == line(cols, first) - column_base
        pick_u = at_u.astype(F32).astype(BF16)
        pick_v = at_v.astype(F32).astype(BF16)
        parts = dot(u_parts[...], pick_u, 1, 0)
        u = parts[:width] + parts[width:]
        parts = dot(v_parts[...], pick_v, 1, 0)
        v = parts[:width] + parts[width:]
        e = dot(harm_t[...], h, 1, 0)
        gz = dot(out_t[...], g, 1, 0)
        uv = u * v
        weights[at_out : at_out + orbitals] += dot(g, (uv * e).astype(BF16), 1, 1)
        weights[at_harm : at_harm + harmonics] += dot(h, (gz * uv).astype(BF16), 1, 1)
        ge = gz * e
        high, low = halves(ge * v)
        sum_u[...] += dot(pick_u, high, 1, 1) + dot(pick_u, low, 1, 1)
        high, low = halves(ge * u)
        sum_v[...] += dot(pick_v, high, 1, 1) + dot(pick_v, low, 1, 1)
        return carry

    lax.fori_loop(0, lax.div(count + BLOCKS_PER_STEP - 1, BLOCKS_PER_STEP), step, 0)
    for at, nodes, sums in ((0, row_nodes, sum_u), (width, column_nodes, sum_v)):
        high, low = halves(sums[...])
        weights[at : at + width] = dot(nodes[...], high, 0, 0) + dot(nodes[...], low, 0, 0)
    chips, chunk = keep.shape[0], keep.shape[1]
    share = chunk - shard
    for chip in range(chips):
        for to, which in ((keep, core), (send, 1 - core)):
            start = pl.multiple_of((2 * chip + which) * shard, 8)
            to[chip, :shard] = sum_u[pl.ds(start, shard), :]
            start = pl.multiple_of((which * chips + chip) * share, 8)
            to[chip, shard:] = weights[pl.ds(start, share), :]


def pair_sums(places, rows, cols, mask, harm, grads, row_nodes, column_nodes, weights_in, chips, share):
    atoms, width = row_nodes.shape
    near = column_nodes.shape[0]
    chunk = near // 3 + share
    w_harm, w_out = weights_in[2:]
    return pl.pallas_call(
        pair_kernel,
        out_shape=(like(chips, chunk, width), like(chips, chunk, width), like(near, width)),
        in_specs=[SMEM] + [VMEM] * 11,
        out_specs=(VMEM,) * 3,
        scratch_shapes=[
            pltpu.VMEM((2 * width, atoms), BF16),
            pltpu.VMEM((2 * width, near), BF16),
            pltpu.VMEM(w_harm.shape[::-1], BF16),
            pltpu.VMEM(w_out.shape[::-1], BF16),
            pltpu.VMEM((atoms, width), F32),
            pltpu.VMEM((2 * chips * share, width), F32),
        ],
        compiler_params=PARAMS,
    )(places, rows, cols, mask, harm, grads, row_nodes, column_nodes, *weights_in)


def total_of(parts):
    total = parts[0].astype(F32)
    for i in range(1, parts.shape[0]):
        total = total + parts[i].astype(F32)
    return total


def weighted(sums, weight):
    high, low = halves(sums)
    return dot(high, weight[...], 1, 1) + dot(low, weight[...], 1, 1)


def when(condition, block):
    return jnp.where(condition, block, jnp.zeros_like(block))


def across_x_kernel(places, parts, sum_v, w_left, row_part, out):
    x, z = places[0], places[1]
    shard = sum_v.shape[0] // 3
    last = places[2] - 1
    total = total_of(parts)
    row_part[...] = weighted(total[:shard], w_left)
    upper = when(z == 0, sum_v[:shard])
    lower = when(z == last, sum_v[2 * shard :])
    for to in range(out.shape[0]):
        out[to, :shard] = when(x - 1 == to, upper) + when(x + 1 == to, lower)
        out[to, shard:] = total[shard:]


def across_z_kernel(places, parts, sum_v, out):
    z = places[1]
    shard = sum_v.shape[0] // 3
    last = places[2] - 1
    total = total_of(parts)
    upper, lower = sum_v[:shard], sum_v[2 * shard :]
    crossed = total[:shard]
    for to in range(out.shape[0]):
        ends = jnp.logical_or(
            jnp.logical_and(z == 0, to == last), jnp.logical_and(z == last, to == 0)
        )
        out[to, :shard] = when(z - 1 == to, upper) + when(z + 1 == to, lower) + when(ends, crossed)
        out[to, shard:] = total[shard:]


def node_kernel(parts, sum_v, row_part, w_right, grad_nodes, shares):
    shard = sum_v.shape[0] // 3
    total = total_of(parts)
    columns = sum_v[shard : 2 * shard] + total[:shard]
    grad_nodes[...] = row_part[...] + weighted(columns, w_right)
    for chip in range(shares.shape[0]):
        shares[chip] = total[shard:].astype(shares.dtype)


def call(kernel, out_shape, *operands, scalars=1):
    specs = [SMEM] * scalars + [VMEM] * (len(operands) - scalars)
    return pl.pallas_call(
        kernel,
        out_shape=out_shape,
        in_specs=specs,
        out_specs=jax.tree.map(lambda _: VMEM, out_shape),
        compiler_params=PARAMS,
    )(*operands)


def split_kernel(core, own, other, left, right, harm, out, whole):
    chips, share = own.shape[0], own.shape[1]
    width = left.shape[0]
    for which, part in ((core[0], own), (1 - core[0], other)):
        for chip in range(chips):
            start = pl.multiple_of((which * chips + chip) * share, 8)
            whole[pl.ds(start, share), :] = part[chip].astype(F32)
    left[...] = whole[:width]
    right[...] = whole[width : 2 * width]
    at_out = 2 * width
    out[...] = whole[at_out : at_out + out.shape[0]]
    at_harm = at_out + OUT_ROWS
    harm[...] = whole[at_harm : at_harm + harm.shape[0]]


def split(core, own, other, harmonics, orbitals):
    chips, share, width = own.shape
    return pl.pallas_call(
        split_kernel,
        out_shape=(
            like(width, width), like(width, width), like(harmonics, width), like(orbitals, width),
        ),
        in_specs=[SMEM, VMEM, VMEM],
        out_specs=(VMEM,) * 4,
        scratch_shapes=[pltpu.VMEM((2 * chips * share, width), F32)],
        compiler_params=PARAMS,
    )(core, own, other)


def groups(size, bits):
    mask = sum(bits)
    found = {}
    for i in range(size):
        found.setdefault(i & ~mask, []).append(i)
    return list(found.values())


def exchange(blocks, axis, bits):
    return lax.all_to_all(
        blocks, axis, 0, 0, tiled=True, axis_index_groups=groups(lax.axis_size(axis), bits)
    )


def swapped(block):
    return lax.ppermute(block, "col", [(i, i ^ 1) for i in range(lax.axis_size("col"))])


def shifted(block, distance):
    devices = range(lax.axis_size("row"))
    return lax.ppermute(
        block, "row", [(i, i + distance) for i in devices if i + distance in devices]
    )


def repeated(block, copies):
    return jnp.broadcast_to(block[None], (copies,) + block.shape)


def body(
    nodes,
    harmonics,
    grad_blocks,
    pair_rows,
    pair_cols,
    pair_mask,
    block_counts,
    w_left,
    w_right,
    w_harm,
    w_out,
):
    shard, width = nodes.shape
    columns = lax.axis_size("col")
    chips = columns // 2
    share = 24
    spread = 4
    row = lax.axis_index("row")
    core = jnp.bitwise_and(lax.axis_index("col"), 1)
    column_nodes = jnp.concatenate([shifted(nodes, 1), nodes, shifted(nodes, -1)])
    row_nodes = exchange(repeated(nodes, columns), "col", COL_BITS).reshape(-1, width)
    places = jnp.stack([block_counts[0, 0], (row - 1) * shard, core]).astype(jnp.int32)
    keep, send, sum_v = pair_sums(
        places, pair_rows[0], pair_cols[0], pair_mask[0], harmonics[0], grad_blocks[0],
        row_nodes, column_nodes, (w_left, w_right, w_harm, w_out), chips, share,
    )
    parts = (keep + swapped(send)).astype(BF16)
    parts = exchange(parts, "col", CHIP_BITS)
    at = jnp.stack([row // spread, row % spread, jnp.int32(spread)]).astype(jnp.int32)
    chunks = like(spread, shard + share, width)
    row_part, parts = call(
        across_x_kernel, (like(shard, width), chunks), at, parts, sum_v, w_left
    )
    parts = exchange(parts, "row", X_BITS)
    parts = call(across_z_kernel, chunks, at, parts, sum_v)
    parts = exchange(parts, "row", Z_BITS)
    grad_nodes, shares = call(
        node_kernel,
        (like(shard, width), jax.ShapeDtypeStruct((chips, share, width), BF16)),
        parts, sum_v, row_part, w_right, scalars=0,
    )
    own_shares = exchange(shares, "col", CHIP_BITS)
    left, right, harm, out = split(
        core.reshape(1), own_shares, swapped(own_shares), w_harm.shape[0], w_out.shape[0]
    )
    return (grad_nodes, left, right, harm, out)


def solution(mesh):
    return jax.shard_map(
        body,
        mesh=mesh,
        in_specs=(
            P(BOTH, None),
            P("row", "col", None, None),
            P("row", "col", None, None),
            P("row", "col", None),
            P("row", "col", None),
            P("row", "col", None),
            P("row", "col"),
            P(),
            P(),
            P(),
            P(),
        ),
        out_specs=(P(BOTH, None), P(), P(), P(), P()),
        check_vma=False,
    )
```

time: 134 us -> 123 us (0.918)
  blocking collectives: 62 us -> 44.6 us
  waiting for transfers between devices: 17.3 us -> 23.9 us
  Pallas kernels: 15 us -> 11.9 us
  starting transfers between devices: 34.4 us -> 36.9 us
    all_to_all x4 -> x3, blocking collectives: 62 us -> 44.6 us  [exchange(): lax.all_to_all(blocks, axis, 0, 0, tiled=True, axis_index_groups=groups(l...]
    all_to_all x1 -> x2, starting transfers between devices: 3.86 us -> 18.8 us  [exchange(): lax.all_to_all(blocks, axis, 0, 0, tiled=True, axis_index_groups=groups(l...]
    all_to_all x1 -> x2, waiting for transfers between devices: 0.01 us -> 14.4 us  [exchange(): lax.all_to_all(blocks, axis, 0, 0, tiled=True, axis_index_groups=groups(l...]
    ppermute x4 -> x2, starting transfers between devices: 18.5 us -> 9.88 us  [shifted(): lax.ppermute(block, 'row', [(i, i + distance) for i in devices if i + dis...]
    ppermute x4 -> x2, waiting for transfers between devices: 13.8 us -> 6.04 us  [shifted(): lax.ppermute(block, 'row', [(i, i + distance) for i in devices if i + dis...]
    ppermute x3 -> x2, starting transfers between devices: 12.1 us -> 8.24 us  [swapped(): lax.ppermute(block, 'col', [(i, i ^ 1) for i in range(lax.axis_size('col'...]
    pallas_call x4, Pallas kernels: 14.1 us -> 11 us  [the longest x1 8.87 us: pair_sums(): pl.pallas_call(pair_kernel, out_shape=(like(chips, chunk, width), like(ch...]
    ppermute x3 -> x2, waiting for transfers between devices: 3.49 us -> 3.49 us  [swapped(): lax.ppermute(block, 'col', [(i, i ^ 1) for i in range(lax.axis_size('col'...]
  transfers between devices with their start and end apart: 8 -> 6, of which waited for: 4 -> 4; matrix products, arithmetic and copies ran while one was open for 0% -> 0% of each run, Pallas kernels for 0% -> 0%
where the time goes in v2:
time: 123 us; the launch traced here: 122 us
  blocking collectives  44.6 us (36%)
  starting transfers between devices  36.9 us (30%)
  waiting for transfers between devices  23.9 us (19%)
  Pallas kernels  11.9 us (10%)
  local copies, waits for them, and re-layouts  2.5 us (2%)
  between operations  1.51 us (1%)
    all_to_all x3, blocking collectives, exchange(): lax.all_to_all(blocks, axis, 0, 0, tiled=True, axis_index_groups=groups(l...  44.6 us
    all_to_all x2, starting transfers between devices, exchange(): lax.all_to_all(blocks, axis, 0, 0, tiled=True, axis_index_groups=groups(l...  18.8 us
    all_to_all x2, waiting for transfers between devices, exchange(): lax.all_to_all(blocks, axis, 0, 0, tiled=True, axis_index_groups=groups(l...  14.4 us
    ppermute x2, starting transfers between devices, shifted(): lax.ppermute(block, 'row', [(i, i + distance) for i in devices if i + dis...  9.88 us
    pallas_call x1, Pallas kernels, pair_sums(): pl.pallas_call(pair_kernel, out_shape=(like(chips, chunk, width), like(ch...  8.87 us
    ppermute x2, starting transfers between devices, swapped(): lax.ppermute(block, 'col', [(i, i ^ 1) for i in range(lax.axis_size('col'...  8.24 us
    ppermute x2, waiting for transfers between devices, shifted(): lax.ppermute(block, 'row', [(i, i + distance) for i in devices if i + dis...  6.04 us
    ppermute x2, waiting for transfers between devices, swapped(): lax.ppermute(block, 'col', [(i, i ^ 1) for i in range(lax.axis_size('col'...  3.49 us
  transfers between devices with their start and end apart: 6, of which 4 were waited for; matrix products, arithmetic and copies ran while one was open for 0% of the time, Pallas kernels for 0%

profile of v2, /device:TPU:1, one launch (start us, length us, event | category | flops | bytes accessed | tf_op | source)
XLA Modules:
  0.0 122.3 jit_solution(11538882192468515223)
XLA Ops:
  0.6 1.6 %broadcast_in_dim.2 = bf16[32,32,256]{2,1,0:T(8,128)(2,1)} broadcast(bf16[32,256]{1,0:T(8,128)(2,1)} %param.11), dimensions={1,2} | broadcast | bytes 540672 | tf_op jit(solution)/shard_map/broadcast_in_dim | solution.py:244
  2.2 10.5 %all-to-all-start = ((bf16[32,32,256]{2,1,0:T(8,128)(2,1)}), bf16[32,32,256]{2,1,0:T(8,128)(2,1)S(1)}, u32[]{:S(2)}, u32[]{:S(2)}) async-start(bf16[32,32,256]{2,1,0:T(8,128)(2,1)} %broadcast_in_dim.2), calls=%async_computation | async-start | bytes 1048576 | tf_op jit(solution)/shard_map/all_to_all | solution.py:227
  12.8 8.6 %collective-permute-start = (bf16[32,256]{1,0:T(8,128)(2,1)S(1)}, bf16[32,256]{1,0:T(8,128)(2,1)S(1)}, u32[]{:S(2)}, u32[]{:S(2)}) collective-permute-start(bf16[32,256]{1,0:T(8,128)(2,1)S(1)} %copy-done.9), channel_id=1, source_target_pairs={{0,32},{32,64},{64,96},{96,128},{128,160},{160,192},{192,224},{224... | collective-permute-start | bytes 49160 | tf_op jit(solution)/shard_map/ppermute | solution.py:238
  21.4 1.3 %collective-permute-start.1 = (bf16[32,256]{1,0:T(8,128)(2,1)S(1)}, bf16[32,256]{1,0:T(8,128)(2,1)S(1)}, u32[]{:S(2)}, u32[]{:S(2)}) collective-permute-start(bf16[32,256]{1,0:T(8,128)(2,1)S(1)} %copy-done.9), channel_id=1, source_target_pairs={{32,0},{64,32},{96,64},{128,96},{160,128},{192,160},{224,192},{256... | collective-permute-start | bytes 49160 | tf_op jit(solution)/shard_map/ppermute | solution.py:238
  23.3 0.1 pad_add_fusion.1.places
  23.5 0.2 copy.20
  23.7 6.0 %collective-permute-done.1 = bf16[32,256]{1,0:T(8,128)(2,1)S(1)} collective-permute-done((bf16[32,256]{1,0:T(8,128)(2,1)S(1)}, bf16[32,256]{1,0:T(8,128)(2,1)S(1)}, u32[]{:S(2)}, u32[]{:S(2)}) %collective-permute-start.1) | collective-permute-done | bytes 16416 | tf_op jit(solution)/shard_map/ppermute | solution.py:238
  29.8 0.6 copy-done.3
  30.5 8.9 %shard_map.146 = (f32[16,56,256]{2,1,0:T(8,128)S(1)}, f32[16,56,256]{2,1,0:T(8,128)S(1)}, f32[96,256]{1,0:T(8,128)S(1)}) custom-call(s32[3]{0:T(128)S(1)} %pad_add_fusion.1.places, s32[16,128]{1,0:T(8,128)S(1)} %bitcast.19, s32[16,128]{1,0:T(8,128)S(1)} %bitcast.20, s32[16,128]{1,0:T(8,128)S(1)} %bitcast.21, bf16[16,25,128]{2,1,0:T(8,128)(2,1)S(1)} %bitcast.18, ...), custom_call_target="tpu_custom_call" | custom-call | tf_op jit(solution)/shard_map/pallas_call | solution.py:108
  39.4 1.9 %collective-permute-start.2 = (f32[16,56,256]{2,1,0:T(8,128)S(1)}, f32[16,56,256]{2,1,0:T(8,128)S(1)}, u32[]{:S(2)}, u32[]{:S(2)}) collective-permute-start(f32[16,56,256]{2,1,0:T(8,128)S(1)} %get-tuple-element.17), channel_id=1, source_target_pairs={{0,1},{1,0},{2,3},{3,2},{4,5},{5,4},{6,7},{7,6},{8,9},{9,8},{10,11... | collective-permute-start | bytes 2752520 | tf_op jit(solution)/shard_map/ppermute | solution.py:233
  41.3 2.4 %collective-permute-done.2 = f32[16,56,256]{2,1,0:T(8,128)S(1)} collective-permute-done((f32[16,56,256]{2,1,0:T(8,128)S(1)}, f32[16,56,256]{2,1,0:T(8,128)S(1)}, u32[]{:S(2)}, u32[]{:S(2)}) %collective-permute-start.2) | collective-permute-done | bytes 917536 | tf_op jit(solution)/shard_map/ppermute | solution.py:233
  43.7 0.9 add_convert_fusion
  44.6 8.2 %all-to-all-start.1 = ((bf16[16,56,256]{2,1,0:T(8,128)(2,1)}), bf16[16,56,256]{2,1,0:T(8,128)(2,1)S(1)}, u32[]{:S(2)}, u32[]{:S(2)}) async-start(bf16[16,56,256]{2,1,0:T(8,128)(2,1)} %add_convert_fusion), calls=%async_computation.1 | async-start | bytes 917504 | tf_op jit(solution)/shard_map/all_to_all | solution.py:227
  52.8 0.1 pad_add_fusion.places
  52.9 14.4 %all-to-all-done.1.parts = bf16[16,56,256]{2,1,0:T(8,128)(2,1)S(1)} async-done(((bf16[16,56,256]{2,1,0:T(8,128)(2,1)}), bf16[16,56,256]{2,1,0:T(8,128)(2,1)S(1)}, u32[]{:S(2)}, u32[]{:S(2)}) %all-to-all-start.1) | async-done | bytes 458784 | tf_op jit(solution)/shard_map/all_to_all | solution.py:227
  67.3 0.7 shard_map.147
  68.0 10.6 %all_to_all.25.parts = f32[4,56,256]{2,1,0:T(8,128)S(1)} all-to-all(f32[4,56,256]{2,1,0:T(8,128)S(1)} %get-tuple-element.19), channel_id=1, replica_groups={{0,128,256,384},{32,160,288,416},{64,192,320,448},{96,224,352,480},{1,1..., dimensions={0} | all-to-all | bytes 458752 | tf_op jit(solution)/shard_map/all_to_all | solution.py:227
  78.6 0.6 shard_map.148
  79.2 21.8 %all_to_all.26.parts = f32[4,56,256]{2,1,0:T(8,128)S(1)} all-to-all(f32[4,56,256]{2,1,0:T(8,128)S(1)} %shard_map.148), channel_id=1, replica_groups={{0,32,64,96},{128,160,192,224},{256,288,320,352},{384,416,448,480},{1,3..., dimensions={0} | all-to-all | bytes 458752 | tf_op jit(solution)/shard_map/all_to_all | solution.py:227
  101.0 0.8 shard_map.149
  101.8 12.2 %all_to_all.27.own = bf16[16,24,256]{2,1,0:T(8,128)(2,1)S(1)} all-to-all(bf16[16,24,256]{2,1,0:T(8,128)(2,1)S(1)} %get-tuple-element.22), channel_id=1, replica_groups={{0,2,4,6,8,10,12,14,16,18,20,22,24,26,28,30},{1,3,5,7,9,11,13,15,17,19,..., dimensions={0} | all-to-all | bytes 393216 | tf_op jit(solution)/shard_map/all_to_all | solution.py:227
  114.0 6.3 %collective-permute-start.3 = (bf16[16,24,256]{2,1,0:T(8,128)(2,1)S(1)}, bf16[16,24,256]{2,1,0:T(8,128)(2,1)S(1)}, u32[]{:S(2)}, u32[]{:S(2)}) collective-permute-start(bf16[16,24,256]{2,1,0:T(8,128)(2,1)S(1)} %all_to_all.27.own), channel_id=1, source_target_pairs={{0,1},{1,0},{2,3},{3,2},{4,5},{5,4},{6,7},{7,6},{8,9},{9,8},{10,11... | collective-permute-start | bytes 589832 | tf_op jit(solution)/shard_map/ppermute | solution.py:233
  120.3 1.0 collective-permute-done.3.other
  121.4 0.9 shard_map.150
  (23 shorter events, 0.1 us)
Async XLA Ops:
  2.2 10.6 %copy-start.9 = (bf16[32,256]{1,0:T(8,128)(2,1)S(1)}, bf16[32,256]{1,0:T(8,128)(2,1)}, u32[]{:S(2)}) copy-start(bf16[32,256]{1,0:T(8,128)(2,1)} %param.11) | copy-start | bytes 49156
  2.2 21.2 %copy-start.8 = (bf16[1,16,25,128]{3,1,2,0:T(8,128)(2,1)S(1)}, bf16[1,16,25,128]{3,1,2,0:T(8,128)(2,1)}, u32[]{:S(2)}) copy-start(bf16[1,16,25,128]{3,1,2,0:T(8,128)(2,1)} %param.12) | copy-start | bytes 307204
  2.2 21.2 %copy-start.7 = (bf16[1,16,169,128]{3,1,2,0:T(8,128)(2,1)S(1)}, bf16[1,16,169,128]{3,1,2,0:T(8,128)(2,1)}, u32[]{:S(2)}) copy-start(bf16[1,16,169,128]{3,1,2,0:T(8,128)(2,1)} %param.13) | copy-start | bytes 2076676
  2.2 27.6 %all-to-all-start = ((bf16[32,32,256]{2,1,0:T(8,128)(2,1)}), bf16[32,32,256]{2,1,0:T(8,128)(2,1)S(1)}, u32[]{:S(2)}, u32[]{:S(2)}) async-start(bf16[32,32,256]{2,1,0:T(8,128)(2,1)} %broadcast_in_dim.2), calls=%async_computation | async-start | bytes 1048576 | tf_op jit(solution)/shard_map/all_to_all | solution.py:227
  12.8 10.9 %collective-permute-start = (bf16[32,256]{1,0:T(8,128)(2,1)S(1)}, bf16[32,256]{1,0:T(8,128)(2,1)S(1)}, u32[]{:S(2)}, u32[]{:S(2)}) collective-permute-start(bf16[32,256]{1,0:T(8,128)(2,1)S(1)} %copy-done.9), channel_id=1, source_target_pairs={{0,32},{32,64},{64,96},{96,128},{128,160},{160,192},{192,224},{224... | collective-permute-start | bytes 49160 | tf_op jit(solution)/shard_map/ppermute | solution.py:238
  21.4 8.4 %collective-permute-start.1 = (bf16[32,256]{1,0:T(8,128)(2,1)S(1)}, bf16[32,256]{1,0:T(8,128)(2,1)S(1)}, u32[]{:S(2)}, u32[]{:S(2)}) collective-permute-start(bf16[32,256]{1,0:T(8,128)(2,1)S(1)} %copy-done.9), channel_id=1, source_target_pairs={{32,0},{64,32},{96,64},{128,96},{160,128},{192,160},{224,192},{256... | collective-permute-start | bytes 49160 | tf_op jit(solution)/shard_map/ppermute | solution.py:238
  23.5 6.3 %copy-start = (bf16[256,256]{1,0:T(8,128)(2,1)S(1)}, bf16[256,256]{1,0:T(8,128)(2,1)}, u32[]{:S(2)}) copy-start(bf16[256,256]{1,0:T(8,128)(2,1)} %w_left.3) | copy-start | bytes 393220
  23.5 6.3 %copy-start.1 = (bf16[256,256]{1,0:T(8,128)(2,1)S(1)}, bf16[256,256]{1,0:T(8,128)(2,1)}, u32[]{:S(2)}) copy-start(bf16[256,256]{1,0:T(8,128)(2,1)} %w_right.3) | copy-start | bytes 393220
  23.5 6.3 %copy-start.4 = (s32[1,16,128]{2,1,0:T(8,128)S(1)}, s32[1,16,128]{2,1,0:T(8,128)}, u32[]{:S(2)}) copy-start(s32[1,16,128]{2,1,0:T(8,128)} %param.14) | copy-start | bytes 24580
  23.5 6.3 %copy-start.5 = (s32[1,16,128]{2,1,0:T(8,128)S(1)}, s32[1,16,128]{2,1,0:T(8,128)}, u32[]{:S(2)}) copy-start(s32[1,16,128]{2,1,0:T(8,128)} %param.15) | copy-start | bytes 24580
  23.5 6.3 %copy-start.6 = (s32[1,16,128]{2,1,0:T(8,128)S(1)}, s32[1,16,128]{2,1,0:T(8,128)}, u32[]{:S(2)}) copy-start(s32[1,16,128]{2,1,0:T(8,128)} %param.16) | copy-start | bytes 24580
  23.7 6.1 %copy-start.2 = (bf16[169,256]{1,0:T(8,128)(2,1)S(1)}, bf16[169,256]{1,0:T(8,128)(2,1)}, u32[]{:S(2)}) copy-start(bf16[169,256]{1,0:T(8,128)(2,1)} %w_out.1) | copy-start | bytes 259588
  29.8 0.7 copy-start.3
  39.4 4.4 %collective-permute-start.2 = (f32[16,56,256]{2,1,0:T(8,128)S(1)}, f32[16,56,256]{2,1,0:T(8,128)S(1)}, u32[]{:S(2)}, u32[]{:S(2)}) collective-permute-start(f32[16,56,256]{2,1,0:T(8,128)S(1)} %get-tuple-element.17), channel_id=1, source_target_pairs={{0,1},{1,0},{2,3},{3,2},{4,5},{5,4},{6,7},{7,6},{8,9},{9,8},{10,11... | collective-permute-start | bytes 2752520 | tf_op jit(solution)/shard_map/ppermute | solution.py:233
  44.6 22.7 %all-to-all-start.1 = ((bf16[16,56,256]{2,1,0:T(8,128)(2,1)}), bf16[16,56,256]{2,1,0:T(8,128)(2,1)S(1)}, u32[]{:S(2)}, u32[]{:S(2)}) async-start(bf16[16,56,256]{2,1,0:T(8,128)(2,1)} %add_convert_fusion), calls=%async_computation.1 | async-start | bytes 917504 | tf_op jit(solution)/shard_map/all_to_all | solution.py:227
  114.0 7.4 %collective-permute-start.3 = (bf16[16,24,256]{2,1,0:T(8,128)(2,1)S(1)}, bf16[16,24,256]{2,1,0:T(8,128)(2,1)S(1)}, u32[]{:S(2)}, u32[]{:S(2)}) collective-permute-start(bf16[16,24,256]{2,1,0:T(8,128)(2,1)S(1)} %all_to_all.27.own), channel_id=1, source_target_pairs={{0,1},{1,0},{2,3},{3,2},{4,5},{5,4},{6,7},{7,6},{8,9},{9,8},{10,11... | collective-permute-start | bytes 589832 | tf_op jit(solution)/shard_map/ppermute | solution.py:233

commit v3 on v2

--- a/solution.py
+++ b/solution.py
@@ -38,10 +38,10 @@
     shard = near // 3
     pairs = BLOCKS_PER_STEP * mask.shape[1]
     orbitals, harmonics = w_out.shape[0], w_harm.shape[0]
-    for parts, weight, nodes in ((u_parts, w_left, row_nodes), (v_parts, w_right, column_nodes)):
-        high, low = halves(dot(weight[...], nodes[...], 0, 1))
-        parts[:width] = high
-        parts[width:] = low
+    high, low = halves(dot(w_left[...], row_nodes[...], 0, 1))
+    u_parts[:width] = high
+    u_parts[width:] = low
+    v_parts[...] = jnp.concatenate(halves(dot(w_right[...], column_nodes[...], 0, 1)), axis=1)
     harm_t[...] = w_harm[...].astype(F32).T.astype(BF16)
     out_t[...] = w_out[...].astype(F32).T.astype(BF16)
     for total in (sum_u, sum_v, weights):
@@ -72,8 +72,7 @@
         pick_v = at_v.astype(F32).astype(BF16)
         parts = dot(u_parts[...], pick_u, 1, 0)
         u = parts[:width] + parts[width:]
-        parts = dot(v_parts[...], pick_v, 1, 0)
-        v = parts[:width] + parts[width:]
+        v = dot(v_parts[...], jnp.concatenate([pick_v, pick_v]), 1, 0)
         e = dot(harm_t[...], h, 1, 0)
         gz = dot(out_t[...], g, 1, 0)
         uv = u * v
@@ -112,7 +111,7 @@
         out_specs=(VMEM,) * 3,
         scratch_shapes=[
             pltpu.VMEM((2 * width, atoms), BF16),
-            pltpu.VMEM((2 * width, near), BF16),
+            pltpu.VMEM((width, 2 * near), BF16),
             pltpu.VMEM(w_harm.shape[::-1], BF16),
             pltpu.VMEM(w_out.shape[::-1], BF16),
             pltpu.VMEM((atoms, width), F32),
@@ -134,53 +133,35 @@
     return dot(high, weight[...], 1, 1) + dot(low, weight[...], 1, 1)
 
 
-def when(condition, block):
-    return jnp.where(condition, block, jnp.zeros_like(block))
-
-
-def across_x_kernel(places, parts, sum_v, w_left, row_part, out):
-    x, z = places[0], places[1]
-    shard = sum_v.shape[0] // 3
-    last = places[2] - 1
+def row_kernel(parts, sum_v, upper, w_left, w_right, nodes_part, out):
+    shard = nodes_part.shape[0]
     total = total_of(parts)
-    row_part[...] = weighted(total[:shard], w_left)
-    upper = when(z == 0, sum_v[:shard])
-    lower = when(z == last, sum_v[2 * shard :])
+    columns = sum_v[shard : 2 * shard] + upper[...]
+    nodes_part[...] = weighted(total[:shard], w_left) + weighted(columns, w_right)
     for to in range(out.shape[0]):
-        out[to, :shard] = when(x - 1 == to, upper) + when(x + 1 == to, lower)
-        out[to, shard:] = total[shard:]
-
-
-def across_z_kernel(places, parts, sum_v, out):
-    z = places[1]
-    shard = sum_v.shape[0] // 3
-    last = places[2] - 1
+        out[to] = total[shard:]
+
+
+def sum_kernel(parts, sum_v, out, lower):
+    shard = lower.shape[0]
     total = total_of(parts)
-    upper, lower = sum_v[:shard], sum_v[2 * shard :]
-    crossed = total[:shard]
     for to in range(out.shape[0]):
-        ends = jnp.logical_or(
-            jnp.logical_and(z == 0, to == last), jnp.logical_and(z == last, to == 0)
-        )
-        out[to, :shard] = when(z - 1 == to, upper) + when(z + 1 == to, lower) + when(ends, crossed)
-        out[to, shard:] = total[shard:]
-
-
-def node_kernel(parts, sum_v, row_part, w_right, grad_nodes, shares):
-    shard = sum_v.shape[0] // 3
-    total = total_of(parts)
-    columns = sum_v[shard : 2 * shard] + total[:shard]
-    grad_nodes[...] = row_part[...] + weighted(columns, w_right)
+        out[to] = total
+    lower[...] = sum_v[2 * shard :]
+
+
+def node_kernel(parts, lower, nodes_part, w_right, grad_nodes, shares):
+    grad_nodes[...] = nodes_part[...] + weighted(lower[...], w_right)
+    total = total_of(parts).astype(shares.dtype)
     for chip in range(shares.shape[0]):
-        shares[chip] = total[shard:].astype(shares.dtype)
-
-
-def call(kernel, out_shape, *operands, scalars=1):
-    specs = [SMEM] * scalars + [VMEM] * (len(operands) - scalars)
+        shares[chip] = total
+
+
+def call(kernel, out_shape, *operands):
     return pl.pallas_call(
         kernel,
         out_shape=out_shape,
-        in_specs=specs,
+        in_specs=[VMEM] * len(operands),
         out_specs=jax.tree.map(lambda _: VMEM, out_shape),
         compiler_params=PARAMS,
     )(*operands)
@@ -272,19 +253,20 @@
         row_nodes, column_nodes, (w_left, w_right, w_harm, w_out), chips, share,
     )
     parts = (keep + swapped(send)).astype(BF16)
+    upper = shifted(sum_v[:shard], -1)
     parts = exchange(parts, "col", CHIP_BITS)
-    at = jnp.stack([row // spread, row % spread, jnp.int32(spread)]).astype(jnp.int32)
-    chunks = like(spread, shard + share, width)
-    row_part, parts = call(
-        across_x_kernel, (like(shard, width), chunks), at, parts, sum_v, w_left
+    block, chunks = like(shard, width), like(spread, share, width)
+    nodes_part, parts = call(
+        row_kernel, (block, chunks), parts, sum_v, upper, w_left, w_right
     )
     parts = exchange(parts, "row", X_BITS)
-    parts = call(across_z_kernel, chunks, at, parts, sum_v)
+    parts, lower = call(sum_kernel, (chunks, block), parts, sum_v)
+    lower = shifted(lower, 1)
     parts = exchange(parts, "row", Z_BITS)
     grad_nodes, shares = call(
         node_kernel,
-        (like(shard, width), jax.ShapeDtypeStruct((chips, share, width), BF16)),
-        parts, sum_v, row_part, w_right, scalars=0,
+        (block, jax.ShapeDtypeStruct((chips, share, width), BF16)),
+        parts, lower, nodes_part, w_right,
     )
     own_shares = exchange(shares, "col", CHIP_BITS)
     left, right, harm, out = split(

time: 123 us -> 123 us (level)
  blocking collectives: 44.6 us -> 23.1 us
  starting transfers between devices: 36.9 us -> 58 us
  waiting for transfers between devices: 23.9 us -> 28.4 us
  Pallas kernels: 11.9 us -> 7.86 us
    all_to_all x3 -> x2, blocking collectives: 44.6 us -> 23.1 us  [exchange(): lax.all_to_all(blocks, axis, 0, 0, tiled=True, axis_index_groups=groups(l...]
    all_to_all x2 -> x3, starting transfers between devices: 18.8 us -> 28.2 us  [exchange(): lax.all_to_all(blocks, axis, 0, 0, tiled=True, axis_index_groups=groups(l...]
    ppermute x2 -> x4, waiting for transfers between devices: 6.04 us -> 14.8 us  [shifted(): lax.ppermute(block, 'row', [(i, i + distance) for i in devices if i + dis...]
    ppermute x2 -> x4, starting transfers between devices: 9.88 us -> 18.4 us  [shifted(): lax.ppermute(block, 'row', [(i, i + distance) for i in devices if i + dis...]
    all_to_all x2 -> x3, waiting for transfers between devices: 14.4 us -> 10.5 us  [exchange(): lax.all_to_all(blocks, axis, 0, 0, tiled=True, axis_index_groups=groups(l...]
    pallas_call x1, Pallas kernels: 8.87 us -> 5.22 us  [pair_sums(): pl.pallas_call(pair_kernel, out_shape=(like(chips, chunk, width), like(ch...]
    ppermute x2, starting transfers between devices: 8.24 us -> 11.4 us  [swapped(): lax.ppermute(block, 'col', [(i, i ^ 1) for i in range(lax.axis_size('col'...]
  transfers between devices with their start and end apart: 6 -> 9, of which waited for: 4 -> 7; matrix products, arithmetic and copies ran while one was open for 0% -> 0% of each run, Pallas kernels for 0% -> 0%
where the time goes in v3:
time: 123 us; the launch traced here: 122 us
  starting transfers between devices  58 us (47%)
  waiting for transfers between devices  28.4 us (23%)
  blocking collectives  23.1 us (19%)
  Pallas kernels  7.86 us (6%)
  local copies, waits for them, and re-layouts  2.49 us (2%)
  between operations  1.52 us (1%)
    all_to_all x3, starting transfers between devices, exchange(): lax.all_to_all(blocks, axis, 0, 0, tiled=True, axis_index_groups=groups(l...  28.2 us
    all_to_all x2, blocking collectives, exchange(): lax.all_to_all(blocks, axis, 0, 0, tiled=True, axis_index_groups=groups(l...  23.1 us
    ppermute x4, starting transfers between devices, shifted(): lax.ppermute(block, 'row', [(i, i + distance) for i in devices if i + dis...  18.4 us
    ppermute x4, waiting for transfers between devices, shifted(): lax.ppermute(block, 'row', [(i, i + distance) for i in devices if i + dis...  14.8 us
    ppermute x2, starting transfers between devices, swapped(): lax.ppermute(block, 'col', [(i, i ^ 1) for i in range(lax.axis_size('col'...  11.4 us
    all_to_all x3, waiting for transfers between devices, exchange(): lax.all_to_all(blocks, axis, 0, 0, tiled=True, axis_index_groups=groups(l...  10.5 us
    pallas_call x1, Pallas kernels, pair_sums(): pl.pallas_call(pair_kernel, out_shape=(like(chips, chunk, width), like(ch...  5.22 us
    ppermute x2, waiting for transfers between devices, swapped(): lax.ppermute(block, 'col', [(i, i ^ 1) for i in range(lax.axis_size('col'...  3.13 us
  transfers between devices with their start and end apart: 9, of which 7 were waited for; matrix products, arithmetic and copies ran while one was open for 0% of the time, Pallas kernels for 0%

profile of v3, /device:TPU:1, one launch (start us, length us, event | category | flops | bytes accessed | tf_op | source)
XLA Modules:
  0.0 122.3 jit_solution(8932571041717578748)
XLA Ops:
  0.6 1.6 %broadcast_in_dim.2 = bf16[32,32,256]{2,1,0:T(8,128)(2,1)} broadcast(bf16[32,256]{1,0:T(8,128)(2,1)} %param.11), dimensions={1,2} | broadcast | bytes 540672 | tf_op jit(solution)/shard_map/broadcast_in_dim | solution.py:225
  2.2 10.5 %all-to-all-start = ((bf16[32,32,256]{2,1,0:T(8,128)(2,1)}), bf16[32,32,256]{2,1,0:T(8,128)(2,1)S(1)}, u32[]{:S(2)}, u32[]{:S(2)}) async-start(bf16[32,32,256]{2,1,0:T(8,128)(2,1)} %broadcast_in_dim.2), calls=%async_computation | async-start | bytes 1048576 | tf_op jit(solution)/shard_map/all_to_all | solution.py:208
  12.8 8.6 %collective-permute-start = (bf16[32,256]{1,0:T(8,128)(2,1)S(1)}, bf16[32,256]{1,0:T(8,128)(2,1)S(1)}, u32[]{:S(2)}, u32[]{:S(2)}) collective-permute-start(bf16[32,256]{1,0:T(8,128)(2,1)S(1)} %copy-done.9), channel_id=1, source_target_pairs={{0,32},{32,64},{64,96},{96,128},{128,160},{160,192},{192,224},{224... | collective-permute-start | bytes 49160 | tf_op jit(solution)/shard_map/ppermute | solution.py:219
  21.4 1.3 %collective-permute-start.1 = (bf16[32,256]{1,0:T(8,128)(2,1)S(1)}, bf16[32,256]{1,0:T(8,128)(2,1)S(1)}, u32[]{:S(2)}, u32[]{:S(2)}) collective-permute-start(bf16[32,256]{1,0:T(8,128)(2,1)S(1)} %copy-done.9), channel_id=1, source_target_pairs={{32,0},{64,32},{96,64},{128,96},{160,128},{192,160},{224,192},{256... | collective-permute-start | bytes 49160 | tf_op jit(solution)/shard_map/ppermute | solution.py:219
  23.7 6.0 %collective-permute-done.1 = bf16[32,256]{1,0:T(8,128)(2,1)S(1)} collective-permute-done((bf16[32,256]{1,0:T(8,128)(2,1)S(1)}, bf16[32,256]{1,0:T(8,128)(2,1)S(1)}, u32[]{:S(2)}, u32[]{:S(2)}) %collective-permute-start.1) | collective-permute-done | bytes 16416 | tf_op jit(solution)/shard_map/ppermute | solution.py:219
  30.5 5.2 %shard_map.146 = (f32[16,56,256]{2,1,0:T(8,128)S(1)}, f32[16,56,256]{2,1,0:T(8,128)S(1)}, f32[96,256]{1,0:T(8,128)S(1)}) custom-call(s32[3]{0:T(128)S(1)} %pad_add_fusion.places, s32[16,128]{1,0:T(8,128)S(1)} %bitcast.17, s32[16,128]{1,0:T(8,128)S(1)} %bitcast.18, s32[16,128]{1,0:T(8,128)S(1)} %bitcast.19, bf16[16,25,128]{2,1,0:T(8,128)(2,1)S(1)} %bitcast.16, ...), custom_call_target="tpu_custom_call" | custom-call | tf_op jit(solution)/shard_map/pallas_call | solution.py:107
  35.7 3.6 %collective-permute-start.2 = (f32[16,56,256]{2,1,0:T(8,128)S(1)}, f32[16,56,256]{2,1,0:T(8,128)S(1)}, u32[]{:S(2)}, u32[]{:S(2)}) collective-permute-start(f32[16,56,256]{2,1,0:T(8,128)S(1)} %get-tuple-element.19), channel_id=1, source_target_pairs={{0,1},{1,0},{2,3},{3,2},{4,5},{5,4},{6,7},{7,6},{8,9},{9,8},{10,11... | collective-permute-start | bytes 2752520 | tf_op jit(solution)/shard_map/ppermute | solution.py:214
  39.3 2.1 %collective-permute-done.2 = f32[16,56,256]{2,1,0:T(8,128)S(1)} collective-permute-done((f32[16,56,256]{2,1,0:T(8,128)S(1)}, f32[16,56,256]{2,1,0:T(8,128)S(1)}, u32[]{:S(2)}, u32[]{:S(2)}) %collective-permute-start.2) | collective-permute-done | bytes 917536 | tf_op jit(solution)/shard_map/ppermute | solution.py:214
  41.4 0.9 add_convert_fusion
  42.2 10.4 %all-to-all-start.1 = ((bf16[16,56,256]{2,1,0:T(8,128)(2,1)}), bf16[16,56,256]{2,1,0:T(8,128)(2,1)S(1)}, u32[]{:S(2)}, u32[]{:S(2)}) async-start(bf16[16,56,256]{2,1,0:T(8,128)(2,1)} %add_convert_fusion), calls=%async_computation.1 | async-start | bytes 917504 | tf_op jit(solution)/shard_map/all_to_all | solution.py:208
  52.7 1.3 %collective-permute-start.3 = (f32[32,256]{1,0:T(8,128)S(1)}, f32[32,256]{1,0:T(8,128)S(1)}, u32[]{:S(2)}, u32[]{:S(2)}) collective-permute-start(f32[32,256]{1,0:T(8,128)S(1)} %slice.3), channel_id=1, source_target_pairs={{32,0},{64,32},{96,64},{128,96},{160,128},{192,160},{224,192},{256... | collective-permute-start | bytes 98312 | tf_op jit(solution)/shard_map/ppermute | solution.py:219
  54.0 7.7 %collective-permute-done.3.upper = f32[32,256]{1,0:T(8,128)S(1)} collective-permute-done((f32[32,256]{1,0:T(8,128)S(1)}, f32[32,256]{1,0:T(8,128)S(1)}, u32[]{:S(2)}, u32[]{:S(2)}) %collective-permute-start.3) | collective-permute-done | bytes 32800 | tf_op jit(solution)/shard_map/ppermute | solution.py:219
  61.7 6.8 %all-to-all-done.1.parts = bf16[16,56,256]{2,1,0:T(8,128)(2,1)S(1)} async-done(((bf16[16,56,256]{2,1,0:T(8,128)(2,1)}), bf16[16,56,256]{2,1,0:T(8,128)(2,1)S(1)}, u32[]{:S(2)}, u32[]{:S(2)}) %all-to-all-start.1) | async-done | bytes 458784 | tf_op jit(solution)/shard_map/all_to_all | solution.py:208
  68.8 10.7 %all_to_all.25.parts = f32[4,24,256]{2,1,0:T(8,128)S(1)} all-to-all(f32[4,24,256]{2,1,0:T(8,128)S(1)} %get-tuple-element.21), channel_id=1, replica_groups={{0,128,256,384},{32,160,288,416},{64,192,320,448},{96,224,352,480},{1,1..., dimensions={0} | all-to-all | bytes 196608 | tf_op jit(solution)/shard_map/all_to_all | solution.py:208
  79.5 0.7 shard_map.148
  80.1 7.2 %all-to-all-start.3 = ((f32[4,24,256]{2,1,0:T(8,128)}), f32[4,24,256]{2,1,0:T(8,128)S(1)}, u32[]{:S(2)}, u32[]{:S(2)}) async-start(f32[4,24,256]{2,1,0:T(8,128)} %get-tuple-element.22), calls=%async_computation.3 | async-start | bytes 196608 | tf_op jit(solution)/shard_map/all_to_all | solution.py:208
  87.4 7.3 %collective-permute-start.4 = (f32[32,256]{1,0:T(8,128)S(1)}, f32[32,256]{1,0:T(8,128)S(1)}, u32[]{:S(2)}, u32[]{:S(2)}) collective-permute-start(f32[32,256]{1,0:T(8,128)S(1)} %get-tuple-element.23), channel_id=1, source_target_pairs={{0,32},{32,64},{64,96},{96,128},{128,160},{160,192},{192,224},{224... | collective-permute-start | bytes 98312 | tf_op jit(solution)/shard_map/ppermute | solution.py:219
  94.6 1.0 collective-permute-done.4.lower
  95.6 3.7 %all-to-all-done.3.parts = f32[4,24,256]{2,1,0:T(8,128)S(1)} async-done(((f32[4,24,256]{2,1,0:T(8,128)}), f32[4,24,256]{2,1,0:T(8,128)S(1)}, u32[]{:S(2)}, u32[]{:S(2)}) %all-to-all-start.3) | async-done | bytes 98336 | tf_op jit(solution)/shard_map/all_to_all | solution.py:208
  99.3 0.8 shard_map.149
  100.1 12.4 %all_to_all.26.own = bf16[16,24,256]{2,1,0:T(8,128)(2,1)S(1)} all-to-all(bf16[16,24,256]{2,1,0:T(8,128)(2,1)S(1)} %get-tuple-element.26), channel_id=1, replica_groups={{0,2,4,6,8,10,12,14,16,18,20,22,24,26,28,30},{1,3,5,7,9,11,13,15,17,19,..., dimensions={0} | all-to-all | bytes 393216 | tf_op jit(solution)/shard_map/all_to_all | solution.py:208
  112.5 7.8 %collective-permute-start.5 = (bf16[16,24,256]{2,1,0:T(8,128)(2,1)S(1)}, bf16[16,24,256]{2,1,0:T(8,128)(2,1)S(1)}, u32[]{:S(2)}, u32[]{:S(2)}) collective-permute-start(bf16[16,24,256]{2,1,0:T(8,128)(2,1)S(1)} %all_to_all.26.own), channel_id=1, source_target_pairs={{0,1},{1,0},{2,3},{3,2},{4,5},{5,4},{6,7},{7,6},{8,9},{9,8},{10,11... | collective-permute-start | bytes 589832 | tf_op jit(solution)/shard_map/ppermute | solution.py:214
  120.3 1.0 collective-permute-done.5.other
  121.3 0.9 shard_map.150
  (28 shorter events, 1.3 us)
Async XLA Ops:
  2.2 10.6 %copy-start.9 = (bf16[32,256]{1,0:T(8,128)(2,1)S(1)}, bf16[32,256]{1,0:T(8,128)(2,1)}, u32[]{:S(2)}) copy-start(bf16[32,256]{1,0:T(8,128)(2,1)} %param.11) | copy-start | bytes 49156
  2.2 21.2 %copy-start.8 = (bf16[1,16,25,128]{3,1,2,0:T(8,128)(2,1)S(1)}, bf16[1,16,25,128]{3,1,2,0:T(8,128)(2,1)}, u32[]{:S(2)}) copy-start(bf16[1,16,25,128]{3,1,2,0:T(8,128)(2,1)} %param.12) | copy-start | bytes 307204
  2.2 21.2 %copy-start.7 = (bf16[1,16,169,128]{3,1,2,0:T(8,128)(2,1)S(1)}, bf16[1,16,169,128]{3,1,2,0:T(8,128)(2,1)}, u32[]{:S(2)}) copy-start(bf16[1,16,169,128]{3,1,2,0:T(8,128)(2,1)} %param.13) | copy-start | bytes 2076676
  2.2 27.6 %all-to-all-start = ((bf16[32,32,256]{2,1,0:T(8,128)(2,1)}), bf16[32,32,256]{2,1,0:T(8,128)(2,1)S(1)}, u32[]{:S(2)}, u32[]{:S(2)}) async-start(bf16[32,32,256]{2,1,0:T(8,128)(2,1)} %broadcast_in_dim.2), calls=%async_computation | async-start | bytes 1048576 | tf_op jit(solution)/shard_map/all_to_all | solution.py:208
  12.8 10.9 %collective-permute-start = (bf16[32,256]{1,0:T(8,128)(2,1)S(1)}, bf16[32,256]{1,0:T(8,128)(2,1)S(1)}, u32[]{:S(2)}, u32[]{:S(2)}) collective-permute-start(bf16[32,256]{1,0:T(8,128)(2,1)S(1)} %copy-done.9), channel_id=1, source_target_pairs={{0,32},{32,64},{64,96},{96,128},{128,160},{160,192},{192,224},{224... | collective-permute-start | bytes 49160 | tf_op jit(solution)/shard_map/ppermute | solution.py:219
  21.4 8.4 %collective-permute-start.1 = (bf16[32,256]{1,0:T(8,128)(2,1)S(1)}, bf16[32,256]{1,0:T(8,128)(2,1)S(1)}, u32[]{:S(2)}, u32[]{:S(2)}) collective-permute-start(bf16[32,256]{1,0:T(8,128)(2,1)S(1)} %copy-done.9), channel_id=1, source_target_pairs={{32,0},{64,32},{96,64},{128,96},{160,128},{192,160},{224,192},{256... | collective-permute-start | bytes 49160 | tf_op jit(solution)/shard_map/ppermute | solution.py:219
  23.5 6.3 %copy-start = (bf16[256,256]{1,0:T(8,128)(2,1)S(1)}, bf16[256,256]{1,0:T(8,128)(2,1)}, u32[]{:S(2)}) copy-start(bf16[256,256]{1,0:T(8,128)(2,1)} %w_right.5) | copy-start | bytes 393220
  23.5 6.3 %copy-start.1 = (bf16[256,256]{1,0:T(8,128)(2,1)S(1)}, bf16[256,256]{1,0:T(8,128)(2,1)}, u32[]{:S(2)}) copy-start(bf16[256,256]{1,0:T(8,128)(2,1)} %w_left.3) | copy-start | bytes 393220
  23.5 6.3 %copy-start.4 = (s32[1,16,128]{2,1,0:T(8,128)S(1)}, s32[1,16,128]{2,1,0:T(8,128)}, u32[]{:S(2)}) copy-start(s32[1,16,128]{2,1,0:T(8,128)} %param.14) | copy-start | bytes 24580
  23.5 6.3 %copy-start.5 = (s32[1,16,128]{2,1,0:T(8,128)S(1)}, s32[1,16,128]{2,1,0:T(8,128)}, u32[]{:S(2)}) copy-start(s32[1,16,128]{2,1,0:T(8,128)} %param.15) | copy-start | bytes 24580
  23.5 6.3 %copy-start.6 = (s32[1,16,128]{2,1,0:T(8,128)S(1)}, s32[1,16,128]{2,1,0:T(8,128)}, u32[]{:S(2)}) copy-start(s32[1,16,128]{2,1,0:T(8,128)} %param.16) | copy-start | bytes 24580
  23.7 6.1 %copy-start.2 = (bf16[169,256]{1,0:T(8,128)(2,1)S(1)}, bf16[169,256]{1,0:T(8,128)(2,1)}, u32[]{:S(2)}) copy-start(bf16[169,256]{1,0:T(8,128)(2,1)} %w_out.1) | copy-start | bytes 259588
  29.8 0.7 copy-start.3
  35.7 5.7 %collective-permute-start.2 = (f32[16,56,256]{2,1,0:T(8,128)S(1)}, f32[16,56,256]{2,1,0:T(8,128)S(1)}, u32[]{:S(2)}, u32[]{:S(2)}) collective-permute-start(f32[16,56,256]{2,1,0:T(8,128)S(1)} %get-tuple-element.19), channel_id=1, source_target_pairs={{0,1},{1,0},{2,3},{3,2},{4,5},{5,4},{6,7},{7,6},{8,9},{9,8},{10,11... | collective-permute-start | bytes 2752520 | tf_op jit(solution)/shard_map/ppermute | solution.py:214
  42.2 26.3 %all-to-all-start.1 = ((bf16[16,56,256]{2,1,0:T(8,128)(2,1)}), bf16[16,56,256]{2,1,0:T(8,128)(2,1)S(1)}, u32[]{:S(2)}, u32[]{:S(2)}) async-start(bf16[16,56,256]{2,1,0:T(8,128)(2,1)} %add_convert_fusion), calls=%async_computation.1 | async-start | bytes 917504 | tf_op jit(solution)/shard_map/all_to_all | solution.py:208
  52.7 9.0 %collective-permute-start.3 = (f32[32,256]{1,0:T(8,128)S(1)}, f32[32,256]{1,0:T(8,128)S(1)}, u32[]{:S(2)}, u32[]{:S(2)}) collective-permute-start(f32[32,256]{1,0:T(8,128)S(1)} %slice.3), channel_id=1, source_target_pairs={{32,0},{64,32},{96,64},{128,96},{160,128},{192,160},{224,192},{256... | collective-permute-start | bytes 98312 | tf_op jit(solution)/shard_map/ppermute | solution.py:219
  80.1 19.2 %all-to-all-start.3 = ((f32[4,24,256]{2,1,0:T(8,128)}), f32[4,24,256]{2,1,0:T(8,128)S(1)}, u32[]{:S(2)}, u32[]{:S(2)}) async-start(f32[4,24,256]{2,1,0:T(8,128)} %get-tuple-element.22), calls=%async_computation.3 | async-start | bytes 196608 | tf_op jit(solution)/shard_map/all_to_all | solution.py:208
  87.4 8.3 %collective-permute-start.4 = (f32[32,256]{1,0:T(8,128)S(1)}, f32[32,256]{1,0:T(8,128)S(1)}, u32[]{:S(2)}, u32[]{:S(2)}) collective-permute-start(f32[32,256]{1,0:T(8,128)S(1)} %get-tuple-element.23), channel_id=1, source_target_pairs={{0,32},{32,64},{64,96},{96,128},{128,160},{160,192},{192,224},{224... | collective-permute-start | bytes 98312 | tf_op jit(solution)/shard_map/ppermute | solution.py:219
  112.5 8.9 %collective-permute-start.5 = (bf16[16,24,256]{2,1,0:T(8,128)(2,1)S(1)}, bf16[16,24,256]{2,1,0:T(8,128)(2,1)S(1)}, u32[]{:S(2)}, u32[]{:S(2)}) collective-permute-start(bf16[16,24,256]{2,1,0:T(8,128)(2,1)S(1)} %all_to_all.26.own), channel_id=1, source_target_pairs={{0,1},{1,0},{2,3},{3,2},{4,5},{5,4},{6,7},{7,6},{8,9},{9,8},{10,11... | collective-permute-start | bytes 589832 | tf_op jit(solution)/shard_map/ppermute | solution.py:214

commit v4 on v3

--- a/solution.py
+++ b/solution.py
@@ -12,7 +12,7 @@
 BOTH = ("row", "col")
 BLOCKS_PER_STEP = 8
 OUT_ROWS = 176
-X_BITS, Z_BITS, CHIP_BITS, COL_BITS = (4, 8), (1, 2), (2, 4, 8, 16), (1, 2, 4, 8, 16)
+X_BITS, Z_BITS, CHIP_BITS = (4, 8), (1, 2), (2, 4, 8, 16)
 
 
 def like(*shape):
@@ -29,19 +29,20 @@
 
 
 def pair_kernel(
-    places, rows, cols, mask, harm, grads, row_nodes, column_nodes, w_left, w_right, w_harm, w_out,
-    keep, send, sum_v, u_parts, v_parts, harm_t, out_t, sum_u, weights,
+    places, rows, cols, mask, harm, grads, own, other, column_nodes, v_parts, w_left, w_harm, w_out,
+    keep, send, middle, ahead, passed, u_parts, harm_t, out_t, sum_u, sum_v, weights,
 ):
     count, column_base, core = places[0], places[1], places[2]
     width = w_left.shape[0]
-    atoms, near = row_nodes.shape[0], column_nodes.shape[0]
+    half, near = own.shape[0], column_nodes.shape[0]
+    atoms = 2 * half
     shard = near // 3
     pairs = BLOCKS_PER_STEP * mask.shape[1]
     orbitals, harmonics = w_out.shape[0], w_harm.shape[0]
-    high, low = halves(dot(w_left[...], row_nodes[...], 0, 1))
-    u_parts[:width] = high
-    u_parts[width:] = low
-    v_parts[...] = jnp.concatenate(halves(dot(w_right[...], column_nodes[...], 0, 1)), axis=1)
+    for first, nodes in ((0, own), (half, other)):
+        high, low = halves(dot(w_left[...], nodes[...], 0, 1))
+        u_parts[:width, first : first + half] = high
+        u_parts[width:, first : first + half] = low
     harm_t[...] = w_harm[...].astype(F32).T.astype(BF16)
     out_t[...] = w_out[...].astype(F32).T.astype(BF16)
     for total in (sum_u, sum_v, weights):
@@ -66,7 +67,11 @@
         g = jnp.concatenate([grads[first + k] for k in range(BLOCKS_PER_STEP)], axis=1)
         g = g * live.astype(F32).astype(BF16)
         h = jnp.concatenate([harm[first + k] for k in range(BLOCKS_PER_STEP)], axis=1)
-        at_u = lax.broadcasted_iota(jnp.int32, (atoms, pairs), 0) == line(rows, first)
+        atom = line(rows, first)
+        owner = lax.div(atom, shard)
+        place = lax.shift_right_logical(owner, 1) * shard + lax.rem(atom, shard)
+        place = place + jnp.where(jnp.bitwise_and(owner, 1) == core, 0, half)
+        at_u = lax.broadcasted_iota(jnp.int32, (atoms, pairs), 0) == place
         at_v = lax.broadcasted_iota(jnp.int32, (near, pairs), 0) == line(cols, first) - column_base
         pick_u = at_u.astype(F32).astype(BF16)
         pick_v = at_v.astype(F32).astype(BF16)
@@ -86,39 +91,53 @@
         return carry
 
     lax.fori_loop(0, lax.div(count + BLOCKS_PER_STEP - 1, BLOCKS_PER_STEP), step, 0)
-    for at, nodes, sums in ((0, row_nodes, sum_u), (width, column_nodes, sum_v)):
-        high, low = halves(sums[...])
-        weights[at : at + width] = dot(nodes[...], high, 0, 0) + dot(nodes[...], low, 0, 0)
+    for at, blocks in (
+        (0, ((own, sum_u[:half]), (other, sum_u[half:]))),
+        (width, ((column_nodes, sum_v[...]),)),
+    ):
+        total = jnp.zeros((width, width), F32)
+        for nodes, sums in blocks:
+            for part in halves(sums):
+                total = total + dot(nodes[...], part, 0, 0)
+        weights[at : at + width] = total
     chips, chunk = keep.shape[0], keep.shape[1]
     share = chunk - shard
     for chip in range(chips):
-        for to, which in ((keep, core), (send, 1 - core)):
-            start = pl.multiple_of((2 * chip + which) * shard, 8)
-            to[chip, :shard] = sum_u[pl.ds(start, shard), :]
+        for to, first, which in ((keep, 0, core), (send, half, 1 - core)):
+            to[chip, :shard] = sum_u[first + chip * shard : first + (chip + 1) * shard]
             start = pl.multiple_of((which * chips + chip) * share, 8)
             to[chip, shard:] = weights[pl.ds(start, share), :]
-
-
-def pair_sums(places, rows, cols, mask, harm, grads, row_nodes, column_nodes, weights_in, chips, share):
-    atoms, width = row_nodes.shape
+    middle[...] = sum_v[shard : 2 * shard]
+    ahead[...] = sum_v[pl.ds(pl.multiple_of(core * 2 * shard, 8), shard), :]
+    passed[...] = sum_v[pl.ds(pl.multiple_of((1 - core) * 2 * shard, 8), shard), :]
+
+
+def project_kernel(own, column_nodes, w_right, copy, v_parts):
+    copy[...] = own[...]
+    v_parts[...] = jnp.concatenate(halves(dot(w_right[...], column_nodes[...], 0, 1)), axis=1)
+
+
+def pair_sums(places, rows, cols, mask, harm, grads, own, other, column_nodes, v_parts, weights_in, chips, share):
+    half, width = own.shape
     near = column_nodes.shape[0]
-    chunk = near // 3 + share
-    w_harm, w_out = weights_in[2:]
+    shard = near // 3
+    chunks, block = like(chips, shard + share, width), like(shard, width)
+    w_harm, w_out = weights_in[1:]
     return pl.pallas_call(
         pair_kernel,
-        out_shape=(like(chips, chunk, width), like(chips, chunk, width), like(near, width)),
-        in_specs=[SMEM] + [VMEM] * 11,
-        out_specs=(VMEM,) * 3,
+        out_shape=(chunks, chunks, block, block, block),
+        in_specs=[SMEM] + [VMEM] * 12,
+        out_specs=(VMEM,) * 5,
         scratch_shapes=[
-            pltpu.VMEM((2 * width, atoms), BF16),
-            pltpu.VMEM((width, 2 * near), BF16),
+            pltpu.VMEM((2 * width, 2 * half), BF16),
             pltpu.VMEM(w_harm.shape[::-1], BF16),
             pltpu.VMEM(w_out.shape[::-1], BF16),
-            pltpu.VMEM((atoms, width), F32),
+            pltpu.VMEM((2 * half, width), F32),
+            pltpu.VMEM((near, width), F32),
             pltpu.VMEM((2 * chips * share, width), F32),
         ],
         compiler_params=PARAMS,
-    )(places, rows, cols, mask, harm, grads, row_nodes, column_nodes, *weights_in)
+    )(places, rows, cols, mask, harm, grads, own, other, column_nodes, v_parts, *weights_in)
 
 
 def total_of(parts):
@@ -133,25 +152,23 @@
     return dot(high, weight[...], 1, 1) + dot(low, weight[...], 1, 1)
 
 
-def row_kernel(parts, sum_v, upper, w_left, w_right, nodes_part, out):
-    shard = nodes_part.shape[0]
+def row_kernel(parts, w_left, row_part, out):
+    shard = row_part.shape[0]
     total = total_of(parts)
-    columns = sum_v[shard : 2 * shard] + upper[...]
-    nodes_part[...] = weighted(total[:shard], w_left) + weighted(columns, w_right)
+    row_part[...] = weighted(total[:shard], w_left)
     for to in range(out.shape[0]):
         out[to] = total[shard:]
 
 
-def sum_kernel(parts, sum_v, out, lower):
-    shard = lower.shape[0]
+def sum_kernel(parts, out):
     total = total_of(parts)
     for to in range(out.shape[0]):
         out[to] = total
-    lower[...] = sum_v[2 * shard :]
-
-
-def node_kernel(parts, lower, nodes_part, w_right, grad_nodes, shares):
-    grad_nodes[...] = nodes_part[...] + weighted(lower[...], w_right)
+
+
+def node_kernel(parts, middle, here, there, row_part, w_right, grad_nodes, shares):
+    columns = middle[...] + here[...] + there[...]
+    grad_nodes[...] = row_part[...] + weighted(columns, w_right)
     total = total_of(parts).astype(shares.dtype)
     for chip in range(shares.shape[0]):
         shares[chip] = total
@@ -219,6 +236,17 @@
     return lax.ppermute(
         block, "row", [(i, i + distance) for i in devices if i + distance in devices]
     )
+
+
+def neighbours(block):
+    rows, columns = lax.axis_size("row"), lax.axis_size("col")
+    route = []
+    for row in range(rows):
+        for column in range(columns):
+            to = row + 2 * (column % 2) - 1
+            if to in range(rows):
+                route.append((row * columns + column, to * columns + column))
+    return lax.ppermute(block, BOTH, route)
 
 
 def repeated(block, copies):
@@ -246,27 +274,40 @@
     row = lax.axis_index("row")
     core = jnp.bitwise_and(lax.axis_index("col"), 1)
     column_nodes = jnp.concatenate([shifted(nodes, 1), nodes, shifted(nodes, -1)])
-    row_nodes = exchange(repeated(nodes, columns), "col", COL_BITS).reshape(-1, width)
+    own = exchange(repeated(nodes, chips), "col", CHIP_BITS).reshape(-1, width)
+    own, v_parts = call(
+        project_kernel,
+        (
+            jax.ShapeDtypeStruct(own.shape, BF16),
+            jax.ShapeDtypeStruct((width, 2 * column_nodes.shape[0]), BF16),
+        ),
+        own, column_nodes, w_right,
+    )
+    other = swapped(own)
     places = jnp.stack([block_counts[0, 0], (row - 1) * shard, core]).astype(jnp.int32)
-    keep, send, sum_v = pair_sums(
+    keep, send, middle, ahead, passed = pair_sums(
         places, pair_rows[0], pair_cols[0], pair_mask[0], harmonics[0], grad_blocks[0],
-        row_nodes, column_nodes, (w_left, w_right, w_harm, w_out), chips, share,
+        own, other, column_nodes, v_parts, (w_left, w_harm, w_out), chips, share,
     )
     parts = (keep + swapped(send)).astype(BF16)
-    upper = shifted(sum_v[:shard], -1)
     parts = exchange(parts, "col", CHIP_BITS)
-    block, chunks = like(shard, width), like(spread, share, width)
-    nodes_part, parts = call(
-        row_kernel, (block, chunks), parts, sum_v, upper, w_left, w_right
+    passed = swapped(passed)
+    both = jnp.where(
+        core == 0, jnp.concatenate([ahead, passed]), jnp.concatenate([passed, ahead])
+    )
+    both = neighbours(both)
+    here = jnp.where(core == 0, both[:shard], both[shard:])
+    there = swapped(jnp.where(core == 0, both[shard:], both[:shard]))
+    row_part, parts = call(
+        row_kernel, (like(shard, width), like(spread, share, width)), parts, w_left
     )
     parts = exchange(parts, "row", X_BITS)
-    parts, lower = call(sum_kernel, (chunks, block), parts, sum_v)
-    lower = shifted(lower, 1)
+    parts = call(sum_kernel, like(spread, share, width), parts)
     parts = exchange(parts, "row", Z_BITS)
     grad_nodes, shares = call(
         node_kernel,
-        (block, jax.ShapeDtypeStruct((chips, share, width), BF16)),
-        parts, lower, nodes_part, w_right,
+        (like(shard, width), jax.ShapeDtypeStruct((chips, share, width), BF16)),
+        parts, middle, here, there, row_part, w_right,
     )
     own_shares = exchange(shares, "col", CHIP_BITS)
     left, right, harm, out = split(

time: 123 us -> 123 us (level)
  blocking collectives: 23.1 us -> 11.3 us
  starting transfers between devices: 58 us -> 66.9 us
    all_to_all x2 -> x1, blocking collectives: 23.1 us -> 11.3 us  [exchange(): lax.all_to_all(blocks, axis, 0, 0, tiled=True, axis_index_groups=groups(l...]
    ppermute x2 -> x5, starting transfers between devices: 11.4 us -> 21.2 us  [swapped(): lax.ppermute(block, 'col', [(i, i ^ 1) for i in range(lax.axis_size('col'...]
    ppermute x4 -> x2, starting transfers between devices: 18.4 us -> 10.1 us  [shifted(): lax.ppermute(block, 'row', [(i, i + distance) for i in devices if i + dis...]
    ppermute x4 -> x2, waiting for transfers between devices: 14.8 us -> 7.06 us  [shifted(): lax.ppermute(block, 'row', [(i, i + distance) for i in devices if i + dis...]
    all_to_all x3 -> x4, waiting for transfers between devices: 10.5 us -> 18 us  [exchange(): lax.all_to_all(blocks, axis, 0, 0, tiled=True, axis_index_groups=groups(l...]
    ppermute x0 -> x1, starting transfers between devices: none -> 6.22 us  [neighbours(): return lax.ppermute(block, BOTH, route)]
    all_to_all x3 -> x4, starting transfers between devices: 28.2 us -> 29.4 us  [exchange(): lax.all_to_all(blocks, axis, 0, 0, tiled=True, axis_index_groups=groups(l...]
    ppermute x2 -> x5, waiting for transfers between devices: 3.13 us -> 4.33 us  [swapped(): lax.ppermute(block, 'col', [(i, i ^ 1) for i in range(lax.axis_size('col'...]
  transfers between devices with their start and end apart: 9 -> 12, of which waited for: 7 -> 6; matrix products, arithmetic and copies ran while one was open for 0% -> 0% of each run, Pallas kernels for 0% -> 1%
where the time goes in v4:
time: 123 us; the launch traced here: 122 us
  starting transfers between devices  66.9 us (54%)
  waiting for transfers between devices  29.4 us (24%)
  blocking collectives  11.3 us (9%)
  Pallas kernels  8.55 us (7%)
  local copies, waits for them, and re-layouts  3.26 us (3%)
  between operations  1.54 us (1%)
    all_to_all x4, starting transfers between devices, exchange(): lax.all_to_all(blocks, axis, 0, 0, tiled=True, axis_index_groups=groups(l...  29.4 us
    ppermute x5, starting transfers between devices, swapped(): lax.ppermute(block, 'col', [(i, i ^ 1) for i in range(lax.axis_size('col'...  21.2 us
    all_to_all x4, waiting for transfers between devices, exchange(): lax.all_to_all(blocks, axis, 0, 0, tiled=True, axis_index_groups=groups(l...  18 us
    all_to_all x1, blocking collectives, exchange(): lax.all_to_all(blocks, axis, 0, 0, tiled=True, axis_index_groups=groups(l...  11.3 us
    ppermute x2, starting transfers between devices, shifted(): lax.ppermute(block, 'row', [(i, i + distance) for i in devices if i + dis...  10.1 us
    ppermute x2, waiting for transfers between devices, shifted(): lax.ppermute(block, 'row', [(i, i + distance) for i in devices if i + dis...  7.06 us
    ppermute x1, starting transfers between devices, neighbours(): return lax.ppermute(block, BOTH, route)  6.22 us
    pallas_call x1, Pallas kernels, pair_sums(): pl.pallas_call(pair_kernel, out_shape=(chunks, chunks, block, block, bloc...  5.14 us
  transfers between devices with their start and end apart: 12, of which 6 were waited for; matrix products, arithmetic and copies ran while one was open for 0% of the time, Pallas kernels for 1%

profile of v4, /device:TPU:1, one launch (start us, length us, event | category | flops | bytes accessed | tf_op | source)
XLA Modules:
  0.0 121.9 jit_solution(11390850383490401243)
XLA Ops:
  0.7 1.5 %broadcast_in_dim.2 = bf16[16,32,256]{2,1,0:T(8,128)(2,1)} broadcast(bf16[32,256]{1,0:T(8,128)(2,1)} %param.11), dimensions={1,2} | broadcast | bytes 278528 | tf_op jit(solution)/shard_map/broadcast_in_dim | solution.py:253
  2.2 9.3 %all-to-all-start = ((bf16[16,32,256]{2,1,0:T(8,128)(2,1)}), bf16[16,32,256]{2,1,0:T(8,128)(2,1)S(1)}, u32[]{:S(2)}, u32[]{:S(2)}) async-start(bf16[16,32,256]{2,1,0:T(8,128)(2,1)} %broadcast_in_dim.2), calls=%async_computation | async-start | bytes 524288 | tf_op jit(solution)/shard_map/all_to_all | solution.py:225
  11.5 8.8 %collective-permute-start = (bf16[32,256]{1,0:T(8,128)(2,1)S(1)}, bf16[32,256]{1,0:T(8,128)(2,1)S(1)}, u32[]{:S(2)}, u32[]{:S(2)}) collective-permute-start(bf16[32,256]{1,0:T(8,128)(2,1)S(1)} %copy-done.9), channel_id=1, source_target_pairs={{0,32},{32,64},{64,96},{96,128},{128,160},{160,192},{192,224},{224... | collective-permute-start | bytes 49160 | tf_op jit(solution)/shard_map/ppermute | solution.py:236
  20.3 1.3 %collective-permute-start.1 = (bf16[32,256]{1,0:T(8,128)(2,1)S(1)}, bf16[32,256]{1,0:T(8,128)(2,1)S(1)}, u32[]{:S(2)}, u32[]{:S(2)}) collective-permute-start(bf16[32,256]{1,0:T(8,128)(2,1)S(1)} %copy-done.9), channel_id=1, source_target_pairs={{32,0},{64,32},{96,64},{128,96},{160,128},{192,160},{224,192},{256... | collective-permute-start | bytes 49160 | tf_op jit(solution)/shard_map/ppermute | solution.py:236
  21.7 7.1 %collective-permute-done.1 = bf16[32,256]{1,0:T(8,128)(2,1)S(1)} collective-permute-done((bf16[32,256]{1,0:T(8,128)(2,1)S(1)}, bf16[32,256]{1,0:T(8,128)(2,1)S(1)}, u32[]{:S(2)}, u32[]{:S(2)}) %collective-permute-start.1) | collective-permute-done | bytes 16416 | tf_op jit(solution)/shard_map/ppermute | solution.py:236
  29.0 4.3 %collective-permute-start.2 = (bf16[512,256]{1,0:T(8,128)(2,1)S(1)}, bf16[512,256]{1,0:T(8,128)(2,1)S(1)}, u32[]{:S(2)}, u32[]{:S(2)}) collective-permute-start(bf16[512,256]{1,0:T(8,128)(2,1)S(1)} %get-tuple-element.20.own), channel_id=1, source_target_pairs={{0,1},{1,0},{2,3},{3,2},{4,5},{5,4},{6,7},{7,6},{8,9},{9,8},{10,11... | collective-permute-start | bytes 786440 | tf_op jit(solution)/shard_map/ppermute | solution.py:231
  35.9 5.1 %shard_map.147 = (f32[16,56,256]{2,1,0:T(8,128)S(1)}, f32[16,56,256]{2,1,0:T(8,128)S(1)}, f32[32,256]{1,0:T(8,128)S(1)}, f32[32,256]{1,0:T(8,128)S(1)}, f32[32,256]{1,0:T(8,128)S(1)}) custom-call(s32[3]{0:T(128)S(1)} %pad_add_fusion.places, s32[16,128]{1,0:T(8,128)S(1)} %bitcast.17, s32[16,128]{1,0:T(8,128)S(1)} %bitcast.18, s32[16,128]{1,0:T(8,128)S(1)} %bitcast.19, ...), custom_call_target="tpu_custom_call" | custom-call | tf_op jit(solution)/shard_map/pallas_call | solution.py:126
  41.0 1.9 %collective-permute-start.3 = (f32[16,56,256]{2,1,0:T(8,128)S(1)}, f32[16,56,256]{2,1,0:T(8,128)S(1)}, u32[]{:S(2)}, u32[]{:S(2)}) collective-permute-start(f32[16,56,256]{2,1,0:T(8,128)S(1)} %get-tuple-element.23), channel_id=1, source_target_pairs={{0,1},{1,0},{2,3},{3,2},{4,5},{5,4},{6,7},{7,6},{8,9},{9,8},{10,11... | collective-permute-start | bytes 2752520 | tf_op jit(solution)/shard_map/ppermute | solution.py:231
  42.9 2.4 %collective-permute-done.3 = f32[16,56,256]{2,1,0:T(8,128)S(1)} collective-permute-done((f32[16,56,256]{2,1,0:T(8,128)S(1)}, f32[16,56,256]{2,1,0:T(8,128)S(1)}, u32[]{:S(2)}, u32[]{:S(2)}) %collective-permute-start.3) | collective-permute-done | bytes 917536 | tf_op jit(solution)/shard_map/ppermute | solution.py:231
  45.4 0.9 add_convert_fusion
  46.2 10.7 %all-to-all-start.1 = ((bf16[16,56,256]{2,1,0:T(8,128)(2,1)}), bf16[16,56,256]{2,1,0:T(8,128)(2,1)S(1)}, u32[]{:S(2)}, u32[]{:S(2)}) async-start(bf16[16,56,256]{2,1,0:T(8,128)(2,1)} %add_convert_fusion), calls=%async_computation.1 | async-start | bytes 917504 | tf_op jit(solution)/shard_map/all_to_all | solution.py:225
  57.0 2.3 %collective-permute-start.4 = (f32[32,256]{1,0:T(8,128)S(1)}, f32[32,256]{1,0:T(8,128)S(1)}, u32[]{:S(2)}, u32[]{:S(2)}) collective-permute-start(f32[32,256]{1,0:T(8,128)S(1)} %get-tuple-element.27), channel_id=1, source_target_pairs={{0,1},{1,0},{2,3},{3,2},{4,5},{5,4},{6,7},{7,6},{8,9},{9,8},{10,11... | collective-permute-start | bytes 98312 | tf_op jit(solution)/shard_map/ppermute | solution.py:231
  59.3 12.1 %all-to-all-done.1.parts = bf16[16,56,256]{2,1,0:T(8,128)(2,1)S(1)} async-done(((bf16[16,56,256]{2,1,0:T(8,128)(2,1)}), bf16[16,56,256]{2,1,0:T(8,128)(2,1)S(1)}, u32[]{:S(2)}, u32[]{:S(2)}) %all-to-all-start.1) | async-done | bytes 458784 | tf_op jit(solution)/shard_map/all_to_all | solution.py:225
  72.2 3.3 %all-to-all-start.2 = ((f32[4,24,256]{2,1,0:T(8,128)}), f32[4,24,256]{2,1,0:T(8,128)S(1)}, u32[]{:S(2)}, u32[]{:S(2)}) async-start(f32[4,24,256]{2,1,0:T(8,128)} %get-tuple-element.24), calls=%async_computation.2 | async-start | bytes 196608 | tf_op jit(solution)/shard_map/all_to_all | solution.py:225
  75.5 6.2 %collective-permute-start.5 = (f32[64,256]{1,0:T(8,128)S(1)}, f32[64,256]{1,0:T(8,128)S(1)}, u32[]{:S(2)}, u32[]{:S(2)}) collective-permute-start(f32[64,256]{1,0:T(8,128)S(1)} %maximum_select_fusion), channel_id=1, source_target_pairs={{1,33},{3,35},{5,37},{7,39},{9,41},{11,43},{13,45},{15,47},{17,49}... | collective-permute-start | bytes 196616 | tf_op jit(solution)/shard_map/ppermute | solution.py:249
  82.4 6.1 %all-to-all-start.3 = ((f32[4,24,256]{2,1,0:T(8,128)}), f32[4,24,256]{2,1,0:T(8,128)S(1)}, u32[]{:S(2)}, u32[]{:S(2)}) async-start(f32[4,24,256]{2,1,0:T(8,128)} %shard_map.149), calls=%async_computation.3 | async-start | bytes 196608 | tf_op jit(solution)/shard_map/all_to_all | solution.py:225
  88.5 5.2 %collective-permute-start.6 = (f32[32,256]{1,0:T(8,128)S(1)}, f32[32,256]{1,0:T(8,128)S(1)}, u32[]{:S(2)}, u32[]{:S(2)}) collective-permute-start(f32[32,256]{1,0:T(8,128)S(1)} %get-tuple-element.35), channel_id=1, source_target_pairs={{0,1},{1,0},{2,3},{3,2},{4,5},{5,4},{6,7},{7,6},{8,9},{9,8},{10,11... | collective-permute-start | bytes 98312 | tf_op jit(solution)/shard_map/ppermute | solution.py:231
  93.7 0.8 collective-permute-done.6.there
  94.6 5.8 %all-to-all-done.3.parts = f32[4,24,256]{2,1,0:T(8,128)S(1)} async-done(((f32[4,24,256]{2,1,0:T(8,128)}), f32[4,24,256]{2,1,0:T(8,128)S(1)}, u32[]{:S(2)}, u32[]{:S(2)}) %all-to-all-start.3) | async-done | bytes 98336 | tf_op jit(solution)/shard_map/all_to_all | solution.py:225
  100.4 0.8 shard_map.150
  101.2 11.3 %all_to_all.25.own = bf16[16,24,256]{2,1,0:T(8,128)(2,1)S(1)} all-to-all(bf16[16,24,256]{2,1,0:T(8,128)(2,1)S(1)} %get-tuple-element.30), channel_id=1, replica_groups={{0,2,4,6,8,10,12,14,16,18,20,22,24,26,28,30},{1,3,5,7,9,11,13,15,17,19,..., dimensions={0} | all-to-all | bytes 393216 | tf_op jit(solution)/shard_map/all_to_all | solution.py:225
  112.5 7.4 %collective-permute-start.7 = (bf16[16,24,256]{2,1,0:T(8,128)(2,1)S(1)}, bf16[16,24,256]{2,1,0:T(8,128)(2,1)S(1)}, u32[]{:S(2)}, u32[]{:S(2)}) collective-permute-start(bf16[16,24,256]{2,1,0:T(8,128)(2,1)S(1)} %all_to_all.25.own), channel_id=1, source_target_pairs={{0,1},{1,0},{2,3},{3,2},{4,5},{5,4},{6,7},{7,6},{8,9},{9,8},{10,11... | collective-permute-start | bytes 589832 | tf_op jit(solution)/shard_map/ppermute | solution.py:231
  119.9 1.0 collective-permute-done.7.other
  121.0 0.9 shard_map.151
  (37 shorter events, 3.5 us)
Async XLA Ops:
  0.6 33.4 %copy-start.7 = (bf16[1,16,169,128]{3,1,2,0:T(8,128)(2,1)S(1)}, bf16[1,16,169,128]{3,1,2,0:T(8,128)(2,1)}, u32[]{:S(2)}) copy-start(bf16[1,16,169,128]{3,1,2,0:T(8,128)(2,1)} %param.13) | copy-start | bytes 2076676
  0.6 10.9 %copy-start.9 = (bf16[32,256]{1,0:T(8,128)(2,1)S(1)}, bf16[32,256]{1,0:T(8,128)(2,1)}, u32[]{:S(2)}) copy-start(bf16[32,256]{1,0:T(8,128)(2,1)} %param.11) | copy-start | bytes 49156
  2.2 26.6 %copy-start = (bf16[256,256]{1,0:T(8,128)(2,1)S(1)}, bf16[256,256]{1,0:T(8,128)(2,1)}, u32[]{:S(2)}) copy-start(bf16[256,256]{1,0:T(8,128)(2,1)} %w_right.3) | copy-start | bytes 393220
  2.2 26.6 %all-to-all-start = ((bf16[16,32,256]{2,1,0:T(8,128)(2,1)}), bf16[16,32,256]{2,1,0:T(8,128)(2,1)S(1)}, u32[]{:S(2)}, u32[]{:S(2)}) async-start(bf16[16,32,256]{2,1,0:T(8,128)(2,1)} %broadcast_in_dim.2), calls=%async_computation | async-start | bytes 524288 | tf_op jit(solution)/shard_map/all_to_all | solution.py:225
  11.5 10.1 %collective-permute-start = (bf16[32,256]{1,0:T(8,128)(2,1)S(1)}, bf16[32,256]{1,0:T(8,128)(2,1)S(1)}, u32[]{:S(2)}, u32[]{:S(2)}) collective-permute-start(bf16[32,256]{1,0:T(8,128)(2,1)S(1)} %copy-done.9), channel_id=1, source_target_pairs={{0,32},{32,64},{64,96},{96,128},{128,160},{160,192},{192,224},{224... | collective-permute-start | bytes 49160 | tf_op jit(solution)/shard_map/ppermute | solution.py:236
  20.3 8.4 %collective-permute-start.1 = (bf16[32,256]{1,0:T(8,128)(2,1)S(1)}, bf16[32,256]{1,0:T(8,128)(2,1)S(1)}, u32[]{:S(2)}, u32[]{:S(2)}) collective-permute-start(bf16[32,256]{1,0:T(8,128)(2,1)S(1)} %copy-done.9), channel_id=1, source_target_pairs={{32,0},{64,32},{96,64},{128,96},{160,128},{192,160},{224,192},{256... | collective-permute-start | bytes 49160 | tf_op jit(solution)/shard_map/ppermute | solution.py:236
  29.0 6.0 %collective-permute-start.2 = (bf16[512,256]{1,0:T(8,128)(2,1)S(1)}, bf16[512,256]{1,0:T(8,128)(2,1)S(1)}, u32[]{:S(2)}, u32[]{:S(2)}) collective-permute-start(bf16[512,256]{1,0:T(8,128)(2,1)S(1)} %get-tuple-element.20.own), channel_id=1, source_target_pairs={{0,1},{1,0},{2,3},{3,2},{4,5},{5,4},{6,7},{7,6},{8,9},{9,8},{10,11... | collective-permute-start | bytes 786440 | tf_op jit(solution)/shard_map/ppermute | solution.py:231
  34.0 0.9 copy-start.8
  34.0 1.0 copy-start.6
  34.9 0.9 copy-start.1
  34.9 1.0 copy-start.2
  34.9 1.0 copy-start.5
  34.9 0.9 copy-start.3
  35.0 0.9 copy-start.4
  41.0 4.4 %collective-permute-start.3 = (f32[16,56,256]{2,1,0:T(8,128)S(1)}, f32[16,56,256]{2,1,0:T(8,128)S(1)}, u32[]{:S(2)}, u32[]{:S(2)}) collective-permute-start(f32[16,56,256]{2,1,0:T(8,128)S(1)} %get-tuple-element.23), channel_id=1, source_target_pairs={{0,1},{1,0},{2,3},{3,2},{4,5},{5,4},{6,7},{7,6},{8,9},{9,8},{10,11... | collective-permute-start | bytes 2752520 | tf_op jit(solution)/shard_map/ppermute | solution.py:231
  46.2 25.2 %all-to-all-start.1 = ((bf16[16,56,256]{2,1,0:T(8,128)(2,1)}), bf16[16,56,256]{2,1,0:T(8,128)(2,1)S(1)}, u32[]{:S(2)}, u32[]{:S(2)}) async-start(bf16[16,56,256]{2,1,0:T(8,128)(2,1)} %add_convert_fusion), calls=%async_computation.1 | async-start | bytes 917504 | tf_op jit(solution)/shard_map/all_to_all | solution.py:225
  57.0 18.5 %collective-permute-start.4 = (f32[32,256]{1,0:T(8,128)S(1)}, f32[32,256]{1,0:T(8,128)S(1)}, u32[]{:S(2)}, u32[]{:S(2)}) collective-permute-start(f32[32,256]{1,0:T(8,128)S(1)} %get-tuple-element.27), channel_id=1, source_target_pairs={{0,1},{1,0},{2,3},{3,2},{4,5},{5,4},{6,7},{7,6},{8,9},{9,8},{10,11... | collective-permute-start | bytes 98312 | tf_op jit(solution)/shard_map/ppermute | solution.py:231
  72.2 9.6 %all-to-all-start.2 = ((f32[4,24,256]{2,1,0:T(8,128)}), f32[4,24,256]{2,1,0:T(8,128)S(1)}, u32[]{:S(2)}, u32[]{:S(2)}) async-start(f32[4,24,256]{2,1,0:T(8,128)} %get-tuple-element.24), calls=%async_computation.2 | async-start | bytes 196608 | tf_op jit(solution)/shard_map/all_to_all | solution.py:225
  75.5 13.0 %collective-permute-start.5 = (f32[64,256]{1,0:T(8,128)S(1)}, f32[64,256]{1,0:T(8,128)S(1)}, u32[]{:S(2)}, u32[]{:S(2)}) collective-permute-start(f32[64,256]{1,0:T(8,128)S(1)} %maximum_select_fusion), channel_id=1, source_target_pairs={{1,33},{3,35},{5,37},{7,39},{9,41},{11,43},{13,45},{15,47},{17,49}... | collective-permute-start | bytes 196616 | tf_op jit(solution)/shard_map/ppermute | solution.py:249
  82.4 18.0 %all-to-all-start.3 = ((f32[4,24,256]{2,1,0:T(8,128)}), f32[4,24,256]{2,1,0:T(8,128)S(1)}, u32[]{:S(2)}, u32[]{:S(2)}) async-start(f32[4,24,256]{2,1,0:T(8,128)} %shard_map.149), calls=%async_computation.3 | async-start | bytes 196608 | tf_op jit(solution)/shard_map/all_to_all | solution.py:225
  88.5 6.0 %collective-permute-start.6 = (f32[32,256]{1,0:T(8,128)S(1)}, f32[32,256]{1,0:T(8,128)S(1)}, u32[]{:S(2)}, u32[]{:S(2)}) collective-permute-start(f32[32,256]{1,0:T(8,128)S(1)} %get-tuple-element.35), channel_id=1, source_target_pairs={{0,1},{1,0},{2,3},{3,2},{4,5},{5,4},{6,7},{7,6},{8,9},{9,8},{10,11... | collective-permute-start | bytes 98312 | tf_op jit(solution)/shard_map/ppermute | solution.py:231
  112.5 8.5 %collective-permute-start.7 = (bf16[16,24,256]{2,1,0:T(8,128)(2,1)S(1)}, bf16[16,24,256]{2,1,0:T(8,128)(2,1)S(1)}, u32[]{:S(2)}, u32[]{:S(2)}) collective-permute-start(bf16[16,24,256]{2,1,0:T(8,128)(2,1)S(1)} %all_to_all.25.own), channel_id=1, source_target_pairs={{0,1},{1,0},{2,3},{3,2},{4,5},{5,4},{6,7},{7,6},{8,9},{9,8},{10,11... | collective-permute-start | bytes 589832 | tf_op jit(solution)/shard_map/ppermute | solution.py:231

commit v5 on v4

--- a/solution.py
+++ b/solution.py
@@ -8,11 +8,11 @@
 F32, BF16 = jnp.float32, jnp.bfloat16
 VMEM = pl.BlockSpec(memory_space=pltpu.VMEM)
 SMEM = pl.BlockSpec(memory_space=pltpu.SMEM)
-PARAMS = pltpu.CompilerParams(vmem_limit_bytes=48 * 1024 * 1024)
+PARAMS = pltpu.CompilerParams(vmem_limit_bytes=32 * 1024 * 1024)
 BOTH = ("row", "col")
 BLOCKS_PER_STEP = 8
 OUT_ROWS = 176
-X_BITS, Z_BITS, CHIP_BITS = (4, 8), (1, 2), (2, 4, 8, 16)
+X_BITS, Z_BITS, CHIP_BITS, COL_BITS = (4, 8), (1, 2), (2, 4, 8, 16), (1, 2, 4, 8, 16)
 
 
 def like(*shape):
@@ -28,58 +28,79 @@
     return high, (x - high.astype(F32)).astype(BF16)
 
 
-def pair_kernel(
-    places, rows, cols, mask, harm, grads, own, other, column_nodes, v_parts, w_left, w_harm, w_out,
-    keep, send, middle, ahead, passed, u_parts, harm_t, out_t, sum_u, sum_v, weights,
+def line(ref, first):
+    return jnp.concatenate([ref[pl.ds(first + k, 1), :] for k in range(BLOCKS_PER_STEP)], axis=1)
+
+
+def beside(ref, first):
+    return jnp.concatenate([ref[first + k] for k in range(BLOCKS_PER_STEP)], axis=1)
+
+
+def masked(places, mask, grads, first):
+    live = [
+        mask[pl.ds(first + k, 1), :] * (first + k < places[0]).astype(jnp.int32)
+        for k in range(BLOCKS_PER_STEP)
+    ]
+    return beside(grads, first) * jnp.concatenate(live, axis=1).astype(F32).astype(BF16)
+
+
+def picks(line_of_pairs, atoms):
+    shape = (atoms, line_of_pairs.shape[1])
+    at = lax.broadcasted_iota(jnp.int32, shape, 0) == line_of_pairs
+    return at.astype(F32).astype(BF16)
+
+
+def steps_of(places):
+    return lax.div(places[0] + BLOCKS_PER_STEP - 1, BLOCKS_PER_STEP)
+
+
+def row_pair_kernel(
+    places, rows, mask, harm, grads, row_nodes, nodes, w_left, w_harm, w_out,
+    u_pairs, e_pairs, gz_pairs, same_nodes, u_parts, harm_t, out_t,
 ):
-    count, column_base, core = places[0], places[1], places[2]
+    same_nodes[...] = nodes[...]
     width = w_left.shape[0]
-    half, near = own.shape[0], column_nodes.shape[0]
-    atoms = 2 * half
-    shard = near // 3
-    pairs = BLOCKS_PER_STEP * mask.shape[1]
-    orbitals, harmonics = w_out.shape[0], w_harm.shape[0]
-    for first, nodes in ((0, own), (half, other)):
-        high, low = halves(dot(w_left[...], nodes[...], 0, 1))
-        u_parts[:width, first : first + half] = high
-        u_parts[width:, first : first + half] = low
+    high, low = halves(dot(w_left[...], row_nodes[...], 0, 1))
+    u_parts[:width] = high
+    u_parts[width:] = low
     harm_t[...] = w_harm[...].astype(F32).T.astype(BF16)
     out_t[...] = w_out[...].astype(F32).T.astype(BF16)
+
+    def step(i, carry):
+        first = BLOCKS_PER_STEP * i
+        parts = dot(u_parts[...], picks(line(rows, first), row_nodes.shape[0]), 1, 0)
+        u_pairs[i] = parts[:width] + parts[width:]
+        e_pairs[i] = dot(harm_t[...], beside(harm, first), 1, 0)
+        gz_pairs[i] = dot(out_t[...], masked(places, mask, grads, first), 1, 0)
+        return carry
+
+    lax.fori_loop(0, steps_of(places), step, 0)
+
+
+def pair_kernel(
+    places, rows, cols, mask, harm, grads, row_nodes, column_nodes, w_right,
+    u_pairs, e_pairs, gz_pairs,
+    keep, send, middle, ahead, passed, v_parts, sum_u, sum_v, weights,
+):
+    column_base, core = places[1], places[2]
+    width = w_right.shape[0]
+    atoms, near = row_nodes.shape[0], column_nodes.shape[0]
+    shard = near // 3
+    orbitals, harmonics = grads.shape[1], harm.shape[1]
+    v_parts[...] = jnp.concatenate(halves(dot(w_right[...], column_nodes[...], 0, 1)), axis=1)
     for total in (sum_u, sum_v, weights):
         total[...] = jnp.zeros_like(total)
     at_out = 2 * width
     at_harm = at_out + OUT_ROWS
 
-    def line(ref, first):
-        return jnp.concatenate(
-            [ref[pl.ds(first + k, 1), :] for k in range(BLOCKS_PER_STEP)], axis=1
-        )
-
     def step(i, carry):
         first = BLOCKS_PER_STEP * i
-        live = jnp.concatenate(
-            [
-                mask[pl.ds(first + k, 1), :] * (first + k < count).astype(jnp.int32)
-                for k in range(BLOCKS_PER_STEP)
-            ],
-            axis=1,
-        )
-        g = jnp.concatenate([grads[first + k] for k in range(BLOCKS_PER_STEP)], axis=1)
-        g = g * live.astype(F32).astype(BF16)
-        h = jnp.concatenate([harm[first + k] for k in range(BLOCKS_PER_STEP)], axis=1)
-        atom = line(rows, first)
-        owner = lax.div(atom, shard)
-        place = lax.shift_right_logical(owner, 1) * shard + lax.rem(atom, shard)
-        place = place + jnp.where(jnp.bitwise_and(owner, 1) == core, 0, half)
-        at_u = lax.broadcasted_iota(jnp.int32, (atoms, pairs), 0) == place
-        at_v = lax.broadcasted_iota(jnp.int32, (near, pairs), 0) == line(cols, first) - column_base
-        pick_u = at_u.astype(F32).astype(BF16)
-        pick_v = at_v.astype(F32).astype(BF16)
-        parts = dot(u_parts[...], pick_u, 1, 0)
-        u = parts[:width] + parts[width:]
+        g = masked(places, mask, grads, first)
+        h = beside(harm, first)
+        pick_u = picks(line(rows, first), atoms)
+        pick_v = picks(line(cols, first) - column_base, near)
         v = dot(v_parts[...], jnp.concatenate([pick_v, pick_v]), 1, 0)
-        e = dot(harm_t[...], h, 1, 0)
-        gz = dot(out_t[...], g, 1, 0)
+        u, e, gz = u_pairs[i], e_pairs[i], gz_pairs[i]
         uv = u * v
         weights[at_out : at_out + orbitals] += dot(g, (uv * e).astype(BF16), 1, 1)
         weights[at_harm : at_harm + harmonics] += dot(h, (gz * uv).astype(BF16), 1, 1)
@@ -90,21 +111,16 @@
         sum_v[...] += dot(pick_v, high, 1, 1) + dot(pick_v, low, 1, 1)
         return carry
 
-    lax.fori_loop(0, lax.div(count + BLOCKS_PER_STEP - 1, BLOCKS_PER_STEP), step, 0)
-    for at, blocks in (
-        (0, ((own, sum_u[:half]), (other, sum_u[half:]))),
-        (width, ((column_nodes, sum_v[...]),)),
-    ):
-        total = jnp.zeros((width, width), F32)
-        for nodes, sums in blocks:
-            for part in halves(sums):
-                total = total + dot(nodes[...], part, 0, 0)
-        weights[at : at + width] = total
+    lax.fori_loop(0, steps_of(places), step, 0)
+    for at, nodes, sums in ((0, row_nodes, sum_u), (width, column_nodes, sum_v)):
+        high, low = halves(sums[...])
+        weights[at : at + width] = dot(nodes[...], high, 0, 0) + dot(nodes[...], low, 0, 0)
     chips, chunk = keep.shape[0], keep.shape[1]
     share = chunk - shard
     for chip in range(chips):
-        for to, first, which in ((keep, 0, core), (send, half, 1 - core)):
-            to[chip, :shard] = sum_u[first + chip * shard : first + (chip + 1) * shard]
+        for to, which in ((keep, core), (send, 1 - core)):
+            start = pl.multiple_of((2 * chip + which) * shard, 8)
+            to[chip, :shard] = sum_u[pl.ds(start, shard), :]
             start = pl.multiple_of((which * chips + chip) * share, 8)
             to[chip, shard:] = weights[pl.ds(start, share), :]
     middle[...] = sum_v[shard : 2 * shard]
@@ -112,32 +128,46 @@
     passed[...] = sum_v[pl.ds(pl.multiple_of((1 - core) * 2 * shard, 8), shard), :]
 
 
-def project_kernel(own, column_nodes, w_right, copy, v_parts):
-    copy[...] = own[...]
-    v_parts[...] = jnp.concatenate(halves(dot(w_right[...], column_nodes[...], 0, 1)), axis=1)
-
-
-def pair_sums(places, rows, cols, mask, harm, grads, own, other, column_nodes, v_parts, weights_in, chips, share):
-    half, width = own.shape
+def row_pairs(places, rows, mask, harm, grads, row_nodes, nodes, w_left, w_harm, w_out):
+    atoms, width = row_nodes.shape
+    pairs = BLOCKS_PER_STEP * rows.shape[1]
+    steps = rows.shape[0] // BLOCKS_PER_STEP
+    per_pair = like(steps, width, pairs)
+    flops = 2 * steps * pairs * width * (2 * atoms + w_harm.shape[0] + w_out.shape[0])
+    return pl.pallas_call(
+        row_pair_kernel,
+        out_shape=(per_pair,) * 3 + (jax.ShapeDtypeStruct(nodes.shape, BF16),),
+        in_specs=[SMEM] + [VMEM] * 9,
+        out_specs=(VMEM,) * 4,
+        scratch_shapes=[
+            pltpu.VMEM((2 * width, atoms), BF16),
+            pltpu.VMEM(w_harm.shape[::-1], BF16),
+            pltpu.VMEM(w_out.shape[::-1], BF16),
+        ],
+        compiler_params=PARAMS,
+        cost_estimate=pl.CostEstimate(flops=flops, bytes_accessed=8 << 20, transcendentals=0),
+    )(places, rows, mask, harm, grads, row_nodes, nodes, w_left, w_harm, w_out)
+
+
+def pair_sums(
+    places, rows, cols, mask, harm, grads, row_nodes, column_nodes, w_right, per_pair, chips, share
+):
+    atoms, width = row_nodes.shape
     near = column_nodes.shape[0]
-    shard = near // 3
-    chunks, block = like(chips, shard + share, width), like(shard, width)
-    w_harm, w_out = weights_in[1:]
+    chunks, block = like(chips, near // 3 + share, width), like(near // 3, width)
     return pl.pallas_call(
         pair_kernel,
-        out_shape=(chunks, chunks, block, block, block),
-        in_specs=[SMEM] + [VMEM] * 12,
+        out_shape=(chunks,) * 2 + (block,) * 3,
+        in_specs=[SMEM] + [VMEM] * 11,
         out_specs=(VMEM,) * 5,
         scratch_shapes=[
-            pltpu.VMEM((2 * width, 2 * half), BF16),
-            pltpu.VMEM(w_harm.shape[::-1], BF16),
-            pltpu.VMEM(w_out.shape[::-1], BF16),
-            pltpu.VMEM((2 * half, width), F32),
+            pltpu.VMEM((width, 2 * near), BF16),
+            pltpu.VMEM((atoms, width), F32),
             pltpu.VMEM((near, width), F32),
             pltpu.VMEM((2 * chips * share, width), F32),
         ],
         compiler_params=PARAMS,
-    )(places, rows, cols, mask, harm, grads, own, other, column_nodes, v_parts, *weights_in)
+    )(places, rows, cols, mask, harm, grads, row_nodes, column_nodes, w_right, *per_pair)
 
 
 def total_of(parts):
@@ -249,8 +279,13 @@
     return lax.ppermute(block, BOTH, route)
 
 
+def repeat_kernel(block, out):
+    for i in range(out.shape[0]):
+        out[i] = block[...]
+
+
 def repeated(block, copies):
-    return jnp.broadcast_to(block[None], (copies,) + block.shape)
+    return call(repeat_kernel, jax.ShapeDtypeStruct((copies,) + block.shape, block.dtype), block)
 
 
 def body(
@@ -273,21 +308,18 @@
     spread = 4
     row = lax.axis_index("row")
     core = jnp.bitwise_and(lax.axis_index("col"), 1)
-    column_nodes = jnp.concatenate([shifted(nodes, 1), nodes, shifted(nodes, -1)])
-    own = exchange(repeated(nodes, chips), "col", CHIP_BITS).reshape(-1, width)
-    own, v_parts = call(
-        project_kernel,
-        (
-            jax.ShapeDtypeStruct(own.shape, BF16),
-            jax.ShapeDtypeStruct((width, 2 * column_nodes.shape[0]), BF16),
-        ),
-        own, column_nodes, w_right,
-    )
-    other = swapped(own)
+    before, after = shifted(nodes, 1), shifted(nodes, -1)
+    row_nodes = exchange(repeated(nodes, columns), "col", COL_BITS).reshape(-1, width)
     places = jnp.stack([block_counts[0, 0], (row - 1) * shard, core]).astype(jnp.int32)
+    rows, cols, mask = pair_rows[0], pair_cols[0], pair_mask[0]
+    harm, grads = harmonics[0], grad_blocks[0]
+    *per_pair, same_nodes = row_pairs(
+        places, rows, mask, harm, grads, row_nodes, nodes, w_left, w_harm, w_out
+    )
+    column_nodes = jnp.concatenate([before, same_nodes, after])
     keep, send, middle, ahead, passed = pair_sums(
-        places, pair_rows[0], pair_cols[0], pair_mask[0], harmonics[0], grad_blocks[0],
-        own, other, column_nodes, v_parts, (w_left, w_harm, w_out), chips, share,
+        places, rows, cols, mask, harm, grads, row_nodes, column_nodes, w_right, per_pair,
+        chips, share,
     )
     parts = (keep + swapped(send)).astype(BF16)
     parts = exchange(parts, "col", CHIP_BITS)

time: 123 us -> 119 us (0.967)
  starting transfers between devices: 66.9 us -> 61.6 us
  Pallas kernels: 8.55 us -> 13.8 us
  waiting for transfers between devices: 29.4 us -> 27.6 us
    ppermute x2, waiting for transfers between devices: 7.06 us -> 0.01 us  [shifted(): lax.ppermute(block, 'row', [(i, i + distance) for i in devices if i + dis...]
    all_to_all x4, waiting for transfers between devices: 18 us -> 23.3 us  [exchange(): lax.all_to_all(blocks, axis, 0, 0, tiled=True, axis_index_groups=groups(l...]
    pallas_call x1 -> x2, Pallas kernels: 5.14 us -> 9.85 us  [the longest x1 5.91 us: pair_sums(): pl.pallas_call(pair_kernel, out_shape=(chunks,) * 2 + (block,) * 3, in_sp...]
    ppermute x5 -> x4, starting transfers between devices: 21.2 us -> 16.5 us  [swapped(): lax.ppermute(block, 'col', [(i, i ^ 1) for i in range(lax.axis_size('col'...]
    broadcast_in_dim x1 -> x0, local copies, waits for them, and re-layouts: 1.52 us -> none  [repeated(): return jnp.broadcast_to(block[None], (copies,) + block.shape)]
    ppermute x5 -> x4, waiting for transfers between devices: 4.33 us -> 4.33 us  [swapped(): lax.ppermute(block, 'col', [(i, i ^ 1) for i in range(lax.axis_size('col'...]
  transfers between devices with their start and end apart: 12 -> 11, of which waited for: 6 -> 6; matrix products, arithmetic and copies ran while one was open for 0% -> 1% of each run, Pallas kernels for 1% -> 5%
where the time goes in v5:
time: 119 us
  starting transfers between devices  61.6 us (52%)
  waiting for transfers between devices  27.6 us (23%)
  Pallas kernels  13.8 us (12%)
  blocking collectives  11 us (9%)
  local copies, waits for them, and re-layouts  2.11 us (2%)
  between operations  1.55 us (1%)
    all_to_all x4, starting transfers between devices, exchange(): lax.all_to_all(blocks, axis, 0, 0, tiled=True, axis_index_groups=groups(l...  28.4 us
    all_to_all x4, waiting for transfers between devices, exchange(): lax.all_to_all(blocks, axis, 0, 0, tiled=True, axis_index_groups=groups(l...  23.3 us
    ppermute x4, starting transfers between devices, swapped(): lax.ppermute(block, 'col', [(i, i ^ 1) for i in range(lax.axis_size('col'...  16.5 us
    all_to_all x1, blocking collectives, exchange(): lax.all_to_all(blocks, axis, 0, 0, tiled=True, axis_index_groups=groups(l...  11 us
    ppermute x2, starting transfers between devices, shifted(): lax.ppermute(block, 'row', [(i, i + distance) for i in devices if i + dis...  9.88 us
    ppermute x1, starting transfers between devices, neighbours(): return lax.ppermute(block, BOTH, route)  6.84 us
    pallas_call x1, Pallas kernels, pair_sums(): pl.pallas_call(pair_kernel, out_shape=(chunks,) * 2 + (block,) * 3, in_sp...  5.91 us
    ppermute x4, waiting for transfers between devices, swapped(): lax.ppermute(block, 'col', [(i, i ^ 1) for i in range(lax.axis_size('col'...  4.33 us
  transfers between devices with their start and end apart: 11, of which 6 were waited for; matrix products, arithmetic and copies ran while one was open for 1% of the time, Pallas kernels for 5%

profile of v5, /device:TPU:1, one launch (start us, length us, event | category | flops | bytes accessed | tf_op | source)
XLA Modules:
  0.0 118.7 jit_solution(8014630684461351782)
XLA Ops:
  1.4 0.9 shard_map.146
  2.3 10.4 %all-to-all-start = ((bf16[32,32,256]{2,1,0:T(8,128)(2,1)}), bf16[32,32,256]{2,1,0:T(8,128)(2,1)S(1)}, u32[]{:S(2)}, u32[]{:S(2)}) async-start(bf16[32,32,256]{2,1,0:T(8,128)(2,1)} %shard_map.146), calls=%async_computation | async-start | bytes 1048576 | tf_op jit(solution)/shard_map/all_to_all | solution.py:255
  12.7 8.6 %collective-permute-start = (bf16[32,256]{1,0:T(8,128)(2,1)}, bf16[32,256]{1,0:T(8,128)(2,1)S(1)}, u32[]{:S(2)}, u32[]{:S(2)}) collective-permute-start(bf16[32,256]{1,0:T(8,128)(2,1)} %nodes.1), channel_id=1, source_target_pairs={{0,32},{32,64},{64,96},{96,128},{128,160},{160,192},{192,224},{224... | collective-permute-start | bytes 49160 | tf_op jit(solution)/shard_map/ppermute | solution.py:266
  21.3 1.3 %collective-permute-start.1 = (bf16[32,256]{1,0:T(8,128)(2,1)}, bf16[32,256]{1,0:T(8,128)(2,1)S(1)}, u32[]{:S(2)}, u32[]{:S(2)}) collective-permute-start(bf16[32,256]{1,0:T(8,128)(2,1)} %nodes.1), channel_id=1, source_target_pairs={{32,0},{64,32},{96,64},{128,96},{160,128},{192,160},{224,192},{256... | collective-permute-start | bytes 49160 | tf_op jit(solution)/shard_map/ppermute | solution.py:266
  23.3 1.3 %copy.20 = bf16[1,16,169,128]{3,2,1,0:T(8,128)(2,1)S(1)} copy(bf16[1,16,169,128]{3,1,2,0:T(8,128)(2,1)} %param.13) | data formatting | bytes 1384448 | tf_op args[2]
  24.7 4.9 %all-to-all-done = bf16[32,32,256]{2,1,0:T(8,128)(2,1)S(1)} async-done(((bf16[32,32,256]{2,1,0:T(8,128)(2,1)}), bf16[32,32,256]{2,1,0:T(8,128)(2,1)S(1)}, u32[]{:S(2)}, u32[]{:S(2)}) %all-to-all-start) | async-done | bytes 524320 | tf_op jit(solution)/shard_map/all_to_all | solution.py:255
  29.7 3.9 %shard_map.147 = (f32[2,256,1024]{2,1,0:T(8,128)S(1)}, f32[2,256,1024]{2,1,0:T(8,128)S(1)}, f32[2,256,1024]{2,1,0:T(8,128)S(1)}, bf16[32,256]{1,0:T(8,128)(2,1)S(1)}) custom-call(s32[3]{0:T(128)S(1)} %pad_add_fusion.places, s32[16,128]{1,0:T(8,128)S(1)} %bitcast.20, s32[16,128]{1,0:T(8,128)S(1)} %bitcast.23, bf16[16,25,128]{2,1,0:T(8,128)(2,1)S(1)} %bitcast.18, ...), custom_call_target="tpu_custom_call" | custom-call | flops 2350907392 | bytes 8388608 | tf_op jit(solution)/shard_map/pallas_call | solution.py:137
  33.7 5.9 %shard_map.148 = (f32[16,56,256]{2,1,0:T(8,128)S(1)}, f32[16,56,256]{2,1,0:T(8,128)S(1)}, f32[32,256]{1,0:T(8,128)S(1)}, f32[32,256]{1,0:T(8,128)S(1)}, f32[32,256]{1,0:T(8,128)S(1)}) custom-call(s32[3]{0:T(128)S(1)} %pad_add_fusion.places, s32[16,128]{1,0:T(8,128)S(1)} %bitcast.21, s32[16,128]{1,0:T(8,128)S(1)} %bitcast.22, s32[16,128]{1,0:T(8,128)S(1)} %bitcast.24, ...), custom_call_target="tpu_custom_call" | custom-call | tf_op jit(solution)/shard_map/pallas_call | solution.py:158
  39.6 1.9 %collective-permute-start.2 = (f32[16,56,256]{2,1,0:T(8,128)S(1)}, f32[16,56,256]{2,1,0:T(8,128)S(1)}, u32[]{:S(2)}, u32[]{:S(2)}) collective-permute-start(f32[16,56,256]{2,1,0:T(8,128)S(1)} %get-tuple-element.27), channel_id=1, source_target_pairs={{0,1},{1,0},{2,3},{3,2},{4,5},{5,4},{6,7},{7,6},{8,9},{9,8},{10,11... | collective-permute-start | bytes 2752520 | tf_op jit(solution)/shard_map/ppermute | solution.py:261
  41.6 2.4 %collective-permute-done.2 = f32[16,56,256]{2,1,0:T(8,128)S(1)} collective-permute-done((f32[16,56,256]{2,1,0:T(8,128)S(1)}, f32[16,56,256]{2,1,0:T(8,128)S(1)}, u32[]{:S(2)}, u32[]{:S(2)}) %collective-permute-start.2) | collective-permute-done | bytes 917536 | tf_op jit(solution)/shard_map/ppermute | solution.py:261
  44.0 0.9 add_convert_fusion
  44.9 4.1 %all-to-all-start.1 = ((bf16[16,56,256]{2,1,0:T(8,128)(2,1)}), bf16[16,56,256]{2,1,0:T(8,128)(2,1)S(1)}, u32[]{:S(2)}, u32[]{:S(2)}) async-start(bf16[16,56,256]{2,1,0:T(8,128)(2,1)} %add_convert_fusion), calls=%async_computation.1 | async-start | bytes 917504 | tf_op jit(solution)/shard_map/all_to_all | solution.py:255
  49.0 2.3 %collective-permute-start.3 = (f32[32,256]{1,0:T(8,128)S(1)}, f32[32,256]{1,0:T(8,128)S(1)}, u32[]{:S(2)}, u32[]{:S(2)}) collective-permute-start(f32[32,256]{1,0:T(8,128)S(1)} %get-tuple-element.31), channel_id=1, source_target_pairs={{0,1},{1,0},{2,3},{3,2},{4,5},{5,4},{6,7},{7,6},{8,9},{9,8},{10,11... | collective-permute-start | bytes 98312 | tf_op jit(solution)/shard_map/ppermute | solution.py:261
  51.3 12.1 %all-to-all-done.1.parts = bf16[16,56,256]{2,1,0:T(8,128)(2,1)S(1)} async-done(((bf16[16,56,256]{2,1,0:T(8,128)(2,1)}), bf16[16,56,256]{2,1,0:T(8,128)(2,1)S(1)}, u32[]{:S(2)}, u32[]{:S(2)}) %all-to-all-start.1) | async-done | bytes 458784 | tf_op jit(solution)/shard_map/all_to_all | solution.py:255
  64.2 5.6 %all-to-all-start.2 = ((f32[4,24,256]{2,1,0:T(8,128)}), f32[4,24,256]{2,1,0:T(8,128)S(1)}, u32[]{:S(2)}, u32[]{:S(2)}) async-start(f32[4,24,256]{2,1,0:T(8,128)} %get-tuple-element.28), calls=%async_computation.2 | async-start | bytes 196608 | tf_op jit(solution)/shard_map/all_to_all | solution.py:255
  69.8 6.8 %collective-permute-start.4 = (f32[64,256]{1,0:T(8,128)S(1)}, f32[64,256]{1,0:T(8,128)S(1)}, u32[]{:S(2)}, u32[]{:S(2)}) collective-permute-start(f32[64,256]{1,0:T(8,128)S(1)} %maximum_select_fusion), channel_id=1, source_target_pairs={{1,33},{3,35},{5,37},{7,39},{9,41},{11,43},{13,45},{15,47},{17,49}... | collective-permute-start | bytes 196616 | tf_op jit(solution)/shard_map/ppermute | solution.py:279
  77.3 8.3 %all-to-all-start.3 = ((f32[4,24,256]{2,1,0:T(8,128)}), f32[4,24,256]{2,1,0:T(8,128)S(1)}, u32[]{:S(2)}, u32[]{:S(2)}) async-start(f32[4,24,256]{2,1,0:T(8,128)} %shard_map.150), calls=%async_computation.3 | async-start | bytes 196608 | tf_op jit(solution)/shard_map/all_to_all | solution.py:255
  85.7 4.8 %collective-permute-start.5 = (f32[32,256]{1,0:T(8,128)S(1)}, f32[32,256]{1,0:T(8,128)S(1)}, u32[]{:S(2)}, u32[]{:S(2)}) collective-permute-start(f32[32,256]{1,0:T(8,128)S(1)} %get-tuple-element.39), channel_id=1, source_target_pairs={{0,1},{1,0},{2,3},{3,2},{4,5},{5,4},{6,7},{7,6},{8,9},{9,8},{10,11... | collective-permute-start | bytes 98312 | tf_op jit(solution)/shard_map/ppermute | solution.py:261
  90.5 0.8 collective-permute-done.5.there
  91.3 6.2 %all-to-all-done.3.parts = f32[4,24,256]{2,1,0:T(8,128)S(1)} async-done(((f32[4,24,256]{2,1,0:T(8,128)}), f32[4,24,256]{2,1,0:T(8,128)S(1)}, u32[]{:S(2)}, u32[]{:S(2)}) %all-to-all-start.3) | async-done | bytes 98336 | tf_op jit(solution)/shard_map/all_to_all | solution.py:255
  98.3 11.0 %all_to_all.25.own = bf16[16,24,256]{2,1,0:T(8,128)(2,1)S(1)} all-to-all(bf16[16,24,256]{2,1,0:T(8,128)(2,1)S(1)} %get-tuple-element.34), channel_id=1, replica_groups={{0,2,4,6,8,10,12,14,16,18,20,22,24,26,28,30},{1,3,5,7,9,11,13,15,17,19,..., dimensions={0} | all-to-all | bytes 393216 | tf_op jit(solution)/shard_map/all_to_all | solution.py:255
  109.3 7.4 %collective-permute-start.6 = (bf16[16,24,256]{2,1,0:T(8,128)(2,1)S(1)}, bf16[16,24,256]{2,1,0:T(8,128)(2,1)S(1)}, u32[]{:S(2)}, u32[]{:S(2)}) collective-permute-start(bf16[16,24,256]{2,1,0:T(8,128)(2,1)S(1)} %all_to_all.25.own), channel_id=1, source_target_pairs={{0,1},{1,0},{2,3},{3,2},{4,5},{5,4},{6,7},{7,6},{8,9},{9,8},{10,11... | collective-permute-start | bytes 589832 | tf_op jit(solution)/shard_map/ppermute | solution.py:261
  116.7 1.0 collective-permute-done.6.other
  117.7 0.9 shard_map.152
  (33 shorter events, 3.1 us)
Async XLA Ops:
  0.6 29.0 %copy-start.1 = (bf16[256,256]{1,0:T(8,128)(2,1)S(1)}, bf16[256,256]{1,0:T(8,128)(2,1)}, u32[]{:S(2)}) copy-start(bf16[256,256]{1,0:T(8,128)(2,1)} %w_left.3) | copy-start | bytes 393220
  0.6 0.8 copy-start.2
  1.4 23.2 %copy-start.9 = (bf16[1,16,25,128]{3,1,2,0:T(8,128)(2,1)S(1)}, bf16[1,16,25,128]{3,1,2,0:T(8,128)(2,1)}, u32[]{:S(2)}) copy-start(bf16[1,16,25,128]{3,1,2,0:T(8,128)(2,1)} %param.12) | copy-start | bytes 307204
  1.4 28.2 %copy-start.3 = (bf16[32,256]{1,0:T(8,128)(2,1)S(1)}, bf16[32,256]{1,0:T(8,128)(2,1)}, u32[]{:S(2)}) copy-start(bf16[32,256]{1,0:T(8,128)(2,1)} %nodes.1) | copy-start | bytes 49156
  1.4 28.2 %copy-start.4 = (s32[1,16,128]{2,1,0:T(8,128)S(1)}, s32[1,16,128]{2,1,0:T(8,128)}, u32[]{:S(2)}) copy-start(s32[1,16,128]{2,1,0:T(8,128)} %param.14) | copy-start | bytes 24580
  1.4 28.2 %copy-start.6 = (s32[1,16,128]{2,1,0:T(8,128)S(1)}, s32[1,16,128]{2,1,0:T(8,128)}, u32[]{:S(2)}) copy-start(s32[1,16,128]{2,1,0:T(8,128)} %param.16) | copy-start | bytes 24580
  1.4 28.3 %copy-start.7 = (bf16[169,256]{1,0:T(8,128)(2,1)S(1)}, bf16[169,256]{1,0:T(8,128)(2,1)}, u32[]{:S(2)}) copy-start(bf16[169,256]{1,0:T(8,128)(2,1)} %w_out.1) | copy-start | bytes 259588
  1.4 28.3 %copy-start.8 = (bf16[25,256]{1,0:T(8,128)(2,1)S(1)}, bf16[25,256]{1,0:T(8,128)(2,1)}, u32[]{:S(2)}) copy-start(bf16[25,256]{1,0:T(8,128)(2,1)} %w_harm.1) | copy-start | bytes 38404
  2.3 27.3 %all-to-all-start = ((bf16[32,32,256]{2,1,0:T(8,128)(2,1)}), bf16[32,32,256]{2,1,0:T(8,128)(2,1)S(1)}, u32[]{:S(2)}, u32[]{:S(2)}) async-start(bf16[32,32,256]{2,1,0:T(8,128)(2,1)} %shard_map.146), calls=%async_computation | async-start | bytes 1048576 | tf_op jit(solution)/shard_map/all_to_all | solution.py:255
  12.7 20.9 %collective-permute-start = (bf16[32,256]{1,0:T(8,128)(2,1)}, bf16[32,256]{1,0:T(8,128)(2,1)S(1)}, u32[]{:S(2)}, u32[]{:S(2)}) collective-permute-start(bf16[32,256]{1,0:T(8,128)(2,1)} %nodes.1), channel_id=1, source_target_pairs={{0,32},{32,64},{64,96},{96,128},{128,160},{160,192},{192,224},{224... | collective-permute-start | bytes 49160 | tf_op jit(solution)/shard_map/ppermute | solution.py:266
  21.3 12.4 %collective-permute-start.1 = (bf16[32,256]{1,0:T(8,128)(2,1)}, bf16[32,256]{1,0:T(8,128)(2,1)S(1)}, u32[]{:S(2)}, u32[]{:S(2)}) collective-permute-start(bf16[32,256]{1,0:T(8,128)(2,1)} %nodes.1), channel_id=1, source_target_pairs={{32,0},{64,32},{96,64},{128,96},{160,128},{192,160},{224,192},{256... | collective-permute-start | bytes 49160 | tf_op jit(solution)/shard_map/ppermute | solution.py:266
  29.7 4.0 %copy-start = (bf16[256,256]{1,0:T(8,128)(2,1)S(1)}, bf16[256,256]{1,0:T(8,128)(2,1)}, u32[]{:S(2)}) copy-start(bf16[256,256]{1,0:T(8,128)(2,1)} %w_right.3) | copy-start | bytes 393220
  29.7 4.0 %copy-start.5 = (s32[1,16,128]{2,1,0:T(8,128)S(1)}, s32[1,16,128]{2,1,0:T(8,128)}, u32[]{:S(2)}) copy-start(s32[1,16,128]{2,1,0:T(8,128)} %param.15) | copy-start | bytes 24580
  39.6 4.4 %collective-permute-start.2 = (f32[16,56,256]{2,1,0:T(8,128)S(1)}, f32[16,56,256]{2,1,0:T(8,128)S(1)}, u32[]{:S(2)}, u32[]{:S(2)}) collective-permute-start(f32[16,56,256]{2,1,0:T(8,128)S(1)} %get-tuple-element.27), channel_id=1, source_target_pairs={{0,1},{1,0},{2,3},{3,2},{4,5},{5,4},{6,7},{7,6},{8,9},{9,8},{10,11... | collective-permute-start | bytes 2752520 | tf_op jit(solution)/shard_map/ppermute | solution.py:261
  44.9 18.6 %all-to-all-start.1 = ((bf16[16,56,256]{2,1,0:T(8,128)(2,1)}), bf16[16,56,256]{2,1,0:T(8,128)(2,1)S(1)}, u32[]{:S(2)}, u32[]{:S(2)}) async-start(bf16[16,56,256]{2,1,0:T(8,128)(2,1)} %add_convert_fusion), calls=%async_computation.1 | async-start | bytes 917504 | tf_op jit(solution)/shard_map/all_to_all | solution.py:255
  49.0 20.8 %collective-permute-start.3 = (f32[32,256]{1,0:T(8,128)S(1)}, f32[32,256]{1,0:T(8,128)S(1)}, u32[]{:S(2)}, u32[]{:S(2)}) collective-permute-start(f32[32,256]{1,0:T(8,128)S(1)} %get-tuple-element.31), channel_id=1, source_target_pairs={{0,1},{1,0},{2,3},{3,2},{4,5},{5,4},{6,7},{7,6},{8,9},{9,8},{10,11... | collective-permute-start | bytes 98312 | tf_op jit(solution)/shard_map/ppermute | solution.py:261
  64.2 12.5 %all-to-all-start.2 = ((f32[4,24,256]{2,1,0:T(8,128)}), f32[4,24,256]{2,1,0:T(8,128)S(1)}, u32[]{:S(2)}, u32[]{:S(2)}) async-start(f32[4,24,256]{2,1,0:T(8,128)} %get-tuple-element.28), calls=%async_computation.2 | async-start | bytes 196608 | tf_op jit(solution)/shard_map/all_to_all | solution.py:255
  69.8 15.8 %collective-permute-start.4 = (f32[64,256]{1,0:T(8,128)S(1)}, f32[64,256]{1,0:T(8,128)S(1)}, u32[]{:S(2)}, u32[]{:S(2)}) collective-permute-start(f32[64,256]{1,0:T(8,128)S(1)} %maximum_select_fusion), channel_id=1, source_target_pairs={{1,33},{3,35},{5,37},{7,39},{9,41},{11,43},{13,45},{15,47},{17,49}... | collective-permute-start | bytes 196616 | tf_op jit(solution)/shard_map/ppermute | solution.py:279
  77.3 20.2 %all-to-all-start.3 = ((f32[4,24,256]{2,1,0:T(8,128)}), f32[4,24,256]{2,1,0:T(8,128)S(1)}, u32[]{:S(2)}, u32[]{:S(2)}) async-start(f32[4,24,256]{2,1,0:T(8,128)} %shard_map.150), calls=%async_computation.3 | async-start | bytes 196608 | tf_op jit(solution)/shard_map/all_to_all | solution.py:255
  85.7 5.6 %collective-permute-start.5 = (f32[32,256]{1,0:T(8,128)S(1)}, f32[32,256]{1,0:T(8,128)S(1)}, u32[]{:S(2)}, u32[]{:S(2)}) collective-permute-start(f32[32,256]{1,0:T(8,128)S(1)} %get-tuple-element.39), channel_id=1, source_target_pairs={{0,1},{1,0},{2,3},{3,2},{4,5},{5,4},{6,7},{7,6},{8,9},{9,8},{10,11... | collective-permute-start | bytes 98312 | tf_op jit(solution)/shard_map/ppermute | solution.py:261
  109.3 8.5 %collective-permute-start.6 = (bf16[16,24,256]{2,1,0:T(8,128)(2,1)S(1)}, bf16[16,24,256]{2,1,0:T(8,128)(2,1)S(1)}, u32[]{:S(2)}, u32[]{:S(2)}) collective-permute-start(bf16[16,24,256]{2,1,0:T(8,128)(2,1)S(1)} %all_to_all.25.own), channel_id=1, source_target_pairs={{0,1},{1,0},{2,3},{3,2},{4,5},{5,4},{6,7},{7,6},{8,9},{9,8},{10,11... | collective-permute-start | bytes 589832 | tf_op jit(solution)/shard_map/ppermute | solution.py:261

commit v6 on v5

--- a/solution.py
+++ b/solution.py
@@ -254,6 +254,18 @@
 def exchange(blocks, axis, bits):
     return lax.all_to_all(
         blocks, axis, 0, 0, tiled=True, axis_index_groups=groups(lax.axis_size(axis), bits)
+    )
+
+
+def crossed(blocks, bits):
+    rows, columns = lax.axis_size("row"), lax.axis_size("col")
+    found = {}
+    for row in range(rows):
+        for column in range(columns):
+            key = (row & ~sum(bits[column % 2]), column)
+            found.setdefault(key, []).append(row * columns + column)
+    return lax.all_to_all(
+        blocks, BOTH, 0, 0, tiled=True, axis_index_groups=list(found.values())
     )
 
 
@@ -333,9 +345,9 @@
     row_part, parts = call(
         row_kernel, (like(shard, width), like(spread, share, width)), parts, w_left
     )
-    parts = exchange(parts, "row", X_BITS)
+    parts = crossed(parts, (X_BITS, Z_BITS))
     parts = call(sum_kernel, like(spread, share, width), parts)
-    parts = exchange(parts, "row", Z_BITS)
+    parts = crossed(parts, (Z_BITS, X_BITS))
     grad_nodes, shares = call(
         node_kernel,
         (like(shard, width), jax.ShapeDtypeStruct((chips, share, width), BF16)),

time: 119 us -> 124 us (1.042)
  blocking collectives: 11 us -> 34.3 us
  waiting for transfers between devices: 27.6 us -> 12.5 us
  Pallas kernels: 13.8 us -> 10.1 us
    all_to_all x1 -> x2, blocking collectives: 11 us -> 34.3 us  [exchange(): lax.all_to_all(blocks, axis, 0, 0, tiled=True, axis_index_groups=groups(l...]
    all_to_all x4 -> x1, waiting for transfers between devices: 23.3 us -> 4.95 us  [exchange(): lax.all_to_all(blocks, axis, 0, 0, tiled=True, axis_index_groups=groups(l...]
    all_to_all x4 -> x1, starting transfers between devices: 28.4 us -> 10.4 us  [exchange(): lax.all_to_all(blocks, axis, 0, 0, tiled=True, axis_index_groups=groups(l...]
    all_to_all x0 -> x2, starting transfers between devices: none -> 14.7 us  [crossed(): lax.all_to_all(blocks, BOTH, 0, 0, tiled=True, axis_index_groups=list(fou...]
    ppermute x4, starting transfers between devices: 16.5 us -> 20.2 us  [swapped(): lax.ppermute(block, 'col', [(i, i ^ 1) for i in range(lax.axis_size('col'...]
    all_to_all x0 -> x2, waiting for transfers between devices: none -> 2.23 us  [crossed(): lax.all_to_all(blocks, BOTH, 0, 0, tiled=True, axis_index_groups=list(fou...]
    pallas_call x1, Pallas kernels: 5.91 us -> 3.72 us  [pair_sums(): pl.pallas_call(pair_kernel, out_shape=(chunks,) * 2 + (block,) * 3, in_sp...]
    pallas_call x1, Pallas kernels: 3.95 us -> 2.42 us  [row_pairs(): pl.pallas_call(row_pair_kernel, out_shape=(per_pair,) * 3 + (jax.ShapeDty...]
  transfers between devices with their start and end apart: 11 -> 10, of which waited for: 6 -> 7; matrix products, arithmetic and copies ran while one was open for 1% -> 1% of each run, Pallas kernels for 5% -> 2%
where the time goes in v6:
time: 124 us; the launch traced here: 123 us
  starting transfers between devices  62.5 us (50%)
  blocking collectives  34.3 us (28%)
  waiting for transfers between devices  12.5 us (10%)
  Pallas kernels  10.1 us (8%)
  local copies, waits for them, and re-layouts  2.11 us (2%)
  between operations  1.53 us (1%)
    all_to_all x2, blocking collectives, exchange(): lax.all_to_all(blocks, axis, 0, 0, tiled=True, axis_index_groups=groups(l...  34.3 us
    ppermute x4, starting transfers between devices, swapped(): lax.ppermute(block, 'col', [(i, i ^ 1) for i in range(lax.axis_size('col'...  20.2 us
    all_to_all x2, starting transfers between devices, crossed(): lax.all_to_all(blocks, BOTH, 0, 0, tiled=True, axis_index_groups=list(fou...  14.7 us
    all_to_all x1, starting transfers between devices, exchange(): lax.all_to_all(blocks, axis, 0, 0, tiled=True, axis_index_groups=groups(l...  10.4 us
    ppermute x2, starting transfers between devices, shifted(): lax.ppermute(block, 'row', [(i, i + distance) for i in devices if i + dis...  9.88 us
    ppermute x1, starting transfers between devices, neighbours(): return lax.ppermute(block, BOTH, route)  7.28 us
    ppermute x4, waiting for transfers between devices, swapped(): lax.ppermute(block, 'col', [(i, i ^ 1) for i in range(lax.axis_size('col'...  5.36 us
    all_to_all x1, waiting for transfers between devices, exchange(): lax.all_to_all(blocks, axis, 0, 0, tiled=True, axis_index_groups=groups(l...  4.95 us
  transfers between devices with their start and end apart: 10, of which 7 were waited for; matrix products, arithmetic and copies ran while one was open for 1% of the time, Pallas kernels for 2%

profile of v6, /device:TPU:1, one launch (start us, length us, event | category | flops | bytes accessed | tf_op | source)
XLA Modules:
  0.0 123.3 jit_solution(5486501990209083861)
XLA Ops:
  1.4 0.9 shard_map.146
  2.3 10.4 %all-to-all-start = ((bf16[32,32,256]{2,1,0:T(8,128)(2,1)}), bf16[32,32,256]{2,1,0:T(8,128)(2,1)S(1)}, u32[]{:S(2)}, u32[]{:S(2)}) async-start(bf16[32,32,256]{2,1,0:T(8,128)(2,1)} %shard_map.146), calls=%async_computation | async-start | bytes 1048576 | tf_op jit(solution)/shard_map/all_to_all | solution.py:255
  12.7 8.6 %collective-permute-start = (bf16[32,256]{1,0:T(8,128)(2,1)}, bf16[32,256]{1,0:T(8,128)(2,1)S(1)}, u32[]{:S(2)}, u32[]{:S(2)}) collective-permute-start(bf16[32,256]{1,0:T(8,128)(2,1)} %nodes.1), channel_id=1, source_target_pairs={{0,32},{32,64},{64,96},{96,128},{128,160},{160,192},{192,224},{224... | collective-permute-start | bytes 49160 | tf_op jit(solution)/shard_map/ppermute | solution.py:278
  21.3 1.3 %collective-permute-start.1 = (bf16[32,256]{1,0:T(8,128)(2,1)}, bf16[32,256]{1,0:T(8,128)(2,1)S(1)}, u32[]{:S(2)}, u32[]{:S(2)}) collective-permute-start(bf16[32,256]{1,0:T(8,128)(2,1)} %nodes.1), channel_id=1, source_target_pairs={{32,0},{64,32},{96,64},{128,96},{160,128},{192,160},{224,192},{256... | collective-permute-start | bytes 49160 | tf_op jit(solution)/shard_map/ppermute | solution.py:278
  23.3 1.3 %copy.20 = bf16[1,16,169,128]{3,2,1,0:T(8,128)(2,1)S(1)} copy(bf16[1,16,169,128]{3,1,2,0:T(8,128)(2,1)} %param.13) | data formatting | bytes 1384448 | tf_op args[2]
  24.7 4.9 %all-to-all-done = bf16[32,32,256]{2,1,0:T(8,128)(2,1)S(1)} async-done(((bf16[32,32,256]{2,1,0:T(8,128)(2,1)}), bf16[32,32,256]{2,1,0:T(8,128)(2,1)S(1)}, u32[]{:S(2)}, u32[]{:S(2)}) %all-to-all-start) | async-done | bytes 524320 | tf_op jit(solution)/shard_map/all_to_all | solution.py:255
  29.7 2.4 %shard_map.147 = (f32[2,256,1024]{2,1,0:T(8,128)S(1)}, f32[2,256,1024]{2,1,0:T(8,128)S(1)}, f32[2,256,1024]{2,1,0:T(8,128)S(1)}, bf16[32,256]{1,0:T(8,128)(2,1)S(1)}) custom-call(s32[3]{0:T(128)S(1)} %pad_add_fusion.places, s32[16,128]{1,0:T(8,128)S(1)} %bitcast.20, s32[16,128]{1,0:T(8,128)S(1)} %bitcast.23, bf16[16,25,128]{2,1,0:T(8,128)(2,1)S(1)} %bitcast.18, ...), custom_call_target="tpu_custom_call" | custom-call | flops 2350907392 | bytes 8388608 | tf_op jit(solution)/shard_map/pallas_call | solution.py:137
  32.2 3.7 %shard_map.148 = (f32[16,56,256]{2,1,0:T(8,128)S(1)}, f32[16,56,256]{2,1,0:T(8,128)S(1)}, f32[32,256]{1,0:T(8,128)S(1)}, f32[32,256]{1,0:T(8,128)S(1)}, f32[32,256]{1,0:T(8,128)S(1)}) custom-call(s32[3]{0:T(128)S(1)} %pad_add_fusion.places, s32[16,128]{1,0:T(8,128)S(1)} %bitcast.21, s32[16,128]{1,0:T(8,128)S(1)} %bitcast.22, s32[16,128]{1,0:T(8,128)S(1)} %bitcast.24, ...), custom_call_target="tpu_custom_call" | custom-call | tf_op jit(solution)/shard_map/pallas_call | solution.py:158
  35.9 2.1 %collective-permute-start.2 = (f32[16,56,256]{2,1,0:T(8,128)S(1)}, f32[16,56,256]{2,1,0:T(8,128)S(1)}, u32[]{:S(2)}, u32[]{:S(2)}) collective-permute-start(f32[16,56,256]{2,1,0:T(8,128)S(1)} %get-tuple-element.27), channel_id=1, source_target_pairs={{0,1},{1,0},{2,3},{3,2},{4,5},{5,4},{6,7},{7,6},{8,9},{9,8},{10,11... | collective-permute-start | bytes 2752520 | tf_op jit(solution)/shard_map/ppermute | solution.py:273
  38.0 2.3 %collective-permute-done.2 = f32[16,56,256]{2,1,0:T(8,128)S(1)} collective-permute-done((f32[16,56,256]{2,1,0:T(8,128)S(1)}, f32[16,56,256]{2,1,0:T(8,128)S(1)}, u32[]{:S(2)}, u32[]{:S(2)}) %collective-permute-start.2) | collective-permute-done | bytes 917536 | tf_op jit(solution)/shard_map/ppermute | solution.py:273
  40.4 23.1 %all_to_all.25.parts = bf16[16,56,256]{2,1,0:T(8,128)(2,1)S(1)} all-to-all(bf16[16,56,256]{2,1,0:T(8,128)(2,1)S(1)} %add_convert_fusion), channel_id=1, replica_groups={{0,2,4,6,8,10,12,14,16,18,20,22,24,26,28,30},{1,3,5,7,9,11,13,15,17,19,..., dimensions={0} | all-to-all | bytes 917504 | tf_op jit(solution)/shard_map/all_to_all | solution.py:255
  64.3 10.3 %all-to-all-start.2 = ((f32[4,24,256]{2,1,0:T(8,128)}), f32[4,24,256]{2,1,0:T(8,128)S(1)}, u32[]{:S(2)}, u32[]{:S(2)}) async-start(f32[4,24,256]{2,1,0:T(8,128)} %get-tuple-element.28), calls=%async_computation.2 | async-start | bytes 196608 | tf_op jit(solution)/shard_map/all_to_all | solution.py:267
  74.6 1.9 %collective-permute-start.3 = (f32[32,256]{1,0:T(8,128)S(1)}, f32[32,256]{1,0:T(8,128)S(1)}, u32[]{:S(2)}, u32[]{:S(2)}) collective-permute-start(f32[32,256]{1,0:T(8,128)S(1)} %get-tuple-element.31), channel_id=1, source_target_pairs={{0,1},{1,0},{2,3},{3,2},{4,5},{5,4},{6,7},{7,6},{8,9},{9,8},{10,11... | collective-permute-start | bytes 98312 | tf_op jit(solution)/shard_map/ppermute | solution.py:273
  76.5 1.2 collective-permute-done.3
  77.7 7.3 %collective-permute-start.4 = (f32[64,256]{1,0:T(8,128)S(1)}, f32[64,256]{1,0:T(8,128)S(1)}, u32[]{:S(2)}, u32[]{:S(2)}) collective-permute-start(f32[64,256]{1,0:T(8,128)S(1)} %maximum_select_fusion), channel_id=1, source_target_pairs={{1,33},{3,35},{5,37},{7,39},{9,41},{11,43},{13,45},{15,47},{17,49}... | collective-permute-start | bytes 196616 | tf_op jit(solution)/shard_map/ppermute | solution.py:291
  85.0 1.5 %all-to-all-done.2.parts = f32[4,24,256]{2,1,0:T(8,128)S(1)} async-done(((f32[4,24,256]{2,1,0:T(8,128)}), f32[4,24,256]{2,1,0:T(8,128)S(1)}, u32[]{:S(2)}, u32[]{:S(2)}) %all-to-all-start.2) | async-done | bytes 98336 | tf_op jit(solution)/shard_map/all_to_all | solution.py:267
  87.1 4.4 %all-to-all-start.3 = ((f32[4,24,256]{2,1,0:T(8,128)}), f32[4,24,256]{2,1,0:T(8,128)S(1)}, u32[]{:S(2)}, u32[]{:S(2)}) async-start(f32[4,24,256]{2,1,0:T(8,128)} %shard_map.150), calls=%async_computation.3 | async-start | bytes 196608 | tf_op jit(solution)/shard_map/all_to_all | solution.py:267
  91.6 3.1 %collective-permute-start.5 = (f32[32,256]{1,0:T(8,128)S(1)}, f32[32,256]{1,0:T(8,128)S(1)}, u32[]{:S(2)}, u32[]{:S(2)}) collective-permute-start(f32[32,256]{1,0:T(8,128)S(1)} %get-tuple-element.39), channel_id=1, source_target_pairs={{0,1},{1,0},{2,3},{3,2},{4,5},{5,4},{6,7},{7,6},{8,9},{9,8},{10,11... | collective-permute-start | bytes 98312 | tf_op jit(solution)/shard_map/ppermute | solution.py:273
  94.6 0.8 collective-permute-done.5.there
  96.2 0.8 shard_map.151
  97.0 11.2 %all_to_all.26.own = bf16[16,24,256]{2,1,0:T(8,128)(2,1)S(1)} all-to-all(bf16[16,24,256]{2,1,0:T(8,128)(2,1)S(1)} %get-tuple-element.34), channel_id=1, replica_groups={{0,2,4,6,8,10,12,14,16,18,20,22,24,26,28,30},{1,3,5,7,9,11,13,15,17,19,..., dimensions={0} | all-to-all | bytes 393216 | tf_op jit(solution)/shard_map/all_to_all | solution.py:255
  108.2 13.2 %collective-permute-start.6 = (bf16[16,24,256]{2,1,0:T(8,128)(2,1)S(1)}, bf16[16,24,256]{2,1,0:T(8,128)(2,1)S(1)}, u32[]{:S(2)}, u32[]{:S(2)}) collective-permute-start(bf16[16,24,256]{2,1,0:T(8,128)(2,1)S(1)} %all_to_all.26.own), channel_id=1, source_target_pairs={{0,1},{1,0},{2,3},{3,2},{4,5},{5,4},{6,7},{7,6},{8,9},{9,8},{10,11... | collective-permute-start | bytes 589832 | tf_op jit(solution)/shard_map/ppermute | solution.py:273
  121.4 1.0 collective-permute-done.6.other
  122.4 0.9 shard_map.152
  (32 shorter events, 3.2 us)
Async XLA Ops:
  0.6 29.0 %copy-start.1 = (bf16[256,256]{1,0:T(8,128)(2,1)S(1)}, bf16[256,256]{1,0:T(8,128)(2,1)}, u32[]{:S(2)}) copy-start(bf16[256,256]{1,0:T(8,128)(2,1)} %w_left.3) | copy-start | bytes 393220
  0.6 0.8 copy-start.2
  1.4 23.1 %copy-start.9 = (bf16[1,16,25,128]{3,1,2,0:T(8,128)(2,1)S(1)}, bf16[1,16,25,128]{3,1,2,0:T(8,128)(2,1)}, u32[]{:S(2)}) copy-start(bf16[1,16,25,128]{3,1,2,0:T(8,128)(2,1)} %param.12) | copy-start | bytes 307204
  1.4 28.2 %copy-start.3 = (bf16[32,256]{1,0:T(8,128)(2,1)S(1)}, bf16[32,256]{1,0:T(8,128)(2,1)}, u32[]{:S(2)}) copy-start(bf16[32,256]{1,0:T(8,128)(2,1)} %nodes.1) | copy-start | bytes 49156
  1.4 28.2 %copy-start.4 = (s32[1,16,128]{2,1,0:T(8,128)S(1)}, s32[1,16,128]{2,1,0:T(8,128)}, u32[]{:S(2)}) copy-start(s32[1,16,128]{2,1,0:T(8,128)} %param.14) | copy-start | bytes 24580
  1.4 28.2 %copy-start.6 = (s32[1,16,128]{2,1,0:T(8,128)S(1)}, s32[1,16,128]{2,1,0:T(8,128)}, u32[]{:S(2)}) copy-start(s32[1,16,128]{2,1,0:T(8,128)} %param.16) | copy-start | bytes 24580
  1.4 28.2 %copy-start.7 = (bf16[169,256]{1,0:T(8,128)(2,1)S(1)}, bf16[169,256]{1,0:T(8,128)(2,1)}, u32[]{:S(2)}) copy-start(bf16[169,256]{1,0:T(8,128)(2,1)} %w_out.1) | copy-start | bytes 259588
  1.4 28.2 %copy-start.8 = (bf16[25,256]{1,0:T(8,128)(2,1)S(1)}, bf16[25,256]{1,0:T(8,128)(2,1)}, u32[]{:S(2)}) copy-start(bf16[25,256]{1,0:T(8,128)(2,1)} %w_harm.1) | copy-start | bytes 38404
  2.3 27.3 %all-to-all-start = ((bf16[32,32,256]{2,1,0:T(8,128)(2,1)}), bf16[32,32,256]{2,1,0:T(8,128)(2,1)S(1)}, u32[]{:S(2)}, u32[]{:S(2)}) async-start(bf16[32,32,256]{2,1,0:T(8,128)(2,1)} %shard_map.146), calls=%async_computation | async-start | bytes 1048576 | tf_op jit(solution)/shard_map/all_to_all | solution.py:255
  12.7 19.4 %collective-permute-start = (bf16[32,256]{1,0:T(8,128)(2,1)}, bf16[32,256]{1,0:T(8,128)(2,1)S(1)}, u32[]{:S(2)}, u32[]{:S(2)}) collective-permute-start(bf16[32,256]{1,0:T(8,128)(2,1)} %nodes.1), channel_id=1, source_target_pairs={{0,32},{32,64},{64,96},{96,128},{128,160},{160,192},{192,224},{224... | collective-permute-start | bytes 49160 | tf_op jit(solution)/shard_map/ppermute | solution.py:278
  21.3 10.8 %collective-permute-start.1 = (bf16[32,256]{1,0:T(8,128)(2,1)}, bf16[32,256]{1,0:T(8,128)(2,1)S(1)}, u32[]{:S(2)}, u32[]{:S(2)}) collective-permute-start(bf16[32,256]{1,0:T(8,128)(2,1)} %nodes.1), channel_id=1, source_target_pairs={{32,0},{64,32},{96,64},{128,96},{160,128},{192,160},{224,192},{256... | collective-permute-start | bytes 49160 | tf_op jit(solution)/shard_map/ppermute | solution.py:278
  29.7 2.5 %copy-start = (bf16[256,256]{1,0:T(8,128)(2,1)S(1)}, bf16[256,256]{1,0:T(8,128)(2,1)}, u32[]{:S(2)}) copy-start(bf16[256,256]{1,0:T(8,128)(2,1)} %w_right.3) | copy-start | bytes 393220
  29.7 2.5 %copy-start.5 = (s32[1,16,128]{2,1,0:T(8,128)S(1)}, s32[1,16,128]{2,1,0:T(8,128)}, u32[]{:S(2)}) copy-start(s32[1,16,128]{2,1,0:T(8,128)} %param.15) | copy-start | bytes 24580
  35.9 4.4 %collective-permute-start.2 = (f32[16,56,256]{2,1,0:T(8,128)S(1)}, f32[16,56,256]{2,1,0:T(8,128)S(1)}, u32[]{:S(2)}, u32[]{:S(2)}) collective-permute-start(f32[16,56,256]{2,1,0:T(8,128)S(1)} %get-tuple-element.27), channel_id=1, source_target_pairs={{0,1},{1,0},{2,3},{3,2},{4,5},{5,4},{6,7},{7,6},{8,9},{9,8},{10,11... | collective-permute-start | bytes 2752520 | tf_op jit(solution)/shard_map/ppermute | solution.py:273
  64.3 22.2 %all-to-all-start.2 = ((f32[4,24,256]{2,1,0:T(8,128)}), f32[4,24,256]{2,1,0:T(8,128)S(1)}, u32[]{:S(2)}, u32[]{:S(2)}) async-start(f32[4,24,256]{2,1,0:T(8,128)} %get-tuple-element.28), calls=%async_computation.2 | async-start | bytes 196608 | tf_op jit(solution)/shard_map/all_to_all | solution.py:267
  74.6 3.1 %collective-permute-start.3 = (f32[32,256]{1,0:T(8,128)S(1)}, f32[32,256]{1,0:T(8,128)S(1)}, u32[]{:S(2)}, u32[]{:S(2)}) collective-permute-start(f32[32,256]{1,0:T(8,128)S(1)} %get-tuple-element.31), channel_id=1, source_target_pairs={{0,1},{1,0},{2,3},{3,2},{4,5},{5,4},{6,7},{7,6},{8,9},{9,8},{10,11... | collective-permute-start | bytes 98312 | tf_op jit(solution)/shard_map/ppermute | solution.py:273
  77.7 13.9 %collective-permute-start.4 = (f32[64,256]{1,0:T(8,128)S(1)}, f32[64,256]{1,0:T(8,128)S(1)}, u32[]{:S(2)}, u32[]{:S(2)}) collective-permute-start(f32[64,256]{1,0:T(8,128)S(1)} %maximum_select_fusion), channel_id=1, source_target_pairs={{1,33},{3,35},{5,37},{7,39},{9,41},{11,43},{13,45},{15,47},{17,49}... | collective-permute-start | bytes 196616 | tf_op jit(solution)/shard_map/ppermute | solution.py:291
  87.1 9.1 %all-to-all-start.3 = ((f32[4,24,256]{2,1,0:T(8,128)}), f32[4,24,256]{2,1,0:T(8,128)S(1)}, u32[]{:S(2)}, u32[]{:S(2)}) async-start(f32[4,24,256]{2,1,0:T(8,128)} %shard_map.150), calls=%async_computation.3 | async-start | bytes 196608 | tf_op jit(solution)/shard_map/all_to_all | solution.py:267
  91.6 3.9 %collective-permute-start.5 = (f32[32,256]{1,0:T(8,128)S(1)}, f32[32,256]{1,0:T(8,128)S(1)}, u32[]{:S(2)}, u32[]{:S(2)}) collective-permute-start(f32[32,256]{1,0:T(8,128)S(1)} %get-tuple-element.39), channel_id=1, source_target_pairs={{0,1},{1,0},{2,3},{3,2},{4,5},{5,4},{6,7},{7,6},{8,9},{9,8},{10,11... | collective-permute-start | bytes 98312 | tf_op jit(solution)/shard_map/ppermute | solution.py:273
  108.2 14.2 %collective-permute-start.6 = (bf16[16,24,256]{2,1,0:T(8,128)(2,1)S(1)}, bf16[16,24,256]{2,1,0:T(8,128)(2,1)S(1)}, u32[]{:S(2)}, u32[]{:S(2)}) collective-permute-start(bf16[16,24,256]{2,1,0:T(8,128)(2,1)S(1)} %all_to_all.26.own), channel_id=1, source_target_pairs={{0,1},{1,0},{2,3},{3,2},{4,5},{5,4},{6,7},{7,6},{8,9},{9,8},{10,11... | collective-permute-start | bytes 589832 | tf_op jit(solution)/shard_map/ppermute | solution.py:273

commit v7 on v5

--- a/solution.py
+++ b/solution.py
@@ -182,33 +182,40 @@
     return dot(high, weight[...], 1, 1) + dot(low, weight[...], 1, 1)
 
 
-def row_kernel(parts, w_left, row_part, out):
-    shard = row_part.shape[0]
+def row_kernel(core, parts, ahead, passed, row_sums, out, both):
+    shard = row_sums.shape[0]
     total = total_of(parts)
-    row_part[...] = weighted(total[:shard], w_left)
+    row_sums[...] = total[:shard]
     for to in range(out.shape[0]):
         out[to] = total[shard:]
-
-
-def sum_kernel(parts, out):
+    first = core[0] == 0
+    both[:shard] = jnp.where(first, ahead[...], passed[...])
+    both[shard:] = jnp.where(first, passed[...], ahead[...])
+
+
+def middle_kernel(parts, out):
     total = total_of(parts)
     for to in range(out.shape[0]):
         out[to] = total
 
 
-def node_kernel(parts, middle, here, there, row_part, w_right, grad_nodes, shares):
-    columns = middle[...] + here[...] + there[...]
-    grad_nodes[...] = row_part[...] + weighted(columns, w_right)
-    total = total_of(parts).astype(shares.dtype)
-    for chip in range(shares.shape[0]):
-        shares[chip] = total
-
-
-def call(kernel, out_shape, *operands):
+def last_kernel(parts, middle, here, there, out, column_sums):
+    total = total_of(parts).astype(out.dtype)
+    for to in range(out.shape[0]):
+        out[to] = total
+    column_sums[...] = middle[...] + here[...] + there[...]
+
+
+def node_kernel(row_sums, column_sums, w_left, w_right, grad_nodes):
+    grad_nodes[...] = weighted(row_sums[...], w_left) + weighted(column_sums[...], w_right)
+
+
+def call(kernel, out_shape, *operands, scalars=0):
+    specs = [SMEM] * scalars + [VMEM] * (len(operands) - scalars)
     return pl.pallas_call(
         kernel,
         out_shape=out_shape,
-        in_specs=[VMEM] * len(operands),
+        in_specs=specs,
         out_specs=jax.tree.map(lambda _: VMEM, out_shape),
         compiler_params=PARAMS,
     )(*operands)
@@ -324,26 +331,27 @@
     parts = (keep + swapped(send)).astype(BF16)
     parts = exchange(parts, "col", CHIP_BITS)
     passed = swapped(passed)
-    both = jnp.where(
-        core == 0, jnp.concatenate([ahead, passed]), jnp.concatenate([passed, ahead])
-    )
+    block, chunks = like(shard, width), like(spread, share, width)
+    core = core.reshape(1)
+    row_sums, parts, both = call(
+        row_kernel, (block, chunks, like(2 * shard, width)), core, parts, ahead, passed, scalars=1
+    )
+    parts = exchange(parts, "row", X_BITS)
     both = neighbours(both)
-    here = jnp.where(core == 0, both[:shard], both[shard:])
-    there = swapped(jnp.where(core == 0, both[shard:], both[:shard]))
-    row_part, parts = call(
-        row_kernel, (like(shard, width), like(spread, share, width)), parts, w_left
-    )
-    parts = exchange(parts, "row", X_BITS)
-    parts = call(sum_kernel, like(spread, share, width), parts)
+    parts = call(middle_kernel, chunks, parts)
     parts = exchange(parts, "row", Z_BITS)
-    grad_nodes, shares = call(
-        node_kernel,
-        (like(shard, width), jax.ShapeDtypeStruct((chips, share, width), BF16)),
-        parts, middle, here, there, row_part, w_right,
-    )
+    first = core[0] == 0
+    here = jnp.where(first, both[:shard], both[shard:])
+    there = swapped(jnp.where(first, both[shard:], both[:shard]))
+    shares, column_sums = call(
+        last_kernel,
+        (jax.ShapeDtypeStruct((chips, share, width), BF16), block),
+        parts, middle, here, there,
+    )
+    grad_nodes = call(node_kernel, block, row_sums, column_sums, w_left, w_right)
     own_shares = exchange(shares, "col", CHIP_BITS)
     left, right, harm, out = split(
-        core.reshape(1), own_shares, swapped(own_shares), w_harm.shape[0], w_out.shape[0]
+        core, own_shares, swapped(own_shares), w_harm.shape[0], w_out.shape[0]
     )
     return (grad_nodes, left, right, harm, out)
 

time: 119 us -> 119 us (level)
  starting transfers between devices: 61.6 us -> 65.8 us
  Pallas kernels: 13.8 us -> 10.2 us
  waiting for transfers between devices: 27.6 us -> 26.2 us
    all_to_all x4, starting transfers between devices: 28.4 us -> 32.5 us  [exchange(): lax.all_to_all(blocks, axis, 0, 0, tiled=True, axis_index_groups=groups(l...]
    pallas_call x1, Pallas kernels: 5.91 us -> 3.72 us  [pair_sums(): pl.pallas_call(pair_kernel, out_shape=(chunks,) * 2 + (block,) * 3, in_sp...]
    pallas_call x1, Pallas kernels: 3.95 us -> 2.42 us  [row_pairs(): pl.pallas_call(row_pair_kernel, out_shape=(per_pair,) * 3 + (jax.ShapeDty...]
    all_to_all x4, waiting for transfers between devices: 23.3 us -> 22.1 us  [exchange(): lax.all_to_all(blocks, axis, 0, 0, tiled=True, axis_index_groups=groups(l...]
    pallas_call x4 -> x5, Pallas kernels: 3.07 us -> 3.1 us  [call(): pl.pallas_call(kernel, out_shape=out_shape, in_specs=specs, out_specs=jax...]
  transfers between devices with their start and end apart: 11 -> 11, of which waited for: 6 -> 7; matrix products, arithmetic and copies ran while one was open for 1% -> 1% of each run, Pallas kernels for 5% -> 3%
where the time goes in v7:
time: 119 us; the launch traced here: 118 us
  starting transfers between devices  65.8 us (55%)
  waiting for transfers between devices  26.2 us (22%)
  blocking collectives  11 us (9%)
  Pallas kernels  10.2 us (9%)
  local copies, waits for them, and re-layouts  2.11 us (2%)
  between operations  1.54 us (1%)
    all_to_all x4, starting transfers between devices, exchange(): lax.all_to_all(blocks, axis, 0, 0, tiled=True, axis_index_groups=groups(l...  32.5 us
    all_to_all x4, waiting for transfers between devices, exchange(): lax.all_to_all(blocks, axis, 0, 0, tiled=True, axis_index_groups=groups(l...  22.1 us
    ppermute x4, starting transfers between devices, swapped(): lax.ppermute(block, 'col', [(i, i ^ 1) for i in range(lax.axis_size('col'...  16.8 us
    all_to_all x1, blocking collectives, exchange(): lax.all_to_all(blocks, axis, 0, 0, tiled=True, axis_index_groups=groups(l...  11 us
    ppermute x2, starting transfers between devices, shifted(): lax.ppermute(block, 'row', [(i, i + distance) for i in devices if i + dis...  9.88 us
    ppermute x1, starting transfers between devices, neighbours(): return lax.ppermute(block, BOTH, route)  6.6 us
    ppermute x4, waiting for transfers between devices, swapped(): lax.ppermute(block, 'col', [(i, i ^ 1) for i in range(lax.axis_size('col'...  4.15 us
    pallas_call x1, Pallas kernels, pair_sums(): pl.pallas_call(pair_kernel, out_shape=(chunks,) * 2 + (block,) * 3, in_sp...  3.72 us
  transfers between devices with their start and end apart: 11, of which 7 were waited for; matrix products, arithmetic and copies ran while one was open for 1% of the time, Pallas kernels for 3%

profile of v7, /device:TPU:1, one launch (start us, length us, event | category | flops | bytes accessed | tf_op | source)
XLA Modules:
  0.0 117.8 jit_solution(10280481473689518925)
XLA Ops:
  1.4 0.9 shard_map.146
  2.3 10.4 %all-to-all-start = ((bf16[32,32,256]{2,1,0:T(8,128)(2,1)}), bf16[32,32,256]{2,1,0:T(8,128)(2,1)S(1)}, u32[]{:S(2)}, u32[]{:S(2)}) async-start(bf16[32,32,256]{2,1,0:T(8,128)(2,1)} %shard_map.146), calls=%async_computation | async-start | bytes 1048576 | tf_op jit(solution)/shard_map/all_to_all | solution.py:262
  12.7 8.6 %collective-permute-start = (bf16[32,256]{1,0:T(8,128)(2,1)}, bf16[32,256]{1,0:T(8,128)(2,1)S(1)}, u32[]{:S(2)}, u32[]{:S(2)}) collective-permute-start(bf16[32,256]{1,0:T(8,128)(2,1)} %nodes.1), channel_id=1, source_target_pairs={{0,32},{32,64},{64,96},{96,128},{128,160},{160,192},{192,224},{224... | collective-permute-start | bytes 49160 | tf_op jit(solution)/shard_map/ppermute | solution.py:273
  21.3 1.3 %collective-permute-start.1 = (bf16[32,256]{1,0:T(8,128)(2,1)}, bf16[32,256]{1,0:T(8,128)(2,1)S(1)}, u32[]{:S(2)}, u32[]{:S(2)}) collective-permute-start(bf16[32,256]{1,0:T(8,128)(2,1)} %nodes.1), channel_id=1, source_target_pairs={{32,0},{64,32},{96,64},{128,96},{160,128},{192,160},{224,192},{256... | collective-permute-start | bytes 49160 | tf_op jit(solution)/shard_map/ppermute | solution.py:273
  23.3 1.3 %copy.20 = bf16[1,16,169,128]{3,2,1,0:T(8,128)(2,1)S(1)} copy(bf16[1,16,169,128]{3,1,2,0:T(8,128)(2,1)} %param.13) | data formatting | bytes 1384448 | tf_op args[2]
  24.7 4.9 %all-to-all-done = bf16[32,32,256]{2,1,0:T(8,128)(2,1)S(1)} async-done(((bf16[32,32,256]{2,1,0:T(8,128)(2,1)}), bf16[32,32,256]{2,1,0:T(8,128)(2,1)S(1)}, u32[]{:S(2)}, u32[]{:S(2)}) %all-to-all-start) | async-done | bytes 524320 | tf_op jit(solution)/shard_map/all_to_all | solution.py:262
  29.7 2.4 %shard_map.147 = (f32[2,256,1024]{2,1,0:T(8,128)S(1)}, f32[2,256,1024]{2,1,0:T(8,128)S(1)}, f32[2,256,1024]{2,1,0:T(8,128)S(1)}, bf16[32,256]{1,0:T(8,128)(2,1)S(1)}) custom-call(s32[3]{0:T(128)S(1)} %pad_add_fusion.places, s32[16,128]{1,0:T(8,128)S(1)} %bitcast.20, s32[16,128]{1,0:T(8,128)S(1)} %bitcast.23, bf16[16,25,128]{2,1,0:T(8,128)(2,1)S(1)} %bitcast.18, ...), custom_call_target="tpu_custom_call" | custom-call | flops 2350907392 | bytes 8388608 | tf_op jit(solution)/shard_map/pallas_call | solution.py:137
  32.2 3.7 %shard_map.148 = (f32[16,56,256]{2,1,0:T(8,128)S(1)}, f32[16,56,256]{2,1,0:T(8,128)S(1)}, f32[32,256]{1,0:T(8,128)S(1)}, f32[32,256]{1,0:T(8,128)S(1)}, f32[32,256]{1,0:T(8,128)S(1)}) custom-call(s32[3]{0:T(128)S(1)} %pad_add_fusion.places, s32[16,128]{1,0:T(8,128)S(1)} %bitcast.21, s32[16,128]{1,0:T(8,128)S(1)} %bitcast.22, s32[16,128]{1,0:T(8,128)S(1)} %bitcast.24, ...), custom_call_target="tpu_custom_call" | custom-call | tf_op jit(solution)/shard_map/pallas_call | solution.py:158
  35.9 2.1 %collective-permute-start.2 = (f32[16,56,256]{2,1,0:T(8,128)S(1)}, f32[16,56,256]{2,1,0:T(8,128)S(1)}, u32[]{:S(2)}, u32[]{:S(2)}) collective-permute-start(f32[16,56,256]{2,1,0:T(8,128)S(1)} %get-tuple-element.28), channel_id=1, source_target_pairs={{0,1},{1,0},{2,3},{3,2},{4,5},{5,4},{6,7},{7,6},{8,9},{9,8},{10,11... | collective-permute-start | bytes 2752520 | tf_op jit(solution)/shard_map/ppermute | solution.py:268
  38.0 2.3 %collective-permute-done.2 = f32[16,56,256]{2,1,0:T(8,128)S(1)} collective-permute-done((f32[16,56,256]{2,1,0:T(8,128)S(1)}, f32[16,56,256]{2,1,0:T(8,128)S(1)}, u32[]{:S(2)}, u32[]{:S(2)}) %collective-permute-start.2) | collective-permute-done | bytes 917536 | tf_op jit(solution)/shard_map/ppermute | solution.py:268
  40.3 0.9 add_convert_fusion
  41.1 9.0 %all-to-all-start.1 = ((bf16[16,56,256]{2,1,0:T(8,128)(2,1)}), bf16[16,56,256]{2,1,0:T(8,128)(2,1)S(1)}, u32[]{:S(2)}, u32[]{:S(2)}) async-start(bf16[16,56,256]{2,1,0:T(8,128)(2,1)} %add_convert_fusion), calls=%async_computation.1 | async-start | bytes 917504 | tf_op jit(solution)/shard_map/all_to_all | solution.py:262
  50.1 2.6 %collective-permute-start.3 = (f32[32,256]{1,0:T(8,128)S(1)}, f32[32,256]{1,0:T(8,128)S(1)}, u32[]{:S(2)}, u32[]{:S(2)}) collective-permute-start(f32[32,256]{1,0:T(8,128)S(1)} %get-tuple-element.30), channel_id=1, source_target_pairs={{0,1},{1,0},{2,3},{3,2},{4,5},{5,4},{6,7},{7,6},{8,9},{9,8},{10,11... | collective-permute-start | bytes 98312 | tf_op jit(solution)/shard_map/ppermute | solution.py:268
  52.7 0.8 collective-permute-done.3.passed
  53.5 10.9 %all-to-all-done.1.parts = bf16[16,56,256]{2,1,0:T(8,128)(2,1)S(1)} async-done(((bf16[16,56,256]{2,1,0:T(8,128)(2,1)}), bf16[16,56,256]{2,1,0:T(8,128)(2,1)S(1)}, u32[]{:S(2)}, u32[]{:S(2)}) %all-to-all-start.1) | async-done | bytes 458784 | tf_op jit(solution)/shard_map/all_to_all | solution.py:262
  65.2 4.6 %all-to-all-start.2 = ((f32[4,24,256]{2,1,0:T(8,128)}), f32[4,24,256]{2,1,0:T(8,128)S(1)}, u32[]{:S(2)}, u32[]{:S(2)}) async-start(f32[4,24,256]{2,1,0:T(8,128)} %get-tuple-element.32), calls=%async_computation.2 | async-start | bytes 196608 | tf_op jit(solution)/shard_map/all_to_all | solution.py:262
  69.7 6.6 %collective-permute-start.4 = (f32[64,256]{1,0:T(8,128)S(1)}, f32[64,256]{1,0:T(8,128)S(1)}, u32[]{:S(2)}, u32[]{:S(2)}) collective-permute-start(f32[64,256]{1,0:T(8,128)S(1)} %get-tuple-element.34), channel_id=1, source_target_pairs={{1,33},{3,35},{5,37},{7,39},{9,41},{11,43},{13,45},{15,47},{17,49}... | collective-permute-start | bytes 196616 | tf_op jit(solution)/shard_map/ppermute | solution.py:286
  77.0 8.6 %all-to-all-start.3 = ((f32[4,24,256]{2,1,0:T(8,128)}), f32[4,24,256]{2,1,0:T(8,128)S(1)}, u32[]{:S(2)}, u32[]{:S(2)}) async-start(f32[4,24,256]{2,1,0:T(8,128)} %shard_map.150), calls=%async_computation.3 | async-start | bytes 196608 | tf_op jit(solution)/shard_map/all_to_all | solution.py:262
  85.6 4.8 %collective-permute-start.5 = (f32[32,256]{1,0:T(8,128)S(1)}, f32[32,256]{1,0:T(8,128)S(1)}, u32[]{:S(2)}, u32[]{:S(2)}) collective-permute-start(f32[32,256]{1,0:T(8,128)S(1)} %get-tuple-element.41), channel_id=1, source_target_pairs={{0,1},{1,0},{2,3},{3,2},{4,5},{5,4},{6,7},{7,6},{8,9},{9,8},{10,11... | collective-permute-start | bytes 98312 | tf_op jit(solution)/shard_map/ppermute | solution.py:268
  91.2 6.2 %all-to-all-done.3.parts = f32[4,24,256]{2,1,0:T(8,128)S(1)} async-done(((f32[4,24,256]{2,1,0:T(8,128)}), f32[4,24,256]{2,1,0:T(8,128)S(1)}, u32[]{:S(2)}, u32[]{:S(2)}) %all-to-all-start.3) | async-done | bytes 98336 | tf_op jit(solution)/shard_map/all_to_all | solution.py:262
  97.4 11.0 %all_to_all.25.own = bf16[16,24,256]{2,1,0:T(8,128)(2,1)S(1)} all-to-all(bf16[16,24,256]{2,1,0:T(8,128)(2,1)S(1)} %get-tuple-element.36), channel_id=1, replica_groups={{0,2,4,6,8,10,12,14,16,18,20,22,24,26,28,30},{1,3,5,7,9,11,13,15,17,19,..., dimensions={0} | all-to-all | bytes 393216 | tf_op jit(solution)/shard_map/all_to_all | solution.py:262
  108.4 7.4 %collective-permute-start.6 = (bf16[16,24,256]{2,1,0:T(8,128)(2,1)S(1)}, bf16[16,24,256]{2,1,0:T(8,128)(2,1)S(1)}, u32[]{:S(2)}, u32[]{:S(2)}) collective-permute-start(bf16[16,24,256]{2,1,0:T(8,128)(2,1)S(1)} %all_to_all.25.own), channel_id=1, source_target_pairs={{0,1},{1,0},{2,3},{3,2},{4,5},{5,4},{6,7},{7,6},{8,9},{9,8},{10,11... | collective-permute-start | bytes 589832 | tf_op jit(solution)/shard_map/ppermute | solution.py:268
  115.8 0.9 shard_map.152
  116.9 0.9 shard_map.153
  (33 shorter events, 3.3 us)
Async XLA Ops:
  0.6 29.0 %copy-start.1 = (bf16[256,256]{1,0:T(8,128)(2,1)S(1)}, bf16[256,256]{1,0:T(8,128)(2,1)}, u32[]{:S(2)}) copy-start(bf16[256,256]{1,0:T(8,128)(2,1)} %w_left.3) | copy-start | bytes 393220
  0.6 0.8 copy-start.2
  1.4 23.2 %copy-start.9 = (bf16[1,16,25,128]{3,1,2,0:T(8,128)(2,1)S(1)}, bf16[1,16,25,128]{3,1,2,0:T(8,128)(2,1)}, u32[]{:S(2)}) copy-start(bf16[1,16,25,128]{3,1,2,0:T(8,128)(2,1)} %param.12) | copy-start | bytes 307204
  1.4 28.2 %copy-start.3 = (bf16[32,256]{1,0:T(8,128)(2,1)S(1)}, bf16[32,256]{1,0:T(8,128)(2,1)}, u32[]{:S(2)}) copy-start(bf16[32,256]{1,0:T(8,128)(2,1)} %nodes.1) | copy-start | bytes 49156
  1.4 28.2 %copy-start.4 = (s32[1,16,128]{2,1,0:T(8,128)S(1)}, s32[1,16,128]{2,1,0:T(8,128)}, u32[]{:S(2)}) copy-start(s32[1,16,128]{2,1,0:T(8,128)} %param.14) | copy-start | bytes 24580
  1.4 28.3 %copy-start.6 = (s32[1,16,128]{2,1,0:T(8,128)S(1)}, s32[1,16,128]{2,1,0:T(8,128)}, u32[]{:S(2)}) copy-start(s32[1,16,128]{2,1,0:T(8,128)} %param.16) | copy-start | bytes 24580
  1.4 28.3 %copy-start.7 = (bf16[169,256]{1,0:T(8,128)(2,1)S(1)}, bf16[169,256]{1,0:T(8,128)(2,1)}, u32[]{:S(2)}) copy-start(bf16[169,256]{1,0:T(8,128)(2,1)} %w_out.1) | copy-start | bytes 259588
  1.4 28.3 %copy-start.8 = (bf16[25,256]{1,0:T(8,128)(2,1)S(1)}, bf16[25,256]{1,0:T(8,128)(2,1)}, u32[]{:S(2)}) copy-start(bf16[25,256]{1,0:T(8,128)(2,1)} %w_harm.1) | copy-start | bytes 38404
  2.3 27.3 %all-to-all-start = ((bf16[32,32,256]{2,1,0:T(8,128)(2,1)}), bf16[32,32,256]{2,1,0:T(8,128)(2,1)S(1)}, u32[]{:S(2)}, u32[]{:S(2)}) async-start(bf16[32,32,256]{2,1,0:T(8,128)(2,1)} %shard_map.146), calls=%async_computation | async-start | bytes 1048576 | tf_op jit(solution)/shard_map/all_to_all | solution.py:262
  12.7 19.4 %collective-permute-start = (bf16[32,256]{1,0:T(8,128)(2,1)}, bf16[32,256]{1,0:T(8,128)(2,1)S(1)}, u32[]{:S(2)}, u32[]{:S(2)}) collective-permute-start(bf16[32,256]{1,0:T(8,128)(2,1)} %nodes.1), channel_id=1, source_target_pairs={{0,32},{32,64},{64,96},{96,128},{128,160},{160,192},{192,224},{224... | collective-permute-start | bytes 49160 | tf_op jit(solution)/shard_map/ppermute | solution.py:273
  21.3 10.8 %collective-permute-start.1 = (bf16[32,256]{1,0:T(8,128)(2,1)}, bf16[32,256]{1,0:T(8,128)(2,1)S(1)}, u32[]{:S(2)}, u32[]{:S(2)}) collective-permute-start(bf16[32,256]{1,0:T(8,128)(2,1)} %nodes.1), channel_id=1, source_target_pairs={{32,0},{64,32},{96,64},{128,96},{160,128},{192,160},{224,192},{256... | collective-permute-start | bytes 49160 | tf_op jit(solution)/shard_map/ppermute | solution.py:273
  29.7 2.5 %copy-start = (bf16[256,256]{1,0:T(8,128)(2,1)S(1)}, bf16[256,256]{1,0:T(8,128)(2,1)}, u32[]{:S(2)}) copy-start(bf16[256,256]{1,0:T(8,128)(2,1)} %w_right.3) | copy-start | bytes 393220
  29.7 2.5 %copy-start.5 = (s32[1,16,128]{2,1,0:T(8,128)S(1)}, s32[1,16,128]{2,1,0:T(8,128)}, u32[]{:S(2)}) copy-start(s32[1,16,128]{2,1,0:T(8,128)} %param.15) | copy-start | bytes 24580
  35.9 4.4 %collective-permute-start.2 = (f32[16,56,256]{2,1,0:T(8,128)S(1)}, f32[16,56,256]{2,1,0:T(8,128)S(1)}, u32[]{:S(2)}, u32[]{:S(2)}) collective-permute-start(f32[16,56,256]{2,1,0:T(8,128)S(1)} %get-tuple-element.28), channel_id=1, source_target_pairs={{0,1},{1,0},{2,3},{3,2},{4,5},{5,4},{6,7},{7,6},{8,9},{9,8},{10,11... | collective-permute-start | bytes 2752520 | tf_op jit(solution)/shard_map/ppermute | solution.py:268
  41.1 23.3 %all-to-all-start.1 = ((bf16[16,56,256]{2,1,0:T(8,128)(2,1)}), bf16[16,56,256]{2,1,0:T(8,128)(2,1)S(1)}, u32[]{:S(2)}, u32[]{:S(2)}) async-start(bf16[16,56,256]{2,1,0:T(8,128)(2,1)} %add_convert_fusion), calls=%async_computation.1 | async-start | bytes 917504 | tf_op jit(solution)/shard_map/all_to_all | solution.py:262
  50.1 3.4 %collective-permute-start.3 = (f32[32,256]{1,0:T(8,128)S(1)}, f32[32,256]{1,0:T(8,128)S(1)}, u32[]{:S(2)}, u32[]{:S(2)}) collective-permute-start(f32[32,256]{1,0:T(8,128)S(1)} %get-tuple-element.30), channel_id=1, source_target_pairs={{0,1},{1,0},{2,3},{3,2},{4,5},{5,4},{6,7},{7,6},{8,9},{9,8},{10,11... | collective-permute-start | bytes 98312 | tf_op jit(solution)/shard_map/ppermute | solution.py:268
  65.2 11.2 %all-to-all-start.2 = ((f32[4,24,256]{2,1,0:T(8,128)}), f32[4,24,256]{2,1,0:T(8,128)S(1)}, u32[]{:S(2)}, u32[]{:S(2)}) async-start(f32[4,24,256]{2,1,0:T(8,128)} %get-tuple-element.32), calls=%async_computation.2 | async-start | bytes 196608 | tf_op jit(solution)/shard_map/all_to_all | solution.py:262
  69.7 15.8 %collective-permute-start.4 = (f32[64,256]{1,0:T(8,128)S(1)}, f32[64,256]{1,0:T(8,128)S(1)}, u32[]{:S(2)}, u32[]{:S(2)}) collective-permute-start(f32[64,256]{1,0:T(8,128)S(1)} %get-tuple-element.34), channel_id=1, source_target_pairs={{1,33},{3,35},{5,37},{7,39},{9,41},{11,43},{13,45},{15,47},{17,49}... | collective-permute-start | bytes 196616 | tf_op jit(solution)/shard_map/ppermute | solution.py:286
  77.0 20.4 %all-to-all-start.3 = ((f32[4,24,256]{2,1,0:T(8,128)}), f32[4,24,256]{2,1,0:T(8,128)S(1)}, u32[]{:S(2)}, u32[]{:S(2)}) async-start(f32[4,24,256]{2,1,0:T(8,128)} %shard_map.150), calls=%async_computation.3 | async-start | bytes 196608 | tf_op jit(solution)/shard_map/all_to_all | solution.py:262
  85.6 5.7 %collective-permute-start.5 = (f32[32,256]{1,0:T(8,128)S(1)}, f32[32,256]{1,0:T(8,128)S(1)}, u32[]{:S(2)}, u32[]{:S(2)}) collective-permute-start(f32[32,256]{1,0:T(8,128)S(1)} %get-tuple-element.41), channel_id=1, source_target_pairs={{0,1},{1,0},{2,3},{3,2},{4,5},{5,4},{6,7},{7,6},{8,9},{9,8},{10,11... | collective-permute-start | bytes 98312 | tf_op jit(solution)/shard_map/ppermute | solution.py:268
  108.4 8.5 %collective-permute-start.6 = (bf16[16,24,256]{2,1,0:T(8,128)(2,1)S(1)}, bf16[16,24,256]{2,1,0:T(8,128)(2,1)S(1)}, u32[]{:S(2)}, u32[]{:S(2)}) collective-permute-start(bf16[16,24,256]{2,1,0:T(8,128)(2,1)S(1)} %all_to_all.25.own), channel_id=1, source_target_pairs={{0,1},{1,0},{2,3},{3,2},{4,5},{5,4},{6,7},{7,6},{8,9},{9,8},{10,11... | collective-permute-start | bytes 589832 | tf_op jit(solution)/shard_map/ppermute | solution.py:268

commit v8 on v7

--- a/solution.py
+++ b/solution.py
@@ -12,7 +12,8 @@
 BOTH = ("row", "col")
 BLOCKS_PER_STEP = 8
 OUT_ROWS = 176
-X_BITS, Z_BITS, CHIP_BITS, COL_BITS = (4, 8), (1, 2), (2, 4, 8, 16), (1, 2, 4, 8, 16)
+SHARD = 32
+X_BITS, Z_BITS, CHIP_BITS = (4, 8), (1, 2), (2, 4, 8, 16)
 
 
 def like(*shape):
@@ -54,22 +55,38 @@
     return lax.div(places[0] + BLOCKS_PER_STEP - 1, BLOCKS_PER_STEP)
 
 
-def row_pair_kernel(
-    places, rows, mask, harm, grads, row_nodes, nodes, w_left, w_harm, w_out,
-    u_pairs, e_pairs, gz_pairs, same_nodes, u_parts, harm_t, out_t,
-):
-    same_nodes[...] = nodes[...]
+def places_of(places, rows, first, shard, half):
+    atom = line(rows, first)
+    owner = lax.div(atom, shard)
+    place = lax.shift_right_logical(owner, 1) * shard + lax.rem(atom, shard)
+    return place + jnp.where(jnp.bitwise_and(owner, 1) == places[2], 0, half)
+
+
+def project(w_left, nodes, u_parts):
     width = w_left.shape[0]
-    high, low = halves(dot(w_left[...], row_nodes[...], 0, 1))
+    high, low = halves(dot(w_left[...], nodes[...], 0, 1))
     u_parts[:width] = high
     u_parts[width:] = low
+
+
+def gathered(u_parts, place):
+    width = u_parts.shape[0] // 2
+    parts = dot(u_parts[...], picks(place, u_parts.shape[1]), 1, 0)
+    return parts[:width] + parts[width:]
+
+
+def own_pair_kernel(
+    places, rows, mask, harm, grads, own, w_left, w_harm, w_out,
+    u_pairs, e_pairs, gz_pairs, u_parts, harm_t, out_t,
+):
+    half = own.shape[0]
+    project(w_left, own, u_parts)
     harm_t[...] = w_harm[...].astype(F32).T.astype(BF16)
     out_t[...] = w_out[...].astype(F32).T.astype(BF16)
 
     def step(i, carry):
         first = BLOCKS_PER_STEP * i
-        parts = dot(u_parts[...], picks(line(rows, first), row_nodes.shape[0]), 1, 0)
-        u_pairs[i] = parts[:width] + parts[width:]
+        u_pairs[i] = gathered(u_parts, places_of(places, rows, first, SHARD, half))
         e_pairs[i] = dot(harm_t[...], beside(harm, first), 1, 0)
         gz_pairs[i] = dot(out_t[...], masked(places, mask, grads, first), 1, 0)
         return carry
@@ -77,14 +94,27 @@
     lax.fori_loop(0, steps_of(places), step, 0)
 
 
+def other_pair_kernel(places, rows, other, nodes, w_left, u_pairs, same_nodes, u_parts):
+    half = other.shape[0]
+    same_nodes[...] = nodes[...]
+    project(w_left, other, u_parts)
+
+    def step(i, carry):
+        place = places_of(places, rows, BLOCKS_PER_STEP * i, SHARD, half)
+        u_pairs[i] = gathered(u_parts, place - half)
+        return carry
+
+    lax.fori_loop(0, steps_of(places), step, 0)
+
+
 def pair_kernel(
-    places, rows, cols, mask, harm, grads, row_nodes, column_nodes, w_right,
-    u_pairs, e_pairs, gz_pairs,
+    places, rows, cols, mask, harm, grads, own, other, column_nodes, w_right,
+    u_pairs, other_u_pairs, e_pairs, gz_pairs,
     keep, send, middle, ahead, passed, v_parts, sum_u, sum_v, weights,
 ):
     column_base, core = places[1], places[2]
     width = w_right.shape[0]
-    atoms, near = row_nodes.shape[0], column_nodes.shape[0]
+    half, near = own.shape[0], column_nodes.shape[0]
     shard = near // 3
     orbitals, harmonics = grads.shape[1], harm.shape[1]
     v_parts[...] = jnp.concatenate(halves(dot(w_right[...], column_nodes[...], 0, 1)), axis=1)
@@ -97,10 +127,10 @@
         first = BLOCKS_PER_STEP * i
         g = masked(places, mask, grads, first)
         h = beside(harm, first)
-        pick_u = picks(line(rows, first), atoms)
+        pick_u = picks(places_of(places, rows, first, shard, half), 2 * half)
         pick_v = picks(line(cols, first) - column_base, near)
         v = dot(v_parts[...], jnp.concatenate([pick_v, pick_v]), 1, 0)
-        u, e, gz = u_pairs[i], e_pairs[i], gz_pairs[i]
+        u, e, gz = u_pairs[i] + other_u_pairs[i], e_pairs[i], gz_pairs[i]
         uv = u * v
         weights[at_out : at_out + orbitals] += dot(g, (uv * e).astype(BF16), 1, 1)
         weights[at_harm : at_harm + harmonics] += dot(h, (gz * uv).astype(BF16), 1, 1)
@@ -112,15 +142,20 @@
         return carry
 
     lax.fori_loop(0, steps_of(places), step, 0)
-    for at, nodes, sums in ((0, row_nodes, sum_u), (width, column_nodes, sum_v)):
-        high, low = halves(sums[...])
-        weights[at : at + width] = dot(nodes[...], high, 0, 0) + dot(nodes[...], low, 0, 0)
+    for at, blocks in (
+        (0, ((own, sum_u[:half]), (other, sum_u[half:]))),
+        (width, ((column_nodes, sum_v[...]),)),
+    ):
+        total = jnp.zeros((width, width), F32)
+        for nodes, sums in blocks:
+            for part in halves(sums):
+                total = total + dot(nodes[...], part, 0, 0)
+        weights[at : at + width] = total
     chips, chunk = keep.shape[0], keep.shape[1]
     share = chunk - shard
     for chip in range(chips):
-        for to, which in ((keep, core), (send, 1 - core)):
-            start = pl.multiple_of((2 * chip + which) * shard, 8)
-            to[chip, :shard] = sum_u[pl.ds(start, shard), :]
+        for to, first, which in ((keep, 0, core), (send, half, 1 - core)):
+            to[chip, :shard] = sum_u[first + chip * shard : first + (chip + 1) * shard]
             start = pl.multiple_of((which * chips + chip) * share, 8)
             to[chip, shard:] = weights[pl.ds(start, share), :]
     middle[...] = sum_v[shard : 2 * shard]
@@ -128,46 +163,59 @@
     passed[...] = sum_v[pl.ds(pl.multiple_of((1 - core) * 2 * shard, 8), shard), :]
 
 
-def row_pairs(places, rows, mask, harm, grads, row_nodes, nodes, w_left, w_harm, w_out):
-    atoms, width = row_nodes.shape
+def own_pairs(places, rows, mask, harm, grads, own, w_left, w_harm, w_out):
+    half, width = own.shape
     pairs = BLOCKS_PER_STEP * rows.shape[1]
     steps = rows.shape[0] // BLOCKS_PER_STEP
-    per_pair = like(steps, width, pairs)
-    flops = 2 * steps * pairs * width * (2 * atoms + w_harm.shape[0] + w_out.shape[0])
     return pl.pallas_call(
-        row_pair_kernel,
-        out_shape=(per_pair,) * 3 + (jax.ShapeDtypeStruct(nodes.shape, BF16),),
-        in_specs=[SMEM] + [VMEM] * 9,
-        out_specs=(VMEM,) * 4,
+        own_pair_kernel,
+        out_shape=(like(steps, width, pairs),) * 3,
+        in_specs=[SMEM] + [VMEM] * 8,
+        out_specs=(VMEM,) * 3,
         scratch_shapes=[
-            pltpu.VMEM((2 * width, atoms), BF16),
+            pltpu.VMEM((2 * width, half), BF16),
             pltpu.VMEM(w_harm.shape[::-1], BF16),
             pltpu.VMEM(w_out.shape[::-1], BF16),
         ],
         compiler_params=PARAMS,
-        cost_estimate=pl.CostEstimate(flops=flops, bytes_accessed=8 << 20, transcendentals=0),
-    )(places, rows, mask, harm, grads, row_nodes, nodes, w_left, w_harm, w_out)
+        cost_estimate=pl.CostEstimate(flops=2 << 30, bytes_accessed=8 << 20, transcendentals=0),
+    )(places, rows, mask, harm, grads, own, w_left, w_harm, w_out)
+
+
+def other_pairs(places, rows, other, nodes, w_left):
+    half, width = other.shape
+    pairs = BLOCKS_PER_STEP * rows.shape[1]
+    steps = rows.shape[0] // BLOCKS_PER_STEP
+    return pl.pallas_call(
+        other_pair_kernel,
+        out_shape=(like(steps, width, pairs), jax.ShapeDtypeStruct(nodes.shape, BF16)),
+        in_specs=[SMEM] + [VMEM] * 4,
+        out_specs=(VMEM,) * 2,
+        scratch_shapes=[pltpu.VMEM((2 * width, half), BF16)],
+        compiler_params=PARAMS,
+        cost_estimate=pl.CostEstimate(flops=2 << 30, bytes_accessed=4 << 20, transcendentals=0),
+    )(places, rows, other, nodes, w_left)
 
 
 def pair_sums(
-    places, rows, cols, mask, harm, grads, row_nodes, column_nodes, w_right, per_pair, chips, share
+    places, rows, cols, mask, harm, grads, own, other, column_nodes, w_right, per_pair, chips, share
 ):
-    atoms, width = row_nodes.shape
+    half, width = own.shape
     near = column_nodes.shape[0]
     chunks, block = like(chips, near // 3 + share, width), like(near // 3, width)
     return pl.pallas_call(
         pair_kernel,
         out_shape=(chunks,) * 2 + (block,) * 3,
-        in_specs=[SMEM] + [VMEM] * 11,
+        in_specs=[SMEM] + [VMEM] * 13,
         out_specs=(VMEM,) * 5,
         scratch_shapes=[
             pltpu.VMEM((width, 2 * near), BF16),
-            pltpu.VMEM((atoms, width), F32),
+            pltpu.VMEM((2 * half, width), F32),
             pltpu.VMEM((near, width), F32),
             pltpu.VMEM((2 * chips * share, width), F32),
         ],
         compiler_params=PARAMS,
-    )(places, rows, cols, mask, harm, grads, row_nodes, column_nodes, w_right, *per_pair)
+    )(places, rows, cols, mask, harm, grads, own, other, column_nodes, w_right, *per_pair)
 
 
 def total_of(parts):
@@ -309,24 +357,25 @@
     w_out,
 ):
     shard, width = nodes.shape
-    columns = lax.axis_size("col")
-    chips = columns // 2
+    chips = lax.axis_size("col") // 2
     share = 24
     spread = 4
     row = lax.axis_index("row")
     core = jnp.bitwise_and(lax.axis_index("col"), 1)
     before, after = shifted(nodes, 1), shifted(nodes, -1)
-    row_nodes = exchange(repeated(nodes, columns), "col", COL_BITS).reshape(-1, width)
+    own = exchange(repeated(nodes, chips), "col", CHIP_BITS).reshape(-1, width)
+    other = swapped(own)
     places = jnp.stack([block_counts[0, 0], (row - 1) * shard, core]).astype(jnp.int32)
     rows, cols, mask = pair_rows[0], pair_cols[0], pair_mask[0]
     harm, grads = harmonics[0], grad_blocks[0]
-    *per_pair, same_nodes = row_pairs(
-        places, rows, mask, harm, grads, row_nodes, nodes, w_left, w_harm, w_out
-    )
+    own_u, e_pairs, gz_pairs = own_pairs(
+        places, rows, mask, harm, grads, own, w_left, w_harm, w_out
+    )
+    other_u, same_nodes = other_pairs(places, rows, other, nodes, w_left)
     column_nodes = jnp.concatenate([before, same_nodes, after])
     keep, send, middle, ahead, passed = pair_sums(
-        places, rows, cols, mask, harm, grads, row_nodes, column_nodes, w_right, per_pair,
-        chips, share,
+        places, rows, cols, mask, harm, grads, own, other, column_nodes, w_right,
+        (own_u, other_u, e_pairs, gz_pairs), chips, share,
     )
     parts = (keep + swapped(send)).astype(BF16)
     parts = exchange(parts, "col", CHIP_BITS)

time: 119 us -> 120 us (level)
  starting transfers between devices: 65.8 us -> 71.4 us
  waiting for transfers between devices: 26.2 us -> 20.7 us
    all_to_all x4, waiting for transfers between devices: 22.1 us -> 16.8 us  [exchange(): lax.all_to_all(blocks, axis, 0, 0, tiled=True, axis_index_groups=groups(l...]
    ppermute x4 -> x5, starting transfers between devices: 16.8 us -> 21.2 us  [swapped(): lax.ppermute(block, 'col', [(i, i ^ 1) for i in range(lax.axis_size('col'...]
    all_to_all x4, starting transfers between devices: 32.5 us -> 33.7 us  [exchange(): lax.all_to_all(blocks, axis, 0, 0, tiled=True, axis_index_groups=groups(l...]
    pallas_call x1 -> x2, Pallas kernels: 2.42 us -> 3.35 us  [the longest x1 1.81 us: own_pairs(): pl.pallas_call(own_pair_kernel, out_shape=(like(steps, width, pairs),) *...]
    ppermute x4 -> x5, waiting for transfers between devices: 4.15 us -> 3.92 us  [swapped(): lax.ppermute(block, 'col', [(i, i ^ 1) for i in range(lax.axis_size('col'...]
  transfers between devices with their start and end apart: 11 -> 12, of which waited for: 7 -> 6; matrix products, arithmetic and copies ran while one was open for 1% -> 1% of each run, Pallas kernels for 3% -> 4%
where the time goes in v8:
time: 120 us; the launch traced here: 119 us
  starting transfers between devices  71.4 us (60%)
  waiting for transfers between devices  20.7 us (17%)
  blocking collectives  11.3 us (9%)
  Pallas kernels  11 us (9%)
  local copies, waits for them, and re-layouts  2.11 us (2%)
  between operations  1.58 us (1%)
    all_to_all x4, starting transfers between devices, exchange(): lax.all_to_all(blocks, axis, 0, 0, tiled=True, axis_index_groups=groups(l...  33.7 us
    ppermute x5, starting transfers between devices, swapped(): lax.ppermute(block, 'col', [(i, i ^ 1) for i in range(lax.axis_size('col'...  21.2 us
    all_to_all x4, waiting for transfers between devices, exchange(): lax.all_to_all(blocks, axis, 0, 0, tiled=True, axis_index_groups=groups(l...  16.8 us
    all_to_all x1, blocking collectives, exchange(): lax.all_to_all(blocks, axis, 0, 0, tiled=True, axis_index_groups=groups(l...  11.3 us
    ppermute x2, starting transfers between devices, shifted(): lax.ppermute(block, 'row', [(i, i + distance) for i in devices if i + dis...  10.1 us
    ppermute x1, starting transfers between devices, neighbours(): return lax.ppermute(block, BOTH, route)  6.33 us
    ppermute x5, waiting for transfers between devices, swapped(): lax.ppermute(block, 'col', [(i, i ^ 1) for i in range(lax.axis_size('col'...  3.92 us
    pallas_call x1, Pallas kernels, pair_sums(): pl.pallas_call(pair_kernel, out_shape=(chunks,) * 2 + (block,) * 3, in_sp...  3.8 us
  transfers between devices with their start and end apart: 12, of which 6 were waited for; matrix products, arithmetic and copies ran while one was open for 1% of the time, Pallas kernels for 4%

profile of v8, /device:TPU:1, one launch (start us, length us, event | category | flops | bytes accessed | tf_op | source)
XLA Modules:
  0.0 119.0 jit_solution(1851155287866880654)
XLA Ops:
  2.1 9.2 %all-to-all-start = ((bf16[16,32,256]{2,1,0:T(8,128)(2,1)}), bf16[16,32,256]{2,1,0:T(8,128)(2,1)S(1)}, u32[]{:S(2)}, u32[]{:S(2)}) async-start(bf16[16,32,256]{2,1,0:T(8,128)(2,1)} %shard_map.146), calls=%async_computation | async-start | bytes 524288 | tf_op jit(solution)/shard_map/all_to_all | solution.py:310
  11.3 8.8 %collective-permute-start.1 = (bf16[32,256]{1,0:T(8,128)(2,1)}, bf16[32,256]{1,0:T(8,128)(2,1)S(1)}, u32[]{:S(2)}, u32[]{:S(2)}) collective-permute-start(bf16[32,256]{1,0:T(8,128)(2,1)} %nodes.1), channel_id=1, source_target_pairs={{0,32},{32,64},{64,96},{96,128},{128,160},{160,192},{192,224},{224... | collective-permute-start | bytes 49160 | tf_op jit(solution)/shard_map/ppermute | solution.py:321
  20.2 1.3 %collective-permute-start.2 = (bf16[32,256]{1,0:T(8,128)(2,1)}, bf16[32,256]{1,0:T(8,128)(2,1)S(1)}, u32[]{:S(2)}, u32[]{:S(2)}) collective-permute-start(bf16[32,256]{1,0:T(8,128)(2,1)} %nodes.1), channel_id=1, source_target_pairs={{32,0},{64,32},{96,64},{128,96},{160,128},{192,160},{224,192},{256... | collective-permute-start | bytes 49160 | tf_op jit(solution)/shard_map/ppermute | solution.py:321
  22.1 1.3 %copy.20 = bf16[1,16,169,128]{3,2,1,0:T(8,128)(2,1)S(1)} copy(bf16[1,16,169,128]{3,1,2,0:T(8,128)(2,1)} %param.13) | data formatting | bytes 1384448 | tf_op args[2]
  23.5 3.1 %collective-permute-start = (bf16[512,256]{1,0:T(8,128)(2,1)S(1)}, bf16[512,256]{1,0:T(8,128)(2,1)S(1)}, u32[]{:S(2)}, u32[]{:S(2)}) collective-permute-start(bf16[512,256]{1,0:T(8,128)(2,1)S(1)} %bitcast.16), channel_id=1, source_target_pairs={{0,1},{1,0},{2,3},{3,2},{4,5},{5,4},{6,7},{7,6},{8,9},{9,8},{10,11... | collective-permute-start | bytes 786440 | tf_op jit(solution)/shard_map/ppermute | solution.py:316
  26.7 1.8 %shard_map.148 = (f32[2,256,1024]{2,1,0:T(8,128)S(1)}, f32[2,256,1024]{2,1,0:T(8,128)S(1)}, f32[2,256,1024]{2,1,0:T(8,128)S(1)}) custom-call(s32[3]{0:T(128)S(1)} %pad_add_fusion.places, s32[16,128]{1,0:T(8,128)S(1)} %bitcast.21, s32[16,128]{1,0:T(8,128)S(1)} %bitcast.25, bf16[16,25,128]{2,1,0:T(8,128)(2,1)S(1)} %bitcast.19, ...), custom_call_target="tpu_custom_call" | custom-call | flops 2147483648 | bytes 8388608 | tf_op jit(solution)/shard_map/pallas_call | solution.py:170
  28.6 1.5 %shard_map.147 = (f32[2,256,1024]{2,1,0:T(8,128)S(1)}, bf16[32,256]{1,0:T(8,128)(2,1)S(1)}) custom-call(s32[3]{0:T(128)S(1)} %pad_add_fusion.places, s32[16,128]{1,0:T(8,128)S(1)} %bitcast.22, bf16[512,256]{1,0:T(8,128)(2,1)S(1)} %collective-permute-done.other, bf16[32,256]{1,0:T(8,128)(2,1)S(1)} %copy-done.3, bf16[256,256]{1,0:T(8,128)(2,1)S(1)} %copy-done.1), custom_call_target="tpu_custom_call" | custom-call | flops 2147483648 | bytes 4194304 | tf_op jit(solution)/shard_map/pallas_call | solution.py:189
  30.2 3.8 %shard_map.149 = (f32[16,56,256]{2,1,0:T(8,128)S(1)}, f32[16,56,256]{2,1,0:T(8,128)S(1)}, f32[32,256]{1,0:T(8,128)S(1)}, f32[32,256]{1,0:T(8,128)S(1)}, f32[32,256]{1,0:T(8,128)S(1)}) custom-call(s32[3]{0:T(128)S(1)} %pad_add_fusion.places, s32[16,128]{1,0:T(8,128)S(1)} %bitcast.23, s32[16,128]{1,0:T(8,128)S(1)} %bitcast.24, s32[16,128]{1,0:T(8,128)S(1)} %bitcast.26, ...), custom_call_target="tpu_custom_call" | custom-call | tf_op jit(solution)/shard_map/pallas_call | solution.py:206
  34.0 2.9 %collective-permute-start.3 = (f32[16,56,256]{2,1,0:T(8,128)S(1)}, f32[16,56,256]{2,1,0:T(8,128)S(1)}, u32[]{:S(2)}, u32[]{:S(2)}) collective-permute-start(f32[16,56,256]{2,1,0:T(8,128)S(1)} %get-tuple-element.30), channel_id=1, source_target_pairs={{0,1},{1,0},{2,3},{3,2},{4,5},{5,4},{6,7},{7,6},{8,9},{9,8},{10,11... | collective-permute-start | bytes 2752520 | tf_op jit(solution)/shard_map/ppermute | solution.py:316
  36.9 2.1 %collective-permute-done.3 = f32[16,56,256]{2,1,0:T(8,128)S(1)} collective-permute-done((f32[16,56,256]{2,1,0:T(8,128)S(1)}, f32[16,56,256]{2,1,0:T(8,128)S(1)}, u32[]{:S(2)}, u32[]{:S(2)}) %collective-permute-start.3) | collective-permute-done | bytes 917536 | tf_op jit(solution)/shard_map/ppermute | solution.py:316
  39.0 0.9 add_convert_fusion
  39.8 10.3 %all-to-all-start.1 = ((bf16[16,56,256]{2,1,0:T(8,128)(2,1)}), bf16[16,56,256]{2,1,0:T(8,128)(2,1)S(1)}, u32[]{:S(2)}, u32[]{:S(2)}) async-start(bf16[16,56,256]{2,1,0:T(8,128)(2,1)} %add_convert_fusion), calls=%async_computation.1 | async-start | bytes 917504 | tf_op jit(solution)/shard_map/all_to_all | solution.py:310
  50.1 2.6 %collective-permute-start.4 = (f32[32,256]{1,0:T(8,128)S(1)}, f32[32,256]{1,0:T(8,128)S(1)}, u32[]{:S(2)}, u32[]{:S(2)}) collective-permute-start(f32[32,256]{1,0:T(8,128)S(1)} %get-tuple-element.32), channel_id=1, source_target_pairs={{0,1},{1,0},{2,3},{3,2},{4,5},{5,4},{6,7},{7,6},{8,9},{9,8},{10,11... | collective-permute-start | bytes 98312 | tf_op jit(solution)/shard_map/ppermute | solution.py:316
  52.7 0.8 collective-permute-done.4.passed
  53.5 10.9 %all-to-all-done.1.parts = bf16[16,56,256]{2,1,0:T(8,128)(2,1)S(1)} async-done(((bf16[16,56,256]{2,1,0:T(8,128)(2,1)}), bf16[16,56,256]{2,1,0:T(8,128)(2,1)S(1)}, u32[]{:S(2)}, u32[]{:S(2)}) %all-to-all-start.1) | async-done | bytes 458784 | tf_op jit(solution)/shard_map/all_to_all | solution.py:310
  65.1 6.1 %all-to-all-start.2 = ((f32[4,24,256]{2,1,0:T(8,128)}), f32[4,24,256]{2,1,0:T(8,128)S(1)}, u32[]{:S(2)}, u32[]{:S(2)}) async-start(f32[4,24,256]{2,1,0:T(8,128)} %get-tuple-element.34), calls=%async_computation.2 | async-start | bytes 196608 | tf_op jit(solution)/shard_map/all_to_all | solution.py:310
  71.2 6.3 %collective-permute-start.5 = (f32[64,256]{1,0:T(8,128)S(1)}, f32[64,256]{1,0:T(8,128)S(1)}, u32[]{:S(2)}, u32[]{:S(2)}) collective-permute-start(f32[64,256]{1,0:T(8,128)S(1)} %get-tuple-element.36), channel_id=1, source_target_pairs={{1,33},{3,35},{5,37},{7,39},{9,41},{11,43},{13,45},{15,47},{17,49}... | collective-permute-start | bytes 196616 | tf_op jit(solution)/shard_map/ppermute | solution.py:334
  78.2 8.2 %all-to-all-start.3 = ((f32[4,24,256]{2,1,0:T(8,128)}), f32[4,24,256]{2,1,0:T(8,128)S(1)}, u32[]{:S(2)}, u32[]{:S(2)}) async-start(f32[4,24,256]{2,1,0:T(8,128)} %shard_map.151), calls=%async_computation.3 | async-start | bytes 196608 | tf_op jit(solution)/shard_map/all_to_all | solution.py:310
  86.4 5.2 %collective-permute-start.6 = (f32[32,256]{1,0:T(8,128)S(1)}, f32[32,256]{1,0:T(8,128)S(1)}, u32[]{:S(2)}, u32[]{:S(2)}) collective-permute-start(f32[32,256]{1,0:T(8,128)S(1)} %get-tuple-element.43), channel_id=1, source_target_pairs={{0,1},{1,0},{2,3},{3,2},{4,5},{5,4},{6,7},{7,6},{8,9},{9,8},{10,11... | collective-permute-start | bytes 98312 | tf_op jit(solution)/shard_map/ppermute | solution.py:316
  92.5 5.8 %all-to-all-done.3.parts = f32[4,24,256]{2,1,0:T(8,128)S(1)} async-done(((f32[4,24,256]{2,1,0:T(8,128)}), f32[4,24,256]{2,1,0:T(8,128)S(1)}, u32[]{:S(2)}, u32[]{:S(2)}) %all-to-all-start.3) | async-done | bytes 98336 | tf_op jit(solution)/shard_map/all_to_all | solution.py:310
  98.3 11.3 %all_to_all.25.own = bf16[16,24,256]{2,1,0:T(8,128)(2,1)S(1)} all-to-all(bf16[16,24,256]{2,1,0:T(8,128)(2,1)S(1)} %get-tuple-element.38), channel_id=1, replica_groups={{0,2,4,6,8,10,12,14,16,18,20,22,24,26,28,30},{1,3,5,7,9,11,13,15,17,19,..., dimensions={0} | all-to-all | bytes 393216 | tf_op jit(solution)/shard_map/all_to_all | solution.py:310
  109.6 7.4 %collective-permute-start.7 = (bf16[16,24,256]{2,1,0:T(8,128)(2,1)S(1)}, bf16[16,24,256]{2,1,0:T(8,128)(2,1)S(1)}, u32[]{:S(2)}, u32[]{:S(2)}) collective-permute-start(bf16[16,24,256]{2,1,0:T(8,128)(2,1)S(1)} %all_to_all.25.own), channel_id=1, source_target_pairs={{0,1},{1,0},{2,3},{3,2},{4,5},{5,4},{6,7},{7,6},{8,9},{9,8},{10,11... | collective-permute-start | bytes 589832 | tf_op jit(solution)/shard_map/ppermute | solution.py:316
  117.1 0.9 shard_map.153
  118.1 0.9 shard_map.154
  (36 shorter events, 4.0 us)
Async XLA Ops:
  0.6 26.1 %copy-start.1 = (bf16[256,256]{1,0:T(8,128)(2,1)S(1)}, bf16[256,256]{1,0:T(8,128)(2,1)}, u32[]{:S(2)}) copy-start(bf16[256,256]{1,0:T(8,128)(2,1)} %w_left.5) | copy-start | bytes 393220
  0.6 0.8 copy-start.2
  1.4 22.0 %copy-start.9 = (bf16[1,16,25,128]{3,1,2,0:T(8,128)(2,1)S(1)}, bf16[1,16,25,128]{3,1,2,0:T(8,128)(2,1)}, u32[]{:S(2)}) copy-start(bf16[1,16,25,128]{3,1,2,0:T(8,128)(2,1)} %param.12) | copy-start | bytes 307204
  1.4 25.3 %copy-start.4 = (s32[1,16,128]{2,1,0:T(8,128)S(1)}, s32[1,16,128]{2,1,0:T(8,128)}, u32[]{:S(2)}) copy-start(s32[1,16,128]{2,1,0:T(8,128)} %param.14) | copy-start | bytes 24580
  1.4 25.3 %copy-start.6 = (s32[1,16,128]{2,1,0:T(8,128)S(1)}, s32[1,16,128]{2,1,0:T(8,128)}, u32[]{:S(2)}) copy-start(s32[1,16,128]{2,1,0:T(8,128)} %param.16) | copy-start | bytes 24580
  1.4 25.3 %copy-start.7 = (bf16[169,256]{1,0:T(8,128)(2,1)S(1)}, bf16[169,256]{1,0:T(8,128)(2,1)}, u32[]{:S(2)}) copy-start(bf16[169,256]{1,0:T(8,128)(2,1)} %w_out.1) | copy-start | bytes 259588
  1.4 25.3 %copy-start.8 = (bf16[25,256]{1,0:T(8,128)(2,1)S(1)}, bf16[25,256]{1,0:T(8,128)(2,1)}, u32[]{:S(2)}) copy-start(bf16[25,256]{1,0:T(8,128)(2,1)} %w_harm.1) | copy-start | bytes 38404
  2.1 21.3 %all-to-all-start = ((bf16[16,32,256]{2,1,0:T(8,128)(2,1)}), bf16[16,32,256]{2,1,0:T(8,128)(2,1)S(1)}, u32[]{:S(2)}, u32[]{:S(2)}) async-start(bf16[16,32,256]{2,1,0:T(8,128)(2,1)} %shard_map.146), calls=%async_computation | async-start | bytes 524288 | tf_op jit(solution)/shard_map/all_to_all | solution.py:310
  11.3 18.8 %collective-permute-start.1 = (bf16[32,256]{1,0:T(8,128)(2,1)}, bf16[32,256]{1,0:T(8,128)(2,1)S(1)}, u32[]{:S(2)}, u32[]{:S(2)}) collective-permute-start(bf16[32,256]{1,0:T(8,128)(2,1)} %nodes.1), channel_id=1, source_target_pairs={{0,32},{32,64},{64,96},{96,128},{128,160},{160,192},{192,224},{224... | collective-permute-start | bytes 49160 | tf_op jit(solution)/shard_map/ppermute | solution.py:321
  20.2 10.0 %collective-permute-start.2 = (bf16[32,256]{1,0:T(8,128)(2,1)}, bf16[32,256]{1,0:T(8,128)(2,1)S(1)}, u32[]{:S(2)}, u32[]{:S(2)}) collective-permute-start(bf16[32,256]{1,0:T(8,128)(2,1)} %nodes.1), channel_id=1, source_target_pairs={{32,0},{64,32},{96,64},{128,96},{160,128},{192,160},{224,192},{256... | collective-permute-start | bytes 49160 | tf_op jit(solution)/shard_map/ppermute | solution.py:321
  23.5 5.1 %collective-permute-start = (bf16[512,256]{1,0:T(8,128)(2,1)S(1)}, bf16[512,256]{1,0:T(8,128)(2,1)S(1)}, u32[]{:S(2)}, u32[]{:S(2)}) collective-permute-start(bf16[512,256]{1,0:T(8,128)(2,1)S(1)} %bitcast.16), channel_id=1, source_target_pairs={{0,1},{1,0},{2,3},{3,2},{4,5},{5,4},{6,7},{7,6},{8,9},{9,8},{10,11... | collective-permute-start | bytes 786440 | tf_op jit(solution)/shard_map/ppermute | solution.py:316
  26.7 1.9 %copy-start.3 = (bf16[32,256]{1,0:T(8,128)(2,1)S(1)}, bf16[32,256]{1,0:T(8,128)(2,1)}, u32[]{:S(2)}) copy-start(bf16[32,256]{1,0:T(8,128)(2,1)} %nodes.1) | copy-start | bytes 49156
  28.6 1.6 %copy-start = (bf16[256,256]{1,0:T(8,128)(2,1)S(1)}, bf16[256,256]{1,0:T(8,128)(2,1)}, u32[]{:S(2)}) copy-start(bf16[256,256]{1,0:T(8,128)(2,1)} %w_right.3) | copy-start | bytes 393220
  28.6 1.6 %copy-start.5 = (s32[1,16,128]{2,1,0:T(8,128)S(1)}, s32[1,16,128]{2,1,0:T(8,128)}, u32[]{:S(2)}) copy-start(s32[1,16,128]{2,1,0:T(8,128)} %param.15) | copy-start | bytes 24580
  34.0 4.9 %collective-permute-start.3 = (f32[16,56,256]{2,1,0:T(8,128)S(1)}, f32[16,56,256]{2,1,0:T(8,128)S(1)}, u32[]{:S(2)}, u32[]{:S(2)}) collective-permute-start(f32[16,56,256]{2,1,0:T(8,128)S(1)} %get-tuple-element.30), channel_id=1, source_target_pairs={{0,1},{1,0},{2,3},{3,2},{4,5},{5,4},{6,7},{7,6},{8,9},{9,8},{10,11... | collective-permute-start | bytes 2752520 | tf_op jit(solution)/shard_map/ppermute | solution.py:316
  39.8 24.6 %all-to-all-start.1 = ((bf16[16,56,256]{2,1,0:T(8,128)(2,1)}), bf16[16,56,256]{2,1,0:T(8,128)(2,1)S(1)}, u32[]{:S(2)}, u32[]{:S(2)}) async-start(bf16[16,56,256]{2,1,0:T(8,128)(2,1)} %add_convert_fusion), calls=%async_computation.1 | async-start | bytes 917504 | tf_op jit(solution)/shard_map/all_to_all | solution.py:310
  50.1 3.4 %collective-permute-start.4 = (f32[32,256]{1,0:T(8,128)S(1)}, f32[32,256]{1,0:T(8,128)S(1)}, u32[]{:S(2)}, u32[]{:S(2)}) collective-permute-start(f32[32,256]{1,0:T(8,128)S(1)} %get-tuple-element.32), channel_id=1, source_target_pairs={{0,1},{1,0},{2,3},{3,2},{4,5},{5,4},{6,7},{7,6},{8,9},{9,8},{10,11... | collective-permute-start | bytes 98312 | tf_op jit(solution)/shard_map/ppermute | solution.py:316
  65.1 12.4 %all-to-all-start.2 = ((f32[4,24,256]{2,1,0:T(8,128)}), f32[4,24,256]{2,1,0:T(8,128)S(1)}, u32[]{:S(2)}, u32[]{:S(2)}) async-start(f32[4,24,256]{2,1,0:T(8,128)} %get-tuple-element.34), calls=%async_computation.2 | async-start | bytes 196608 | tf_op jit(solution)/shard_map/all_to_all | solution.py:310
  71.2 15.2 %collective-permute-start.5 = (f32[64,256]{1,0:T(8,128)S(1)}, f32[64,256]{1,0:T(8,128)S(1)}, u32[]{:S(2)}, u32[]{:S(2)}) collective-permute-start(f32[64,256]{1,0:T(8,128)S(1)} %get-tuple-element.36), channel_id=1, source_target_pairs={{1,33},{3,35},{5,37},{7,39},{9,41},{11,43},{13,45},{15,47},{17,49}... | collective-permute-start | bytes 196616 | tf_op jit(solution)/shard_map/ppermute | solution.py:334
  78.2 20.1 %all-to-all-start.3 = ((f32[4,24,256]{2,1,0:T(8,128)}), f32[4,24,256]{2,1,0:T(8,128)S(1)}, u32[]{:S(2)}, u32[]{:S(2)}) async-start(f32[4,24,256]{2,1,0:T(8,128)} %shard_map.151), calls=%async_computation.3 | async-start | bytes 196608 | tf_op jit(solution)/shard_map/all_to_all | solution.py:310
  86.4 6.0 %collective-permute-start.6 = (f32[32,256]{1,0:T(8,128)S(1)}, f32[32,256]{1,0:T(8,128)S(1)}, u32[]{:S(2)}, u32[]{:S(2)}) collective-permute-start(f32[32,256]{1,0:T(8,128)S(1)} %get-tuple-element.43), channel_id=1, source_target_pairs={{0,1},{1,0},{2,3},{3,2},{4,5},{5,4},{6,7},{7,6},{8,9},{9,8},{10,11... | collective-permute-start | bytes 98312 | tf_op jit(solution)/shard_map/ppermute | solution.py:316
  109.6 8.5 %collective-permute-start.7 = (bf16[16,24,256]{2,1,0:T(8,128)(2,1)S(1)}, bf16[16,24,256]{2,1,0:T(8,128)(2,1)S(1)}, u32[]{:S(2)}, u32[]{:S(2)}) collective-permute-start(bf16[16,24,256]{2,1,0:T(8,128)(2,1)S(1)} %all_to_all.25.own), channel_id=1, source_target_pairs={{0,1},{1,0},{2,3},{3,2},{4,5},{5,4},{6,7},{7,6},{8,9},{9,8},{10,11... | collective-permute-start | bytes 589832 | tf_op jit(solution)/shard_map/ppermute | solution.py:316

commit v9 on v7

--- a/solution.py
+++ b/solution.py
@@ -286,13 +286,26 @@
     return lax.ppermute(block, BOTH, route)
 
 
-def repeat_kernel(block, out):
-    for i in range(out.shape[0]):
-        out[i] = block[...]
+def repeat_kernel(block, out, sems):
+    copies = [
+        pltpu.make_async_copy(block, out.at[i], sems.at[i]) for i in range(out.shape[0])
+    ]
+    for copy in copies:
+        copy.start()
+    for copy in copies:
+        copy.wait()
 
 
 def repeated(block, copies):
-    return call(repeat_kernel, jax.ShapeDtypeStruct((copies,) + block.shape, block.dtype), block)
+    anywhere = pl.BlockSpec(memory_space=pl.ANY)
+    return pl.pallas_call(
+        repeat_kernel,
+        out_shape=jax.ShapeDtypeStruct((copies,) + block.shape, block.dtype),
+        in_specs=[anywhere],
+        out_specs=anywhere,
+        scratch_shapes=[pltpu.SemaphoreType.DMA((copies,))],
+        compiler_params=PARAMS,
+    )(block)
 
 
 def body(

time: 119 us -> 119 us (level)
    pallas_call x5 -> x4, Pallas kernels: 3.1 us -> 2.23 us  [call(): pl.pallas_call(kernel, out_shape=out_shape, in_specs=specs, out_specs=jax...]
where the time goes in v9:
time: 119 us; the launch traced here: 118 us
  starting transfers between devices  66.3 us (56%)
  waiting for transfers between devices  26.2 us (22%)
  blocking collectives  11 us (9%)
  Pallas kernels  10.4 us (9%)
  local copies, waits for them, and re-layouts  2.11 us (2%)
  between operations  1.55 us (1%)
    all_to_all x4, starting transfers between devices, exchange(): lax.all_to_all(blocks, axis, 0, 0, tiled=True, axis_index_groups=groups(l...  32.9 us
    all_to_all x4, waiting for transfers between devices, exchange(): lax.all_to_all(blocks, axis, 0, 0, tiled=True, axis_index_groups=groups(l...  22 us
    ppermute x4, starting transfers between devices, swapped(): lax.ppermute(block, 'col', [(i, i ^ 1) for i in range(lax.axis_size('col'...  16.9 us
    all_to_all x1, blocking collectives, exchange(): lax.all_to_all(blocks, axis, 0, 0, tiled=True, axis_index_groups=groups(l...  11 us
    ppermute x2, starting transfers between devices, shifted(): lax.ppermute(block, 'row', [(i, i + distance) for i in devices if i + dis...  9.88 us
    ppermute x1, starting transfers between devices, neighbours(): return lax.ppermute(block, BOTH, route)  6.61 us
    ppermute x4, waiting for transfers between devices, swapped(): lax.ppermute(block, 'col', [(i, i ^ 1) for i in range(lax.axis_size('col'...  4.14 us
    pallas_call x1, Pallas kernels, pair_sums(): pl.pallas_call(pair_kernel, out_shape=(chunks,) * 2 + (block,) * 3, in_sp...  3.72 us
  transfers between devices with their start and end apart: 11, of which 7 were waited for; matrix products, arithmetic and copies ran while one was open for 1% of the time, Pallas kernels for 3%

profile of v9, /device:TPU:1, one launch (start us, length us, event | category | flops | bytes accessed | tf_op | source)
XLA Modules:
  0.0 118.4 jit_solution(60336820429605351)
XLA Ops:
  1.4 1.1 shard_map.146
  2.5 10.4 %all-to-all-start = ((bf16[32,32,256]{2,1,0:T(8,128)(2,1)}), bf16[32,32,256]{2,1,0:T(8,128)(2,1)S(1)}, u32[]{:S(2)}, u32[]{:S(2)}) async-start(bf16[32,32,256]{2,1,0:T(8,128)(2,1)} %shard_map.146), calls=%async_computation | async-start | bytes 1048576 | tf_op jit(solution)/shard_map/all_to_all | solution.py:262
  13.0 8.6 %collective-permute-start = (bf16[32,256]{1,0:T(8,128)(2,1)}, bf16[32,256]{1,0:T(8,128)(2,1)S(1)}, u32[]{:S(2)}, u32[]{:S(2)}) collective-permute-start(bf16[32,256]{1,0:T(8,128)(2,1)} %nodes.1), channel_id=1, source_target_pairs={{0,32},{32,64},{64,96},{96,128},{128,160},{160,192},{192,224},{224... | collective-permute-start | bytes 49160 | tf_op jit(solution)/shard_map/ppermute | solution.py:273
  21.6 1.3 %collective-permute-start.1 = (bf16[32,256]{1,0:T(8,128)(2,1)}, bf16[32,256]{1,0:T(8,128)(2,1)S(1)}, u32[]{:S(2)}, u32[]{:S(2)}) collective-permute-start(bf16[32,256]{1,0:T(8,128)(2,1)} %nodes.1), channel_id=1, source_target_pairs={{32,0},{64,32},{96,64},{128,96},{160,128},{192,160},{224,192},{256... | collective-permute-start | bytes 49160 | tf_op jit(solution)/shard_map/ppermute | solution.py:273
  23.5 1.3 %copy.20 = bf16[1,16,169,128]{3,2,1,0:T(8,128)(2,1)S(1)} copy(bf16[1,16,169,128]{3,1,2,0:T(8,128)(2,1)} %param.13) | data formatting | bytes 1384448 | tf_op args[2]
  25.0 4.9 %all-to-all-done = bf16[32,32,256]{2,1,0:T(8,128)(2,1)S(1)} async-done(((bf16[32,32,256]{2,1,0:T(8,128)(2,1)}), bf16[32,32,256]{2,1,0:T(8,128)(2,1)S(1)}, u32[]{:S(2)}, u32[]{:S(2)}) %all-to-all-start) | async-done | bytes 524320 | tf_op jit(solution)/shard_map/all_to_all | solution.py:262
  30.0 2.4 %shard_map.147 = (f32[2,256,1024]{2,1,0:T(8,128)S(1)}, f32[2,256,1024]{2,1,0:T(8,128)S(1)}, f32[2,256,1024]{2,1,0:T(8,128)S(1)}, bf16[32,256]{1,0:T(8,128)(2,1)S(1)}) custom-call(s32[3]{0:T(128)S(1)} %pad_add_fusion.places, s32[16,128]{1,0:T(8,128)S(1)} %bitcast.20, s32[16,128]{1,0:T(8,128)S(1)} %bitcast.23, bf16[16,25,128]{2,1,0:T(8,128)(2,1)S(1)} %bitcast.18, ...), custom_call_target="tpu_custom_call" | custom-call | flops 2350907392 | bytes 8388608 | tf_op jit(solution)/shard_map/pallas_call | solution.py:137
  32.5 3.7 %shard_map.148 = (f32[16,56,256]{2,1,0:T(8,128)S(1)}, f32[16,56,256]{2,1,0:T(8,128)S(1)}, f32[32,256]{1,0:T(8,128)S(1)}, f32[32,256]{1,0:T(8,128)S(1)}, f32[32,256]{1,0:T(8,128)S(1)}) custom-call(s32[3]{0:T(128)S(1)} %pad_add_fusion.places, s32[16,128]{1,0:T(8,128)S(1)} %bitcast.21, s32[16,128]{1,0:T(8,128)S(1)} %bitcast.22, s32[16,128]{1,0:T(8,128)S(1)} %bitcast.24, ...), custom_call_target="tpu_custom_call" | custom-call | tf_op jit(solution)/shard_map/pallas_call | solution.py:158
  36.2 2.1 %collective-permute-start.2 = (f32[16,56,256]{2,1,0:T(8,128)S(1)}, f32[16,56,256]{2,1,0:T(8,128)S(1)}, u32[]{:S(2)}, u32[]{:S(2)}) collective-permute-start(f32[16,56,256]{2,1,0:T(8,128)S(1)} %get-tuple-element.28), channel_id=1, source_target_pairs={{0,1},{1,0},{2,3},{3,2},{4,5},{5,4},{6,7},{7,6},{8,9},{9,8},{10,11... | collective-permute-start | bytes 2752520 | tf_op jit(solution)/shard_map/ppermute | solution.py:268
  38.2 2.3 %collective-permute-done.2 = f32[16,56,256]{2,1,0:T(8,128)S(1)} collective-permute-done((f32[16,56,256]{2,1,0:T(8,128)S(1)}, f32[16,56,256]{2,1,0:T(8,128)S(1)}, u32[]{:S(2)}, u32[]{:S(2)}) %collective-permute-start.2) | collective-permute-done | bytes 917536 | tf_op jit(solution)/shard_map/ppermute | solution.py:268
  40.5 0.9 add_convert_fusion
  41.4 8.7 %all-to-all-start.1 = ((bf16[16,56,256]{2,1,0:T(8,128)(2,1)}), bf16[16,56,256]{2,1,0:T(8,128)(2,1)S(1)}, u32[]{:S(2)}, u32[]{:S(2)}) async-start(bf16[16,56,256]{2,1,0:T(8,128)(2,1)} %add_convert_fusion), calls=%async_computation.1 | async-start | bytes 917504 | tf_op jit(solution)/shard_map/all_to_all | solution.py:262
  50.1 2.6 %collective-permute-start.3 = (f32[32,256]{1,0:T(8,128)S(1)}, f32[32,256]{1,0:T(8,128)S(1)}, u32[]{:S(2)}, u32[]{:S(2)}) collective-permute-start(f32[32,256]{1,0:T(8,128)S(1)} %get-tuple-element.30), channel_id=1, source_target_pairs={{0,1},{1,0},{2,3},{3,2},{4,5},{5,4},{6,7},{7,6},{8,9},{9,8},{10,11... | collective-permute-start | bytes 98312 | tf_op jit(solution)/shard_map/ppermute | solution.py:268
  52.7 0.8 collective-permute-done.3.passed
  53.6 10.9 %all-to-all-done.1.parts = bf16[16,56,256]{2,1,0:T(8,128)(2,1)S(1)} async-done(((bf16[16,56,256]{2,1,0:T(8,128)(2,1)}), bf16[16,56,256]{2,1,0:T(8,128)(2,1)S(1)}, u32[]{:S(2)}, u32[]{:S(2)}) %all-to-all-start.1) | async-done | bytes 458784 | tf_op jit(solution)/shard_map/all_to_all | solution.py:262
  65.2 4.6 %all-to-all-start.2 = ((f32[4,24,256]{2,1,0:T(8,128)}), f32[4,24,256]{2,1,0:T(8,128)S(1)}, u32[]{:S(2)}, u32[]{:S(2)}) async-start(f32[4,24,256]{2,1,0:T(8,128)} %get-tuple-element.32), calls=%async_computation.2 | async-start | bytes 196608 | tf_op jit(solution)/shard_map/all_to_all | solution.py:262
  69.8 6.6 %collective-permute-start.4 = (f32[64,256]{1,0:T(8,128)S(1)}, f32[64,256]{1,0:T(8,128)S(1)}, u32[]{:S(2)}, u32[]{:S(2)}) collective-permute-start(f32[64,256]{1,0:T(8,128)S(1)} %get-tuple-element.34), channel_id=1, source_target_pairs={{1,33},{3,35},{5,37},{7,39},{9,41},{11,43},{13,45},{15,47},{17,49}... | collective-permute-start | bytes 196616 | tf_op jit(solution)/shard_map/ppermute | solution.py:286
  77.1 9.1 %all-to-all-start.3 = ((f32[4,24,256]{2,1,0:T(8,128)}), f32[4,24,256]{2,1,0:T(8,128)S(1)}, u32[]{:S(2)}, u32[]{:S(2)}) async-start(f32[4,24,256]{2,1,0:T(8,128)} %shard_map.150), calls=%async_computation.3 | async-start | bytes 196608 | tf_op jit(solution)/shard_map/all_to_all | solution.py:262
  86.2 4.9 %collective-permute-start.5 = (f32[32,256]{1,0:T(8,128)S(1)}, f32[32,256]{1,0:T(8,128)S(1)}, u32[]{:S(2)}, u32[]{:S(2)}) collective-permute-start(f32[32,256]{1,0:T(8,128)S(1)} %get-tuple-element.41), channel_id=1, source_target_pairs={{0,1},{1,0},{2,3},{3,2},{4,5},{5,4},{6,7},{7,6},{8,9},{9,8},{10,11... | collective-permute-start | bytes 98312 | tf_op jit(solution)/shard_map/ppermute | solution.py:268
  91.9 6.1 %all-to-all-done.3.parts = f32[4,24,256]{2,1,0:T(8,128)S(1)} async-done(((f32[4,24,256]{2,1,0:T(8,128)}), f32[4,24,256]{2,1,0:T(8,128)S(1)}, u32[]{:S(2)}, u32[]{:S(2)}) %all-to-all-start.3) | async-done | bytes 98336 | tf_op jit(solution)/shard_map/all_to_all | solution.py:262
  98.1 11.0 %all_to_all.25.own = bf16[16,24,256]{2,1,0:T(8,128)(2,1)S(1)} all-to-all(bf16[16,24,256]{2,1,0:T(8,128)(2,1)S(1)} %get-tuple-element.36), channel_id=1, replica_groups={{0,2,4,6,8,10,12,14,16,18,20,22,24,26,28,30},{1,3,5,7,9,11,13,15,17,19,..., dimensions={0} | all-to-all | bytes 393216 | tf_op jit(solution)/shard_map/all_to_all | solution.py:262
  109.0 7.4 %collective-permute-start.6 = (bf16[16,24,256]{2,1,0:T(8,128)(2,1)S(1)}, bf16[16,24,256]{2,1,0:T(8,128)(2,1)S(1)}, u32[]{:S(2)}, u32[]{:S(2)}) collective-permute-start(bf16[16,24,256]{2,1,0:T(8,128)(2,1)S(1)} %all_to_all.25.own), channel_id=1, source_target_pairs={{0,1},{1,0},{2,3},{3,2},{4,5},{5,4},{6,7},{7,6},{8,9},{9,8},{10,11... | collective-permute-start | bytes 589832 | tf_op jit(solution)/shard_map/ppermute | solution.py:268
  116.5 0.9 shard_map.152
  117.5 0.9 shard_map.153
  (33 shorter events, 3.3 us)
Async XLA Ops:
  0.6 29.3 %copy-start.1 = (bf16[256,256]{1,0:T(8,128)(2,1)S(1)}, bf16[256,256]{1,0:T(8,128)(2,1)}, u32[]{:S(2)}) copy-start(bf16[256,256]{1,0:T(8,128)(2,1)} %w_left.3) | copy-start | bytes 393220
  0.6 0.8 copy-start.2
  1.4 23.4 %copy-start.9 = (bf16[1,16,25,128]{3,1,2,0:T(8,128)(2,1)S(1)}, bf16[1,16,25,128]{3,1,2,0:T(8,128)(2,1)}, u32[]{:S(2)}) copy-start(bf16[1,16,25,128]{3,1,2,0:T(8,128)(2,1)} %param.12) | copy-start | bytes 307204
  1.4 28.5 %copy-start.3 = (bf16[32,256]{1,0:T(8,128)(2,1)S(1)}, bf16[32,256]{1,0:T(8,128)(2,1)}, u32[]{:S(2)}) copy-start(bf16[32,256]{1,0:T(8,128)(2,1)} %nodes.1) | copy-start | bytes 49156
  1.4 28.5 %copy-start.4 = (s32[1,16,128]{2,1,0:T(8,128)S(1)}, s32[1,16,128]{2,1,0:T(8,128)}, u32[]{:S(2)}) copy-start(s32[1,16,128]{2,1,0:T(8,128)} %param.14) | copy-start | bytes 24580
  1.4 28.5 %copy-start.6 = (s32[1,16,128]{2,1,0:T(8,128)S(1)}, s32[1,16,128]{2,1,0:T(8,128)}, u32[]{:S(2)}) copy-start(s32[1,16,128]{2,1,0:T(8,128)} %param.16) | copy-start | bytes 24580
  1.4 28.5 %copy-start.7 = (bf16[169,256]{1,0:T(8,128)(2,1)S(1)}, bf16[169,256]{1,0:T(8,128)(2,1)}, u32[]{:S(2)}) copy-start(bf16[169,256]{1,0:T(8,128)(2,1)} %w_out.1) | copy-start | bytes 259588
  1.4 28.5 %copy-start.8 = (bf16[25,256]{1,0:T(8,128)(2,1)S(1)}, bf16[25,256]{1,0:T(8,128)(2,1)}, u32[]{:S(2)}) copy-start(bf16[25,256]{1,0:T(8,128)(2,1)} %w_harm.1) | copy-start | bytes 38404
  2.5 27.4 %all-to-all-start = ((bf16[32,32,256]{2,1,0:T(8,128)(2,1)}), bf16[32,32,256]{2,1,0:T(8,128)(2,1)S(1)}, u32[]{:S(2)}, u32[]{:S(2)}) async-start(bf16[32,32,256]{2,1,0:T(8,128)(2,1)} %shard_map.146), calls=%async_computation | async-start | bytes 1048576 | tf_op jit(solution)/shard_map/all_to_all | solution.py:262
  13.0 19.4 %collective-permute-start = (bf16[32,256]{1,0:T(8,128)(2,1)}, bf16[32,256]{1,0:T(8,128)(2,1)S(1)}, u32[]{:S(2)}, u32[]{:S(2)}) collective-permute-start(bf16[32,256]{1,0:T(8,128)(2,1)} %nodes.1), channel_id=1, source_target_pairs={{0,32},{32,64},{64,96},{96,128},{128,160},{160,192},{192,224},{224... | collective-permute-start | bytes 49160 | tf_op jit(solution)/shard_map/ppermute | solution.py:273
  21.6 10.8 %collective-permute-start.1 = (bf16[32,256]{1,0:T(8,128)(2,1)}, bf16[32,256]{1,0:T(8,128)(2,1)S(1)}, u32[]{:S(2)}, u32[]{:S(2)}) collective-permute-start(bf16[32,256]{1,0:T(8,128)(2,1)} %nodes.1), channel_id=1, source_target_pairs={{32,0},{64,32},{96,64},{128,96},{160,128},{192,160},{224,192},{256... | collective-permute-start | bytes 49160 | tf_op jit(solution)/shard_map/ppermute | solution.py:273
  29.9 2.5 %copy-start = (bf16[256,256]{1,0:T(8,128)(2,1)S(1)}, bf16[256,256]{1,0:T(8,128)(2,1)}, u32[]{:S(2)}) copy-start(bf16[256,256]{1,0:T(8,128)(2,1)} %w_right.3) | copy-start | bytes 393220
  30.0 2.5 %copy-start.5 = (s32[1,16,128]{2,1,0:T(8,128)S(1)}, s32[1,16,128]{2,1,0:T(8,128)}, u32[]{:S(2)}) copy-start(s32[1,16,128]{2,1,0:T(8,128)} %param.15) | copy-start | bytes 24580
  36.2 4.4 %collective-permute-start.2 = (f32[16,56,256]{2,1,0:T(8,128)S(1)}, f32[16,56,256]{2,1,0:T(8,128)S(1)}, u32[]{:S(2)}, u32[]{:S(2)}) collective-permute-start(f32[16,56,256]{2,1,0:T(8,128)S(1)} %get-tuple-element.28), channel_id=1, source_target_pairs={{0,1},{1,0},{2,3},{3,2},{4,5},{5,4},{6,7},{7,6},{8,9},{9,8},{10,11... | collective-permute-start | bytes 2752520 | tf_op jit(solution)/shard_map/ppermute | solution.py:268
  41.4 23.1 %all-to-all-start.1 = ((bf16[16,56,256]{2,1,0:T(8,128)(2,1)}), bf16[16,56,256]{2,1,0:T(8,128)(2,1)S(1)}, u32[]{:S(2)}, u32[]{:S(2)}) async-start(bf16[16,56,256]{2,1,0:T(8,128)(2,1)} %add_convert_fusion), calls=%async_computation.1 | async-start | bytes 917504 | tf_op jit(solution)/shard_map/all_to_all | solution.py:262
  50.1 3.4 %collective-permute-start.3 = (f32[32,256]{1,0:T(8,128)S(1)}, f32[32,256]{1,0:T(8,128)S(1)}, u32[]{:S(2)}, u32[]{:S(2)}) collective-permute-start(f32[32,256]{1,0:T(8,128)S(1)} %get-tuple-element.30), channel_id=1, source_target_pairs={{0,1},{1,0},{2,3},{3,2},{4,5},{5,4},{6,7},{7,6},{8,9},{9,8},{10,11... | collective-permute-start | bytes 98312 | tf_op jit(solution)/shard_map/ppermute | solution.py:268
  65.2 11.3 %all-to-all-start.2 = ((f32[4,24,256]{2,1,0:T(8,128)}), f32[4,24,256]{2,1,0:T(8,128)S(1)}, u32[]{:S(2)}, u32[]{:S(2)}) async-start(f32[4,24,256]{2,1,0:T(8,128)} %get-tuple-element.32), calls=%async_computation.2 | async-start | bytes 196608 | tf_op jit(solution)/shard_map/all_to_all | solution.py:262
  69.8 16.4 %collective-permute-start.4 = (f32[64,256]{1,0:T(8,128)S(1)}, f32[64,256]{1,0:T(8,128)S(1)}, u32[]{:S(2)}, u32[]{:S(2)}) collective-permute-start(f32[64,256]{1,0:T(8,128)S(1)} %get-tuple-element.34), channel_id=1, source_target_pairs={{1,33},{3,35},{5,37},{7,39},{9,41},{11,43},{13,45},{15,47},{17,49}... | collective-permute-start | bytes 196616 | tf_op jit(solution)/shard_map/ppermute | solution.py:286
  77.1 20.9 %all-to-all-start.3 = ((f32[4,24,256]{2,1,0:T(8,128)}), f32[4,24,256]{2,1,0:T(8,128)S(1)}, u32[]{:S(2)}, u32[]{:S(2)}) async-start(f32[4,24,256]{2,1,0:T(8,128)} %shard_map.150), calls=%async_computation.3 | async-start | bytes 196608 | tf_op jit(solution)/shard_map/all_to_all | solution.py:262
  86.2 5.7 %collective-permute-start.5 = (f32[32,256]{1,0:T(8,128)S(1)}, f32[32,256]{1,0:T(8,128)S(1)}, u32[]{:S(2)}, u32[]{:S(2)}) collective-permute-start(f32[32,256]{1,0:T(8,128)S(1)} %get-tuple-element.41), channel_id=1, source_target_pairs={{0,1},{1,0},{2,3},{3,2},{4,5},{5,4},{6,7},{7,6},{8,9},{9,8},{10,11... | collective-permute-start | bytes 98312 | tf_op jit(solution)/shard_map/ppermute | solution.py:268
  109.0 8.5 %collective-permute-start.6 = (bf16[16,24,256]{2,1,0:T(8,128)(2,1)S(1)}, bf16[16,24,256]{2,1,0:T(8,128)(2,1)S(1)}, u32[]{:S(2)}, u32[]{:S(2)}) collective-permute-start(bf16[16,24,256]{2,1,0:T(8,128)(2,1)S(1)} %all_to_all.25.own), channel_id=1, source_target_pairs={{0,1},{1,0},{2,3},{3,2},{4,5},{5,4},{6,7},{7,6},{8,9},{9,8},{10,11... | collective-permute-start | bytes 589832 | tf_op jit(solution)/shard_map/ppermute | solution.py:268

commit v10 on v7

--- a/solution.py
+++ b/solution.py
@@ -261,6 +261,18 @@
 def exchange(blocks, axis, bits):
     return lax.all_to_all(
         blocks, axis, 0, 0, tiled=True, axis_index_groups=groups(lax.axis_size(axis), bits)
+    )
+
+
+def crossed(blocks, bits):
+    rows, columns = lax.axis_size("row"), lax.axis_size("col")
+    found = {}
+    for row in range(rows):
+        for column in range(columns):
+            key = (row & ~sum(bits[column // 2 % 2]), column)
+            found.setdefault(key, []).append(row * columns + column)
+    return lax.all_to_all(
+        blocks, BOTH, 0, 0, tiled=True, axis_index_groups=list(found.values())
     )
 
 
@@ -336,10 +348,10 @@
     row_sums, parts, both = call(
         row_kernel, (block, chunks, like(2 * shard, width)), core, parts, ahead, passed, scalars=1
     )
-    parts = exchange(parts, "row", X_BITS)
+    parts = crossed(parts, (X_BITS, Z_BITS))
     both = neighbours(both)
     parts = call(middle_kernel, chunks, parts)
-    parts = exchange(parts, "row", Z_BITS)
+    parts = crossed(parts, (Z_BITS, X_BITS))
     first = core[0] == 0
     here = jnp.where(first, both[:shard], both[shard:])
     there = swapped(jnp.where(first, both[shard:], both[:shard]))

time: 119 us -> 120 us (level)
  starting transfers between devices: 65.8 us -> 61.5 us
  Pallas kernels: 10.2 us -> 13.9 us
  blocking collectives: 11 us -> 12.6 us
    all_to_all x4 -> x2, starting transfers between devices: 32.5 us -> 15.7 us  [exchange(): lax.all_to_all(blocks, axis, 0, 0, tiled=True, axis_index_groups=groups(l...]
    all_to_all x0 -> x2, starting transfers between devices: none -> 12.2 us  [crossed(): lax.all_to_all(blocks, BOTH, 0, 0, tiled=True, axis_index_groups=list(fou...]
    all_to_all x4 -> x2, waiting for transfers between devices: 22.1 us -> 15.9 us  [exchange(): lax.all_to_all(blocks, axis, 0, 0, tiled=True, axis_index_groups=groups(l...]
    all_to_all x0 -> x2, waiting for transfers between devices: none -> 6.14 us  [crossed(): lax.all_to_all(blocks, BOTH, 0, 0, tiled=True, axis_index_groups=list(fou...]
    pallas_call x1, Pallas kernels: 3.72 us -> 5.9 us  [pair_sums(): pl.pallas_call(pair_kernel, out_shape=(chunks,) * 2 + (block,) * 3, in_sp...]
    all_to_all x1, blocking collectives: 11 us -> 12.6 us  [exchange(): lax.all_to_all(blocks, axis, 0, 0, tiled=True, axis_index_groups=groups(l...]
    pallas_call x1, Pallas kernels: 2.42 us -> 3.95 us  [row_pairs(): pl.pallas_call(row_pair_kernel, out_shape=(per_pair,) * 3 + (jax.ShapeDty...]
    ppermute x1, starting transfers between devices: 6.6 us -> 7.91 us  [neighbours(): return lax.ppermute(block, BOTH, route)]
  transfers between devices with their start and end apart: 11 -> 11, of which waited for: 7 -> 7; matrix products, arithmetic and copies ran while one was open for 1% -> 1% of each run, Pallas kernels for 3% -> 5%
where the time goes in v10:
time: 120 us; the launch traced here: 119 us
  starting transfers between devices  61.5 us (51%)
  waiting for transfers between devices  26.2 us (22%)
  Pallas kernels  13.9 us (12%)
  blocking collectives  12.6 us (10%)
  local copies, waits for them, and re-layouts  2.11 us (2%)
  between operations  1.54 us (1%)
    all_to_all x2, waiting for transfers between devices, exchange(): lax.all_to_all(blocks, axis, 0, 0, tiled=True, axis_index_groups=groups(l...  15.9 us
    ppermute x4, starting transfers between devices, swapped(): lax.ppermute(block, 'col', [(i, i ^ 1) for i in range(lax.axis_size('col'...  15.8 us
    all_to_all x2, starting transfers between devices, exchange(): lax.all_to_all(blocks, axis, 0, 0, tiled=True, axis_index_groups=groups(l...  15.7 us
    all_to_all x1, blocking collectives, exchange(): lax.all_to_all(blocks, axis, 0, 0, tiled=True, axis_index_groups=groups(l...  12.6 us
    all_to_all x2, starting transfers between devices, crossed(): lax.all_to_all(blocks, BOTH, 0, 0, tiled=True, axis_index_groups=list(fou...  12.2 us
    ppermute x2, starting transfers between devices, shifted(): lax.ppermute(block, 'row', [(i, i + distance) for i in devices if i + dis...  9.88 us
    ppermute x1, starting transfers between devices, neighbours(): return lax.ppermute(block, BOTH, route)  7.91 us
    all_to_all x2, waiting for transfers between devices, crossed(): lax.all_to_all(blocks, BOTH, 0, 0, tiled=True, axis_index_groups=list(fou...  6.14 us
  transfers between devices with their start and end apart: 11, of which 7 were waited for; matrix products, arithmetic and copies ran while one was open for 1% of the time, Pallas kernels for 5%

profile of v10, /device:TPU:1, one launch (start us, length us, event | category | flops | bytes accessed | tf_op | source)
XLA Modules:
  0.0 118.7 jit_solution(3659056346519037181)
XLA Ops:
  1.4 0.9 shard_map.146
  2.3 10.4 %all-to-all-start = ((bf16[32,32,256]{2,1,0:T(8,128)(2,1)}), bf16[32,32,256]{2,1,0:T(8,128)(2,1)S(1)}, u32[]{:S(2)}, u32[]{:S(2)}) async-start(bf16[32,32,256]{2,1,0:T(8,128)(2,1)} %shard_map.146), calls=%async_computation | async-start | bytes 1048576 | tf_op jit(solution)/shard_map/all_to_all | solution.py:262
  12.7 8.6 %collective-permute-start = (bf16[32,256]{1,0:T(8,128)(2,1)}, bf16[32,256]{1,0:T(8,128)(2,1)S(1)}, u32[]{:S(2)}, u32[]{:S(2)}) collective-permute-start(bf16[32,256]{1,0:T(8,128)(2,1)} %nodes.1), channel_id=1, source_target_pairs={{0,32},{32,64},{64,96},{96,128},{128,160},{160,192},{192,224},{224... | collective-permute-start | bytes 49160 | tf_op jit(solution)/shard_map/ppermute | solution.py:285
  21.3 1.3 %collective-permute-start.1 = (bf16[32,256]{1,0:T(8,128)(2,1)}, bf16[32,256]{1,0:T(8,128)(2,1)S(1)}, u32[]{:S(2)}, u32[]{:S(2)}) collective-permute-start(bf16[32,256]{1,0:T(8,128)(2,1)} %nodes.1), channel_id=1, source_target_pairs={{32,0},{64,32},{96,64},{128,96},{160,128},{192,160},{224,192},{256... | collective-permute-start | bytes 49160 | tf_op jit(solution)/shard_map/ppermute | solution.py:285
  23.3 1.3 %copy.20 = bf16[1,16,169,128]{3,2,1,0:T(8,128)(2,1)S(1)} copy(bf16[1,16,169,128]{3,1,2,0:T(8,128)(2,1)} %param.13) | data formatting | bytes 1384448 | tf_op args[2]
  24.7 4.9 %all-to-all-done = bf16[32,32,256]{2,1,0:T(8,128)(2,1)S(1)} async-done(((bf16[32,32,256]{2,1,0:T(8,128)(2,1)}), bf16[32,32,256]{2,1,0:T(8,128)(2,1)S(1)}, u32[]{:S(2)}, u32[]{:S(2)}) %all-to-all-start) | async-done | bytes 524320 | tf_op jit(solution)/shard_map/all_to_all | solution.py:262
  29.7 4.0 %shard_map.147 = (f32[2,256,1024]{2,1,0:T(8,128)S(1)}, f32[2,256,1024]{2,1,0:T(8,128)S(1)}, f32[2,256,1024]{2,1,0:T(8,128)S(1)}, bf16[32,256]{1,0:T(8,128)(2,1)S(1)}) custom-call(s32[3]{0:T(128)S(1)} %pad_add_fusion.places, s32[16,128]{1,0:T(8,128)S(1)} %bitcast.20, s32[16,128]{1,0:T(8,128)S(1)} %bitcast.23, bf16[16,25,128]{2,1,0:T(8,128)(2,1)S(1)} %bitcast.18, ...), custom_call_target="tpu_custom_call" | custom-call | flops 2350907392 | bytes 8388608 | tf_op jit(solution)/shard_map/pallas_call | solution.py:137
  33.7 5.9 %shard_map.148 = (f32[16,56,256]{2,1,0:T(8,128)S(1)}, f32[16,56,256]{2,1,0:T(8,128)S(1)}, f32[32,256]{1,0:T(8,128)S(1)}, f32[32,256]{1,0:T(8,128)S(1)}, f32[32,256]{1,0:T(8,128)S(1)}) custom-call(s32[3]{0:T(128)S(1)} %pad_add_fusion.places, s32[16,128]{1,0:T(8,128)S(1)} %bitcast.21, s32[16,128]{1,0:T(8,128)S(1)} %bitcast.22, s32[16,128]{1,0:T(8,128)S(1)} %bitcast.24, ...), custom_call_target="tpu_custom_call" | custom-call | tf_op jit(solution)/shard_map/pallas_call | solution.py:158
  39.6 2.1 %collective-permute-start.2 = (f32[16,56,256]{2,1,0:T(8,128)S(1)}, f32[16,56,256]{2,1,0:T(8,128)S(1)}, u32[]{:S(2)}, u32[]{:S(2)}) collective-permute-start(f32[16,56,256]{2,1,0:T(8,128)S(1)} %get-tuple-element.28), channel_id=1, source_target_pairs={{0,1},{1,0},{2,3},{3,2},{4,5},{5,4},{6,7},{7,6},{8,9},{9,8},{10,11... | collective-permute-start | bytes 2752520 | tf_op jit(solution)/shard_map/ppermute | solution.py:280
  41.7 2.3 %collective-permute-done.2 = f32[16,56,256]{2,1,0:T(8,128)S(1)} collective-permute-done((f32[16,56,256]{2,1,0:T(8,128)S(1)}, f32[16,56,256]{2,1,0:T(8,128)S(1)}, u32[]{:S(2)}, u32[]{:S(2)}) %collective-permute-start.2) | collective-permute-done | bytes 917536 | tf_op jit(solution)/shard_map/ppermute | solution.py:280
  44.0 0.9 add_convert_fusion
  44.9 5.3 %all-to-all-start.1 = ((bf16[16,56,256]{2,1,0:T(8,128)(2,1)}), bf16[16,56,256]{2,1,0:T(8,128)(2,1)S(1)}, u32[]{:S(2)}, u32[]{:S(2)}) async-start(bf16[16,56,256]{2,1,0:T(8,128)(2,1)} %add_convert_fusion), calls=%async_computation.1 | async-start | bytes 917504 | tf_op jit(solution)/shard_map/all_to_all | solution.py:262
  50.1 2.6 %collective-permute-start.3 = (f32[32,256]{1,0:T(8,128)S(1)}, f32[32,256]{1,0:T(8,128)S(1)}, u32[]{:S(2)}, u32[]{:S(2)}) collective-permute-start(f32[32,256]{1,0:T(8,128)S(1)} %get-tuple-element.30), channel_id=1, source_target_pairs={{0,1},{1,0},{2,3},{3,2},{4,5},{5,4},{6,7},{7,6},{8,9},{9,8},{10,11... | collective-permute-start | bytes 98312 | tf_op jit(solution)/shard_map/ppermute | solution.py:280
  52.7 0.8 collective-permute-done.3.passed
  53.5 10.9 %all-to-all-done.1.parts = bf16[16,56,256]{2,1,0:T(8,128)(2,1)S(1)} async-done(((bf16[16,56,256]{2,1,0:T(8,128)(2,1)}), bf16[16,56,256]{2,1,0:T(8,128)(2,1)S(1)}, u32[]{:S(2)}, u32[]{:S(2)}) %all-to-all-start.1) | async-done | bytes 458784 | tf_op jit(solution)/shard_map/all_to_all | solution.py:262
  65.2 3.5 %all-to-all-start.2 = ((f32[4,24,256]{2,1,0:T(8,128)}), f32[4,24,256]{2,1,0:T(8,128)S(1)}, u32[]{:S(2)}, u32[]{:S(2)}) async-start(f32[4,24,256]{2,1,0:T(8,128)} %get-tuple-element.32), calls=%async_computation.2 | async-start | bytes 196608 | tf_op jit(solution)/shard_map/all_to_all | solution.py:274
  68.7 7.9 %collective-permute-start.4 = (f32[64,256]{1,0:T(8,128)S(1)}, f32[64,256]{1,0:T(8,128)S(1)}, u32[]{:S(2)}, u32[]{:S(2)}) collective-permute-start(f32[64,256]{1,0:T(8,128)S(1)} %get-tuple-element.34), channel_id=1, source_target_pairs={{1,33},{3,35},{5,37},{7,39},{9,41},{11,43},{13,45},{15,47},{17,49}... | collective-permute-start | bytes 196616 | tf_op jit(solution)/shard_map/ppermute | solution.py:298
  77.2 8.7 %all-to-all-start.3 = ((f32[4,24,256]{2,1,0:T(8,128)}), f32[4,24,256]{2,1,0:T(8,128)S(1)}, u32[]{:S(2)}, u32[]{:S(2)}) async-start(f32[4,24,256]{2,1,0:T(8,128)} %shard_map.150), calls=%async_computation.3 | async-start | bytes 196608 | tf_op jit(solution)/shard_map/all_to_all | solution.py:274
  85.9 4.9 %collective-permute-start.5 = (f32[32,256]{1,0:T(8,128)S(1)}, f32[32,256]{1,0:T(8,128)S(1)}, u32[]{:S(2)}, u32[]{:S(2)}) collective-permute-start(f32[32,256]{1,0:T(8,128)S(1)} %get-tuple-element.41), channel_id=1, source_target_pairs={{0,1},{1,0},{2,3},{3,2},{4,5},{5,4},{6,7},{7,6},{8,9},{9,8},{10,11... | collective-permute-start | bytes 98312 | tf_op jit(solution)/shard_map/ppermute | solution.py:280
  91.6 6.1 %all-to-all-done.3.parts = f32[4,24,256]{2,1,0:T(8,128)S(1)} async-done(((f32[4,24,256]{2,1,0:T(8,128)}), f32[4,24,256]{2,1,0:T(8,128)S(1)}, u32[]{:S(2)}, u32[]{:S(2)}) %all-to-all-start.3) | async-done | bytes 98336 | tf_op jit(solution)/shard_map/all_to_all | solution.py:274
  97.8 12.6 %all_to_all.25.own = bf16[16,24,256]{2,1,0:T(8,128)(2,1)S(1)} all-to-all(bf16[16,24,256]{2,1,0:T(8,128)(2,1)S(1)} %get-tuple-element.36), channel_id=1, replica_groups={{0,2,4,6,8,10,12,14,16,18,20,22,24,26,28,30},{1,3,5,7,9,11,13,15,17,19,..., dimensions={0} | all-to-all | bytes 393216 | tf_op jit(solution)/shard_map/all_to_all | solution.py:262
  110.4 6.4 %collective-permute-start.6 = (bf16[16,24,256]{2,1,0:T(8,128)(2,1)S(1)}, bf16[16,24,256]{2,1,0:T(8,128)(2,1)S(1)}, u32[]{:S(2)}, u32[]{:S(2)}) collective-permute-start(bf16[16,24,256]{2,1,0:T(8,128)(2,1)S(1)} %all_to_all.25.own), channel_id=1, source_target_pairs={{0,1},{1,0},{2,3},{3,2},{4,5},{5,4},{6,7},{7,6},{8,9},{9,8},{10,11... | collective-permute-start | bytes 589832 | tf_op jit(solution)/shard_map/ppermute | solution.py:280
  116.8 0.9 shard_map.152
  117.8 0.9 shard_map.153
  (33 shorter events, 3.3 us)
Async XLA Ops:
  0.6 29.0 %copy-start.1 = (bf16[256,256]{1,0:T(8,128)(2,1)S(1)}, bf16[256,256]{1,0:T(8,128)(2,1)}, u32[]{:S(2)}) copy-start(bf16[256,256]{1,0:T(8,128)(2,1)} %w_left.3) | copy-start | bytes 393220
  0.6 0.8 copy-start.2
  1.4 23.2 %copy-start.9 = (bf16[1,16,25,128]{3,1,2,0:T(8,128)(2,1)S(1)}, bf16[1,16,25,128]{3,1,2,0:T(8,128)(2,1)}, u32[]{:S(2)}) copy-start(bf16[1,16,25,128]{3,1,2,0:T(8,128)(2,1)} %param.12) | copy-start | bytes 307204
  1.4 28.2 %copy-start.3 = (bf16[32,256]{1,0:T(8,128)(2,1)S(1)}, bf16[32,256]{1,0:T(8,128)(2,1)}, u32[]{:S(2)}) copy-start(bf16[32,256]{1,0:T(8,128)(2,1)} %nodes.1) | copy-start | bytes 49156
  1.4 28.2 %copy-start.4 = (s32[1,16,128]{2,1,0:T(8,128)S(1)}, s32[1,16,128]{2,1,0:T(8,128)}, u32[]{:S(2)}) copy-start(s32[1,16,128]{2,1,0:T(8,128)} %param.14) | copy-start | bytes 24580
  1.4 28.3 %copy-start.6 = (s32[1,16,128]{2,1,0:T(8,128)S(1)}, s32[1,16,128]{2,1,0:T(8,128)}, u32[]{:S(2)}) copy-start(s32[1,16,128]{2,1,0:T(8,128)} %param.16) | copy-start | bytes 24580
  1.4 28.3 %copy-start.7 = (bf16[169,256]{1,0:T(8,128)(2,1)S(1)}, bf16[169,256]{1,0:T(8,128)(2,1)}, u32[]{:S(2)}) copy-start(bf16[169,256]{1,0:T(8,128)(2,1)} %w_out.1) | copy-start | bytes 259588
  1.4 28.3 %copy-start.8 = (bf16[25,256]{1,0:T(8,128)(2,1)S(1)}, bf16[25,256]{1,0:T(8,128)(2,1)}, u32[]{:S(2)}) copy-start(bf16[25,256]{1,0:T(8,128)(2,1)} %w_harm.1) | copy-start | bytes 38404
  2.3 27.3 %all-to-all-start = ((bf16[32,32,256]{2,1,0:T(8,128)(2,1)}), bf16[32,32,256]{2,1,0:T(8,128)(2,1)S(1)}, u32[]{:S(2)}, u32[]{:S(2)}) async-start(bf16[32,32,256]{2,1,0:T(8,128)(2,1)} %shard_map.146), calls=%async_computation | async-start | bytes 1048576 | tf_op jit(solution)/shard_map/all_to_all | solution.py:262
  12.7 20.9 %collective-permute-start = (bf16[32,256]{1,0:T(8,128)(2,1)}, bf16[32,256]{1,0:T(8,128)(2,1)S(1)}, u32[]{:S(2)}, u32[]{:S(2)}) collective-permute-start(bf16[32,256]{1,0:T(8,128)(2,1)} %nodes.1), channel_id=1, source_target_pairs={{0,32},{32,64},{64,96},{96,128},{128,160},{160,192},{192,224},{224... | collective-permute-start | bytes 49160 | tf_op jit(solution)/shard_map/ppermute | solution.py:285
  21.3 12.4 %collective-permute-start.1 = (bf16[32,256]{1,0:T(8,128)(2,1)}, bf16[32,256]{1,0:T(8,128)(2,1)S(1)}, u32[]{:S(2)}, u32[]{:S(2)}) collective-permute-start(bf16[32,256]{1,0:T(8,128)(2,1)} %nodes.1), channel_id=1, source_target_pairs={{32,0},{64,32},{96,64},{128,96},{160,128},{192,160},{224,192},{256... | collective-permute-start | bytes 49160 | tf_op jit(solution)/shard_map/ppermute | solution.py:285
  29.7 4.0 %copy-start = (bf16[256,256]{1,0:T(8,128)(2,1)S(1)}, bf16[256,256]{1,0:T(8,128)(2,1)}, u32[]{:S(2)}) copy-start(bf16[256,256]{1,0:T(8,128)(2,1)} %w_right.3) | copy-start | bytes 393220
  29.7 4.0 %copy-start.5 = (s32[1,16,128]{2,1,0:T(8,128)S(1)}, s32[1,16,128]{2,1,0:T(8,128)}, u32[]{:S(2)}) copy-start(s32[1,16,128]{2,1,0:T(8,128)} %param.15) | copy-start | bytes 24580
  39.6 4.4 %collective-permute-start.2 = (f32[16,56,256]{2,1,0:T(8,128)S(1)}, f32[16,56,256]{2,1,0:T(8,128)S(1)}, u32[]{:S(2)}, u32[]{:S(2)}) collective-permute-start(f32[16,56,256]{2,1,0:T(8,128)S(1)} %get-tuple-element.28), channel_id=1, source_target_pairs={{0,1},{1,0},{2,3},{3,2},{4,5},{5,4},{6,7},{7,6},{8,9},{9,8},{10,11... | collective-permute-start | bytes 2752520 | tf_op jit(solution)/shard_map/ppermute | solution.py:280
  44.9 19.6 %all-to-all-start.1 = ((bf16[16,56,256]{2,1,0:T(8,128)(2,1)}), bf16[16,56,256]{2,1,0:T(8,128)(2,1)S(1)}, u32[]{:S(2)}, u32[]{:S(2)}) async-start(bf16[16,56,256]{2,1,0:T(8,128)(2,1)} %add_convert_fusion), calls=%async_computation.1 | async-start | bytes 917504 | tf_op jit(solution)/shard_map/all_to_all | solution.py:262
  50.1 3.4 %collective-permute-start.3 = (f32[32,256]{1,0:T(8,128)S(1)}, f32[32,256]{1,0:T(8,128)S(1)}, u32[]{:S(2)}, u32[]{:S(2)}) collective-permute-start(f32[32,256]{1,0:T(8,128)S(1)} %get-tuple-element.30), channel_id=1, source_target_pairs={{0,1},{1,0},{2,3},{3,2},{4,5},{5,4},{6,7},{7,6},{8,9},{9,8},{10,11... | collective-permute-start | bytes 98312 | tf_op jit(solution)/shard_map/ppermute | solution.py:280
  65.2 11.4 %all-to-all-start.2 = ((f32[4,24,256]{2,1,0:T(8,128)}), f32[4,24,256]{2,1,0:T(8,128)S(1)}, u32[]{:S(2)}, u32[]{:S(2)}) async-start(f32[4,24,256]{2,1,0:T(8,128)} %get-tuple-element.32), calls=%async_computation.2 | async-start | bytes 196608 | tf_op jit(solution)/shard_map/all_to_all | solution.py:274
  68.7 17.3 %collective-permute-start.4 = (f32[64,256]{1,0:T(8,128)S(1)}, f32[64,256]{1,0:T(8,128)S(1)}, u32[]{:S(2)}, u32[]{:S(2)}) collective-permute-start(f32[64,256]{1,0:T(8,128)S(1)} %get-tuple-element.34), channel_id=1, source_target_pairs={{1,33},{3,35},{5,37},{7,39},{9,41},{11,43},{13,45},{15,47},{17,49}... | collective-permute-start | bytes 196616 | tf_op jit(solution)/shard_map/ppermute | solution.py:298
  77.2 20.5 %all-to-all-start.3 = ((f32[4,24,256]{2,1,0:T(8,128)}), f32[4,24,256]{2,1,0:T(8,128)S(1)}, u32[]{:S(2)}, u32[]{:S(2)}) async-start(f32[4,24,256]{2,1,0:T(8,128)} %shard_map.150), calls=%async_computation.3 | async-start | bytes 196608 | tf_op jit(solution)/shard_map/all_to_all | solution.py:274
  85.9 5.7 %collective-permute-start.5 = (f32[32,256]{1,0:T(8,128)S(1)}, f32[32,256]{1,0:T(8,128)S(1)}, u32[]{:S(2)}, u32[]{:S(2)}) collective-permute-start(f32[32,256]{1,0:T(8,128)S(1)} %get-tuple-element.41), channel_id=1, source_target_pairs={{0,1},{1,0},{2,3},{3,2},{4,5},{5,4},{6,7},{7,6},{8,9},{9,8},{10,11... | collective-permute-start | bytes 98312 | tf_op jit(solution)/shard_map/ppermute | solution.py:280
  110.4 7.4 %collective-permute-start.6 = (bf16[16,24,256]{2,1,0:T(8,128)(2,1)S(1)}, bf16[16,24,256]{2,1,0:T(8,128)(2,1)S(1)}, u32[]{:S(2)}, u32[]{:S(2)}) collective-permute-start(bf16[16,24,256]{2,1,0:T(8,128)(2,1)S(1)} %all_to_all.25.own), channel_id=1, source_target_pairs={{0,1},{1,0},{2,3},{3,2},{4,5},{5,4},{6,7},{7,6},{8,9},{9,8},{10,11... | collective-permute-start | bytes 589832 | tf_op jit(solution)/shard_map/ppermute | solution.py:280
